TPU v7x, 32 devices: a whole 2x2x4 slice. The times are simulated.
32 devices in a mesh: seq: 16 (over z, y, x), mp: 2 (over core).
Axes of the slice: x: 2, y: 2, z: 4, core: 2. Of those that a mesh axis runs over, the one named last changes fastest.
Arguments:
- tokens: bfloat16 [12288, 1536], P('seq'), may hold values from -6 to 6
- starts: int32 [12288], P('seq'), may hold values from 0 to 1, as said below
- w_in: bfloat16 [1536, 3, 1536], P('seq', None, 'mp'), may hold values from -0.15625 to 0.15625
- w_out: bfloat16 [1536, 1536], P('mp', 'seq'), may hold values from -0.15625 to 0.15625
- gate_up: bfloat16 [1536, 2, 6912], P('seq', None, 'mp'), may hold values from -0.15625 to 0.15625
- w_down: bfloat16 [6912, 1536], P('mp', 'seq'), may hold values from -0.078125 to 0.078125
- gain_mix: bfloat16 [1536], P('seq'), may hold values from 0.099609375 to 1.8984375
- gain_ffn: bfloat16 [1536], P('seq'), may hold values from 0.099609375 to 1.8984375
- conv_taps: bfloat16 [3, 2, 768], P(None, 'mp', 'seq'), may hold values from -3.5 to 3.5
- cotangent: bfloat16 [12288, 1536], P('seq'), may hold values from -6 to 6
Outputs:
- out_acts: bfloat16 [12288, 1536], P('seq')
- grad_tokens: float32 [12288, 1536], P('seq')
- grad_w_in: float32 [1536, 3, 1536], P('seq', None, 'mp')
- grad_w_out: float32 [1536, 1536], P('mp', 'seq')
- grad_gate_up: float32 [1536, 2, 6912], P('seq', None, 'mp')
- grad_w_down: float32 [6912, 1536], P('mp', 'seq')
- grad_gain_mix: float32 [1536], P('seq')
- grad_gain_ffn: float32 [1536], P('seq')
- grad_conv_taps: float32 [3, 2, 768], P(None, 'mp', 'seq')
Inputs may be any that keep to these rules, and one draw needn't show every extreme that they name: Token 0 always starts a sequence; further starts may fall on any token, a device's first or last token included.
All inputs are finite; a program needn't handle non-finite values.
Results may differ from a plain program's by a relative error of at most 0.011.
Values may be sent and summed in bfloat16 or wider, within the bound.
No kernel may reach another device: no remote copies, remote signals or barrier semaphores. Data moves between devices by JAX's collectives and lax.ppermute only.
A program may use at most 256 MiB of HBM per device.

v0:
```python
import jax
import jax.numpy as jnp
from jax import lax
from jax.sharding import PartitionSpec as P

epsilon = 1e-05


def passed_along(value, axis, steps):
    count = lax.axis_size(axis)
    first, last = (max(0, -steps), min(count, count - steps))
    return lax.ppermute(value, axis, [(source, source + steps) for source in range(first, last)])


def norm_back(grad_norm, hat_vals, inv_vals, gain):
    grad_hat = grad_norm * gain
    inner = jnp.mean(grad_hat * hat_vals, axis=-1, keepdims=True)
    return (inv_vals * (grad_hat - hat_vals * inner), jnp.sum(grad_norm * hat_vals, axis=0))


def per_device(
    tokens, starts, w_in, w_out, gate_up, w_down, gain_mix, gain_ffn, conv_taps, cotangent
):
    gathered = (
        lax.all_gather(w_in, "seq", axis=0, tiled=True),
        lax.all_gather(w_out, "seq", axis=1, tiled=True),
        lax.all_gather(gate_up, "seq", axis=0, tiled=True),
        lax.all_gather(w_down, "seq", axis=1, tiled=True),
        lax.all_gather(gain_mix, "seq", axis=0, tiled=True),
        lax.all_gather(gain_ffn, "seq", axis=0, tiled=True),
        lax.all_gather(conv_taps, "seq", axis=2, tiled=True),
    )
    in_full, out_full, gu_full, down_full, gmix_full, gffn_full, taps_full = gathered
    gain_one = gmix_full.astype(jnp.float32)
    gain_two = gffn_full.astype(jnp.float32)
    taps = taps_full[:, 0, :].astype(jnp.float32)
    inputs = tokens.astype(jnp.float32)
    begins = starts.astype(jnp.float32)[:, None]
    earlier = jnp.concatenate([jnp.zeros((1, 1), jnp.float32), begins[:-1]], axis=0)
    keep_one = 1.0 - begins
    keep_two = (1.0 - begins) * (1.0 - earlier)
    inv_mix = lax.rsqrt(jnp.mean(inputs * inputs, axis=-1, keepdims=True) + epsilon)
    hat_mix = inputs * inv_mix
    norm_mix = (hat_mix * gain_one).astype(jnp.bfloat16)
    projected = jnp.einsum("td,dkc->tkc", norm_mix, in_full, preferred_element_type=jnp.float32)
    b_part = projected[:, 0]
    c_part = projected[:, 1]
    x_part = projected[:, 2]
    mixed_in = (b_part * x_part).astype(jnp.bfloat16)
    carry_out = jnp.stack(
        [(mixed_in[-2] * (1.0 - begins[-1, 0])).astype(jnp.bfloat16), mixed_in[-1]], axis=0
    )
    carry_in = passed_along(carry_out, "seq", 1)
    extended = jnp.concatenate([carry_in, mixed_in], axis=0).astype(jnp.float32)
    convolved = (
        taps[0] * extended[2:]
        + taps[1] * keep_one * extended[1:-1]
        + taps[2] * keep_two * extended[:-2]
    )
    gated = (c_part * convolved).astype(jnp.bfloat16)
    mixer = lax.psum(jnp.dot(gated, out_full, preferred_element_type=jnp.float32), "mp")
    middle = inputs + mixer
    inv_ffn = lax.rsqrt(jnp.mean(middle * middle, axis=-1, keepdims=True) + epsilon)
    hat_ffn = middle * inv_ffn
    norm_ffn = (hat_ffn * gain_two).astype(jnp.bfloat16)
    gate_vals = jnp.einsum("td,dkf->tkf", norm_ffn, gu_full, preferred_element_type=jnp.float32)
    gate_part = gate_vals[:, 0]
    up_part = gate_vals[:, 1]
    sig_gate = jax.nn.sigmoid(gate_part)
    silu_gate = gate_part * sig_gate
    act_vals = (silu_gate * up_part).astype(jnp.bfloat16)
    ffn_out = lax.psum(
        jnp.dot(act_vals, down_full, preferred_element_type=jnp.float32).astype(jnp.bfloat16), "mp"
    ).astype(jnp.float32)
    output_vals = (middle + ffn_out).astype(jnp.bfloat16)
    grad_act = jnp.einsum("td,fd->tf", cotangent, down_full, preferred_element_type=jnp.float32)
    grad_down = jnp.einsum("tf,td->fd", act_vals, cotangent, preferred_element_type=jnp.float32)
    grad_gate = grad_act * up_part * sig_gate * (1.0 + gate_part * (1.0 - sig_gate))
    grad_up = grad_act * silu_gate
    grad_gu = jnp.stack([grad_gate, grad_up], axis=1).astype(jnp.bfloat16)
    grad_gate_up = jnp.einsum("td,tkf->dkf", norm_ffn, grad_gu, preferred_element_type=jnp.float32)
    grad_norm_ffn = lax.psum(
        jnp.einsum("tkf,dkf->td", grad_gu, gu_full, preferred_element_type=jnp.float32), "mp"
    )
    grad_from_ffn, grad_gain_ffn = norm_back(grad_norm_ffn, hat_ffn, inv_ffn, gain_two)
    grad_middle = cotangent.astype(jnp.float32) + grad_from_ffn
    grad_mixer = grad_middle.astype(jnp.bfloat16)
    grad_out = jnp.einsum("tc,td->cd", gated, grad_mixer, preferred_element_type=jnp.float32)
    grad_gated = jnp.einsum("td,cd->tc", grad_mixer, out_full, preferred_element_type=jnp.float32)
    grad_c = grad_gated * convolved
    grad_conv = grad_gated * c_part
    grad_taps = jnp.stack(
        [
            jnp.sum(grad_conv * extended[2:], axis=0),
            jnp.sum(grad_conv * keep_one * extended[1:-1], axis=0),
            jnp.sum(grad_conv * keep_two * extended[:-2], axis=0),
        ],
        axis=0,
    )
    term_zero = taps[0] * grad_conv
    term_one = taps[1] * keep_one * grad_conv
    term_two = taps[2] * keep_two * grad_conv
    grad_ext = (
        jnp.pad(term_zero, ((2, 0), (0, 0)))
        + jnp.pad(term_one, ((1, 1), (0, 0)))
        + jnp.pad(term_two, ((0, 2), (0, 0)))
    )
    back_carry = passed_along(grad_ext[:2], "seq", -1)
    tail_gate = jnp.concatenate([1.0 - begins[-1:], jnp.ones((1, 1), jnp.float32)], axis=0)
    grad_local = grad_ext[2:]
    grad_mixed = jnp.concatenate(
        [grad_local[:-2], grad_local[-2:] + back_carry * tail_gate], axis=0
    )
    grad_mixed = grad_mixed.astype(jnp.bfloat16).astype(jnp.float32)
    grad_proj = jnp.stack([grad_mixed * x_part, grad_c, grad_mixed * b_part], axis=1).astype(
        jnp.bfloat16
    )
    grad_in = jnp.einsum("td,tkc->dkc", norm_mix, grad_proj, preferred_element_type=jnp.float32)
    grad_norm_mix = lax.psum(
        jnp.einsum("tkc,dkc->td", grad_proj, in_full, preferred_element_type=jnp.float32).astype(
            jnp.bfloat16
        ),
        "mp",
    ).astype(jnp.float32)
    grad_from_mix, grad_gain_mix = norm_back(grad_norm_mix, hat_mix, inv_mix, gain_one)
    grad_inputs = grad_middle + grad_from_mix
    reduced = (
        lax.psum_scatter(grad_in, "seq", scatter_dimension=0, tiled=True),
        lax.psum_scatter(grad_out, "seq", scatter_dimension=1, tiled=True),
        lax.psum_scatter(grad_gate_up, "seq", scatter_dimension=0, tiled=True),
        lax.psum_scatter(grad_down, "seq", scatter_dimension=1, tiled=True),
        lax.psum_scatter(grad_gain_mix, "seq", scatter_dimension=0, tiled=True),
        lax.psum_scatter(grad_gain_ffn, "seq", scatter_dimension=0, tiled=True),
        lax.psum_scatter(grad_taps[:, None, :], "seq", scatter_dimension=2, tiled=True),
    )
    red_in, red_out, red_gate_up, red_down, red_gain_mix, red_gain_ffn, red_taps = reduced
    return (
        output_vals,
        grad_inputs,
        red_in,
        red_out,
        red_gate_up,
        red_down,
        red_gain_mix,
        red_gain_ffn,
        red_taps,
    )


def solution(mesh):
    placed = (
        P("seq", None),
        P("seq"),
        P("seq", None, "mp"),
        P("mp", "seq"),
        P("seq", None, "mp"),
        P("mp", "seq"),
        P("seq"),
        P("seq"),
        P(None, "mp", "seq"),
        P("seq", None),
    )
    return jax.shard_map(
        per_device,
        mesh=mesh,
        in_specs=placed,
        out_specs=(
            P("seq", None),
            P("seq", None),
            P("seq", None, "mp"),
            P("mp", "seq"),
            P("seq", None, "mp"),
            P("mp", "seq"),
            P("seq"),
            P("seq"),
            P(None, "mp", "seq"),
        ),
        check_vma=False,
    )
```

profile of v0, /device:TPU:25, one launch (start us, length us, event | category | flops | bytes accessed | tf_op | source)
XLA Modules:
  0.0 2153.8 jit_solution(15320659057131973842)
XLA Ops:
  7.2 0.7 all-gather.5.cloned.1.call-update
  8.0 0.7 all-gather.7.cloned.1.call-update
  8.7 0.7 convert_element_type.99
  10.0 1.3 fusion.49
  12.0 0.9 dynamic-update-slice
  12.9 0.8 dynamic-update-slice.1
  13.7 28.2 %all-reduce.8 = (bf16[1536]{0:T(1024)(128)(2,1)S(1)}, bf16[1536]{0:T(1024)(128)(2,1)S(1)}) all-reduce(bf16[1536]{0:T(1024)(128)(2,1)S(1)} %dynamic-update-slice, bf16[1536]{0:T(1024)(128)(2,1)S(1)} %dynamic-update-slice.1), channel_id=1, replica_groups=mesh['seq'=16,'mp'=2] {'seq'}, use_global_device_ids=true, to_apply=%add.3 | all-reduce | flops 3072 | bytes 12288
  41.9 0.8 copy.28
  42.7 35.0 %all_gather.23 = bf16[3,1,768]{0,1,2:T(2,128)(2,1)S(1)} all-gather(bf16[3,1,48]{0,1,2:T(2,128)(2,1)S(1)} %copy.28), channel_id=1, replica_groups=mesh['seq'=16,'mp'=2] {'seq'}, dimensions={2}, use_global_device_ids=true | all-gather | bytes 4896 | tf_op jit(solution)/shard_map/all_gather | solution.py:31
  78.7 2.2 fusion.15
  81.1 7.6 slice_reduce_fusion.2
  88.6 26.7 %all-gather.5.cloned.1.call-done = bf16[1536,3,768]{2,0,1:T(8,128)(2,1)} async-done(((bf16[96,3,768]{2,0,1:T(8,128)(2,1)}), bf16[1536,3,768]{2,0,1:T(8,128)(2,1)}) %all-gather.5.cloned.1.call-update) | async-done | bytes 7077904 | tf_op jit(solution)/shard_map/all_gather | solution.py:25
  115.3 8.2 fusion.26
  123.8 3.5 collective-permute-start
  127.6 2.5 collective-permute-done
  130.4 2.6 multiply_convert_fusion.5
  133.0 48.0 %all-gather.7.cloned.1.call-done = bf16[768,1536]{0,1:T(8,128)(2,1)} async-done(((bf16[768,96]{0,1:T(8,128)(2,1)}), bf16[768,1536]{0,1:T(8,128)(2,1)}) %all-gather.7.cloned.1.call-update) | async-done | bytes 2359312 | tf_op jit(solution)/shard_map/all_gather | solution.py:26
  181.1 6.2 fusion.50
  187.4 2.5 copy.29
  190.6 26.8 %all-reduce.14.cloned.1.call-done = f32[768,1536]{1,0:T(8,128)} async-done(((f32[768,1536]{1,0:T(8,128)}), f32[768,1536]{1,0:T(8,128)}) %all-reduce.14.cloned.1.call-update) | async-done | bytes 4718608 | tf_op jit(solution)/shard_map/psum | solution.py:61
  217.3 5.9 multiply_reduce_fusion.2
  223.2 230.3 %all-gather.9.cloned.1.call-done = bf16[1536,2,3456]{2,0,1:T(8,128)(2,1)} async-done(((bf16[96,2,3456]{2,0,1:T(8,128)(2,1)}), bf16[1536,2,3456]{2,0,1:T(8,128)(2,1)}) %all-gather.9.cloned.1.call-update) | async-done | bytes 21233680 | tf_op jit(solution)/shard_map/all_gather | solution.py:27
  453.5 24.6 %fusion.35 = f32[768,2,3456]{2,0,1:T(8,128)} fusion(bf16[1536,2,3456]{2,0,1:T(8,128)(2,1)} %all-gather.9.cloned.1.call-done, f32[768,1536]{1,0:T(8,128)} %get-tuple-element.54, f32[1536]{0:T(1024)S(1)} %convert_element_type.103, f32[768]{0:T(1024)S(1)} %add_rsqrt_fusion), kind=kOutput, calls=%fused_computation.75 | convolution fusion | flops 16310992896 | bytes 47195136 | tf_op jit(solution)/shard_map/td,dkf->tkf/dot_general | solution.py:66
  478.1 110.2 %all-gather.11.cloned.1.call-done = bf16[3456,1536]{0,1:T(8,128)(2,1)} async-done(((bf16[3456,96]{0,1:T(8,128)(2,1)}), bf16[3456,1536]{0,1:T(8,128)(2,1)}) %all-gather.11.cloned.1.call-update) | async-done | bytes 10616848 | tf_op jit(solution)/shard_map/all_gather | solution.py:28
  588.3 23.9 %fusion.9 = (bf16[768,1,3456]{2,0,1:T(8,128)(2,1)}, bf16[768,1,3456]{2,0,1:T(8,128)(2,1)}, bf16[768,3456]{1,0:T(8,128)(2,1)}) fusion(f32[768,2,3456]{2,0,1:T(8,128)} %fusion.35, bf16[768,1536]{1,0:T(8,128)(2,1)} %param.19, bf16[3456,1536]{0,1:T(8,128)(2,1)} %all-gather.11.cloned.1.call-done), kind=kOutput, calls=%fused_computation.20 | convolution fusion | flops 8193540096 | bytes 50135040 | tf_op jit(solution)/shard_map/td,fd->tf/dot_general | solution.py:76
  612.1 24.6 %fusion.16 = f32[768,1536]{1,0:T(8,128)} fusion(bf16[1536,2,3456]{2,0,1:T(8,128)(2,1)} %all-gather.9.cloned.1.call-done, bf16[768,1,3456]{2,0,1:T(8,128)(2,1)} %get-tuple-element.58, bf16[768,1,3456]{2,0,1:T(8,128)(2,1)} %get-tuple-element.57), kind=kOutput, calls=%fused_computation.34 | convolution fusion | flops 16312762368 | bytes 36569088 | tf_op jit(solution)/shard_map/tkf,dkf->td/dot_general | solution.py:83
  637.4 14.0 convolution_convert_fusion
  651.4 15.3 all-reduce.16.cloned.1.call-done
  666.7 5.7 multiply_reduce_fusion
  672.5 3.8 multiply_add_fusion
  676.4 2.0 fusion.32
  678.7 1.0 copy-done.8
  679.7 3.5 multiply_reduce_fusion.5
  683.8 0.6 pad_add_fusion.1
  684.5 0.7 copy-done.3
  685.2 0.8 copy-done.5
  686.6 0.6 broadcast_in_dim.2
  687.2 2.2 copy.37
  689.4 3.1 bitcast_reduce_fusion
  692.5 4.1 collective-permute-start.1
  696.9 0.7 collective-permute-done.1
  697.6 0.8 fusion.42
  698.4 2.9 fusion.17
  701.4 1.0 copy-done.12
  702.7 9.9 bitcast_convert_fusion
  712.7 0.6 copy-done.17
  713.4 26.7 %fusion.5 = f32[1536,2,3456]{2,0,1:T(8,128)} fusion(bf16[768,1,3456]{2,0,1:T(8,128)(2,1)} %get-tuple-element.58, bf16[768,1,3456]{2,0,1:T(8,128)(2,1)} %get-tuple-element.57, f32[768,1536]{1,0:T(8,128)} %get-tuple-element.54, f32[1536]{0:T(1024)S(1)} %copy-done.17, f32[768]{0:T(1024)S(1)} %add_rsqrt_fusion), kind=kOutput, calls=%fused_computation.15 | convolution fusion | flops 16332226560 | bytes 57811968 | tf_op jit(solution)/shard_map/td,tkf->dkf/dot_general | solution.py:81
  740.1 1.2 copy-done.10
  741.3 6.5 fusion.30
  747.9 1.6 copy-done.2
  749.5 10.8 fusion.24
  760.4 16.0 fusion.51
  777.1 35.0 %reduce-scatter.16.cloned.1.call-done = f32[48,3]{1,0:T(8,128)} async-done(((f32[768,3]{1,0:T(8,128)}), f32[48,3]{1,0:T(8,128)}) %reduce-scatter.16.cloned.1.call-update) | async-done | bytes 592
  812.1 0.8 reshape_bitcast_fusion
  812.9 0.7 copy.38
  813.6 33.4 %all-reduce.18.cloned.1.call-done = (bf16[768,1536]{1,0:T(8,128)(2,1)}, bf16[768,1536]{1,0:T(8,128)(2,1)}) async-done(((bf16[768,1536]{1,0:T(8,128)(2,1)}, bf16[768,1536]{1,0:T(8,128)(2,1)}), (bf16[768,1536]{1,0:T(8,128)(2,1)}, bf16[768,1536]{1,0:T(8,128)(2,1)})) %all-reduce.18.cloned.1.call-update) | async-done | bytes 4718608 | tf_op jit(solution)/shard_map/psum | solution.py:72
  847.0 3.2 fusion.14
  850.2 59.0 %all-reduce.7 = (f32[1536]{0:T(1024)S(1)}, f32[1536]{0:T(1024)S(1)}) all-reduce(f32[1536]{0:T(1024)S(1)} %get-tuple-element.41, f32[1536]{0:T(1024)S(1)} %copy-done.20), channel_id=6, replica_groups=mesh['seq'=16,'mp'=2] {'seq'}, use_global_device_ids=true, to_apply=%region_13.14.clone | all-reduce | flops 3072 | bytes 24576
  910.4 8.7 fusion.11
  919.1 539.0 %reduce-scatter.12.cloned.1.call-done = f32[96,2,3456]{2,0,1:T(8,128)} async-done(((f32[1536,2,3456]{2,0,1:T(8,128)}), f32[96,2,3456]{2,0,1:T(8,128)}) %reduce-scatter.12.cloned.1.call-update) | async-done | bytes 2654224 | tf_op jit(solution)/shard_map/reduce_scatter | solution.py:130
  1458.1 5.3 copy.32
  1463.4 134.8 %reduce-scatter.10.cloned.1.call-done = f32[768,96]{0,1:T(8,128)} async-done(((f32[768,1536]{0,1:T(8,128)}), f32[768,96]{0,1:T(8,128)}) %reduce-scatter.10.cloned.1.call-update) | async-done | bytes 294928 | tf_op jit(solution)/shard_map/reduce_scatter | solution.py:129
  1598.2 228.2 %reduce-scatter.8.cloned.1.call-done = f32[96,3,768]{2,0,1:T(8,128)} async-done(((f32[1536,3,768]{2,0,1:T(8,128)}), f32[96,3,768]{2,0,1:T(8,128)}) %reduce-scatter.8.cloned.1.call-update) | async-done | bytes 884752 | tf_op jit(solution)/shard_map/reduce_scatter | solution.py:128
  1826.5 320.3 %reduce-scatter.14.cloned.1.call-done = f32[3456,96]{0,1:T(8,128)} async-done(((f32[3456,1536]{0,1:T(8,128)}), f32[3456,96]{0,1:T(8,128)}) %reduce-scatter.14.cloned.1.call-update) | async-done | bytes 1327120 | tf_op jit(solution)/shard_map/reduce_scatter | solution.py:131
  (88 shorter events, 7.1 us)
Async XLA Ops:
  7.2 73.8 %copy-start.21 = (s32[768]{0:T(1024)S(1)}, s32[768]{0:T(1024)}, u32[]{:S(2)}) copy-start(s32[768]{0:T(1024)} %param.11) | copy-start | bytes 9220
  7.2 108.1 %copy-start.1 = (bf16[768,1536]{1,0:T(8,128)(2,1)S(1)}, bf16[768,1536]{1,0:T(8,128)(2,1)}, u32[]{:S(2)}) copy-start(bf16[768,1536]{1,0:T(8,128)(2,1)} %param.10) | copy-start | bytes 7077892
  7.2 108.1 %all-gather.5.cloned.1.call-start = ((), (), s32[]{:S(2)}) async-start(), calls=%async_computation.5 | async-start | bytes 7520256 | tf_op jit(solution)/shard_map/all_gather | solution.py:25
  7.9 173.1 %all-gather.7.cloned.1.call-start = ((), (), s32[]{:S(2)}) async-start(), calls=%async_computation.6 | async-start | bytes 2506752 | tf_op jit(solution)/shard_map/all_gather | solution.py:26
  8.7 208.6 %all-reduce.14.cloned.1.call-start = ((), (), s32[]{:S(2)}) async-start(), calls=%async_computation.7 | async-start | bytes 9437184 | tf_op jit(solution)/shard_map/psum | solution.py:61
  41.9 81.7 %copy-start.14 = (f32[1536]{0:T(1024)}, f32[1536]{0:T(1024)S(1)}, u32[]{:S(2)}) copy-start(f32[1536]{0:T(1024)S(1)} %convert_element_type.94) | copy-start | bytes 18436
  81.0 42.6 %copy-start.18 = (f32[768]{0:T(1024)}, f32[768]{0:T(1024)S(1)}, u32[]{:S(2)}) copy-start(f32[768]{0:T(1024)S(1)} %add_rsqrt_fusion.1) | copy-start | bytes 9220
  123.5 6.8 copy-start
  123.8 6.3 collective-permute-start
  187.3 266.2 %all-gather.9.cloned.1.call-start = ((), (), s32[]{:S(2)}) async-start(), calls=%async_computation.8 | async-start | bytes 22560768 | tf_op jit(solution)/shard_map/all_gather | solution.py:27
  189.9 398.4 %all-gather.11.cloned.1.call-start = ((), (), s32[]{:S(2)}) async-start(), calls=%async_computation.9 | async-start | bytes 11280384 | tf_op jit(solution)/shard_map/all_gather | solution.py:28
  190.5 476.2 %all-reduce.16.cloned.1.call-start = ((), (), s32[]{:S(2)}) async-start(), calls=%async_computation.10 | async-start | bytes 9437184 | tf_op jit(solution)/shard_map/psum | solution.py:82
  190.6 481.8 %copy-start.16 = (f32[1536]{0:T(1024)}, f32[1536]{0:T(1024)S(1)}, u32[]{:S(2)}) copy-start(f32[1536]{0:T(1024)S(1)} %convert_element_type.103) | copy-start | bytes 18436
  636.8 175.3 %reduce-scatter.16.cloned.1.call-start = ((), (), s32[]{:S(2)}) async-start(), calls=%async_computation.15 | async-start | bytes 417792
  666.7 5.7 copy-start.7
  666.7 5.9 copy-start.9
  672.5 3.8 copy-start.22
  676.3 2.4 copy-start.6
  676.4 3.4 copy-start.8
  683.8 1.4 copy-start.3
  683.8 2.2 copy-start.5
  692.4 154.6 %all-reduce.18.cloned.1.call-start = ((), (), s32[]{:S(2)}) async-start(), calls=%async_computation.16 | async-start | bytes 9437184 | tf_op jit(solution)/shard_map/psum | solution.py:72
  692.5 5.1 copy-start.4
  692.5 5.1 collective-permute-start.1
  698.4 4.3 copy-start.11
  701.3 1.0 copy-start.12
  701.3 1.4 copy-start.13
  712.7 0.7 copy-start.17
  712.7 745.4 %reduce-scatter.12.cloned.1.call-start = ((), (), s32[]{:S(2)}) async-start(), calls=%async_computation.13 | async-start | bytes 45121536 | tf_op jit(solution)/shard_map/reduce_scatter | solution.py:130
  740.0 1.3 copy-start.10
  740.1 858.2 %reduce-scatter.10.cloned.1.call-start = ((), (), s32[]{:S(2)}) async-start(), calls=%async_computation.12 | async-start | bytes 5013504 | tf_op jit(solution)/shard_map/reduce_scatter | solution.py:129
  747.8 1.7 copy-start.2
  747.8 1.7 copy-start.15
  747.8 1.7 copy-start.19
  747.9 1078.6 %reduce-scatter.8.cloned.1.call-start = ((), (), s32[]{:S(2)}) async-start(), calls=%async_computation.11 | async-start | bytes 15040512 | tf_op jit(solution)/shard_map/reduce_scatter | solution.py:128
  760.3 1386.4 %reduce-scatter.14.cloned.1.call-start = ((), (), s32[]{:S(2)}) async-start(), calls=%async_computation.14 | async-start | bytes 22560768 | tf_op jit(solution)/shard_map/reduce_scatter | solution.py:131
  776.4 73.8 %copy-start.20 = (f32[1536]{0:T(1024)S(1)}, f32[1536]{0:T(1024)}, u32[]{:S(2)}) copy-start(f32[1536]{0:T(1024)} %get-tuple-element.36) | copy-start | bytes 18436
Sparse Core Ops, SparseCore 0:
  10.7 104.5 all-gather.4
  118.1 62.9 all-gather.6
  187.4 29.8 all-reduce.13
  220.8 232.6 all-gather.8
  456.6 131.6 all-gather.10
  636.9 29.7 all-reduce.15
  692.6 119.4 reduce-scatter.15
  815.4 31.6 all-reduce.17
  853.3 604.7 reduce-scatter.11
  1464.5 133.6 reduce-scatter.9
  1604.6 221.8 reduce-scatter.7
  1833.9 312.7 reduce-scatter.13
where the time goes:
time: 2160 us; the launch traced here: 2150 us
  waiting for transfers between devices  1750 us (81%)
  matrix products  173 us (8%)
  blocking collectives  122 us (6%)
  other arithmetic  43.6 us (2%)
  local copies, waits for them, and re-layouts  36.5 us (2%)
    reduce_scatter x1, waiting for transfers between devices, per_device(): lax.psum_scatter(grad_gate_up, 'seq', scatter_dimension=0, tiled=True)  539 us
    reduce_scatter x1, waiting for transfers between devices, per_device(): lax.psum_scatter(grad_down, 'seq', scatter_dimension=1, tiled=True)  320 us
    all_gather x1, waiting for transfers between devices, per_device(): lax.all_gather(gate_up, 'seq', axis=0, tiled=True)  230 us
    reduce_scatter x1, waiting for transfers between devices, per_device(): lax.psum_scatter(grad_in, 'seq', scatter_dimension=0, tiled=True)  228 us
    reduce_scatter x1, waiting for transfers between devices, per_device(): lax.psum_scatter(grad_out, 'seq', scatter_dimension=1, tiled=True)  135 us
    all_gather x1, waiting for transfers between devices, per_device(): lax.all_gather(w_down, 'seq', axis=1, tiled=True)  110 us
    unnamed x2, blocking collectives  87.1 us
    all_gather x1, waiting for transfers between devices, per_device(): lax.all_gather(w_out, 'seq', axis=1, tiled=True)  48 us
  transfers between devices with their start and end apart: 14, of which 14 were waited for; matrix products, arithmetic and copies ran while one was open for 8% of the time, Pallas kernels for 0%

commit v1 on v0

v1 whole, which is shorter than its diff:
```python
import jax
import jax.numpy as jnp
import numpy as np
from jax import lax
from jax.sharding import Mesh, PartitionSpec as P

epsilon = 1e-05
f32 = jnp.float32
bf16 = jnp.bfloat16
PLANE = ("y", "x")
SWAP = ((0, 1), (1, 0))


def dot(left, right, dims):
    return lax.dot_general(left, right, ((dims[0], dims[1]), ((), ())), preferred_element_type=f32)


def by_xor(stack):
    x_bit, y_bit = lax.axis_index("x") == 1, lax.axis_index("y") == 1
    stack = jnp.where(x_bit, jnp.stack([stack[1], stack[0], stack[3], stack[2]]), stack)
    return jnp.where(y_bit, jnp.stack([stack[2], stack[3], stack[0], stack[1]]), stack)


def plane_swap(value, offset):
    if offset == 1:
        return lax.ppermute(value, "x", SWAP)
    if offset == 2:
        return lax.ppermute(value, "y", SWAP)
    return lax.ppermute(value, PLANE, [(i, i ^ 3) for i in range(4)])


def plane_exchange(stack):
    relative = by_xor(stack)
    got = [relative[0]] + [plane_swap(relative[r], r) for r in (1, 2, 3)]
    return by_xor(jnp.stack(got))


def plane_gather(own):
    half = own.shape[0] // 32 * 16
    from_x = plane_swap(own, 1)
    from_y = plane_swap(own, 2)
    top = plane_swap(from_x[:half], 2)
    low = plane_swap(from_y[half:], 1)
    return [own, from_x, from_y, jnp.concatenate([top, low], axis=0)]


def plane_reduce(parts):
    half = parts.shape[1] // 32 * 16
    low_in = plane_swap(jnp.stack([parts[1, half:], parts[3, half:]]), 1)
    top_in = plane_swap(jnp.stack([parts[2, :half], parts[3, :half]]), 2)
    low_on = (parts[2, half:].astype(f32) + low_in[1].astype(f32)).astype(bf16)
    top_on = (parts[1, :half].astype(f32) + top_in[1].astype(f32)).astype(bf16)
    low_last = plane_swap(low_on, 2)
    top_last = plane_swap(top_on, 1)
    top = parts[0, :half].astype(f32) + top_in[0].astype(f32) + top_last.astype(f32)
    low = parts[0, half:].astype(f32) + low_in[0].astype(f32) + low_last.astype(f32)
    return jnp.concatenate([top, low], axis=0)


def core_swap(value):
    return lax.ppermute(value, "mp", SWAP)


def halves_turned(value):
    width = value.shape[-1] // 2
    return jnp.concatenate([value[..., width:], value[..., :width]], axis=-1)


def halo_forward(tails):
    planes = lax.axis_size("z")
    tails = halves_turned(tails)
    got = core_swap(tails)
    jump = [(2 * z + 1, 2 * z + 2) for z in range(planes - 1)]
    before = lax.ppermute(by_xor(tails)[3], ("z", "mp"), jump)
    shifted = by_xor(jnp.concatenate([before[None], by_xor(got)[:3]], axis=0))
    return jnp.where(lax.axis_index("mp") == 1, got, shifted)


def halo_backward(heads):
    planes = lax.axis_size("z")
    heads = halves_turned(heads)
    got = core_swap(heads)
    jump = [(2 * z + 2, 2 * z + 1) for z in range(planes - 1)]
    after = lax.ppermute(by_xor(heads)[0], ("z", "mp"), jump)
    shifted = by_xor(jnp.concatenate([by_xor(got)[1:], after[None]], axis=0))
    return jnp.where(lax.axis_index("mp") == 1, shifted, got)


def both_cores(own):
    other = core_swap(own)
    first = lax.axis_index("mp") == 0
    return jnp.concatenate([jnp.where(first, own, other), jnp.where(first, other, own)], axis=0)


def per_device(
    tokens, starts, w_in, w_out, gate_up, w_down, gain_mix, gain_ffn, conv_taps, cotangent
):
    planes = lax.axis_size("z")
    core = lax.axis_index("mp")
    rows, _, half_c = w_in.shape
    half_f = w_down.shape[0]
    width = tokens.shape[1]
    seg = tokens.shape[0] // 2
    chan, hid = half_c // 4, half_f // 4
    pad = -hid % 128
    hid_p = hid + pad
    plane_rows = 4 * rows
    tap_len = conv_taps.shape[2]

    def mine(value):
        return lax.dynamic_slice_in_dim(value, core * seg, seg, axis=0)

    gain_one = gain_mix.astype(f32)[:, None, None]
    gain_two = gain_ffn.astype(f32)[:, None, None]
    in_scaled = (w_in.astype(f32) * gain_one).astype(bf16).reshape(rows, 3, 4, chan)
    in_quart = jnp.transpose(in_scaled, (2, 0, 1, 3)).reshape(4, rows, 3 * chan)
    out_quart = jnp.transpose(w_out.reshape(4, chan, rows), (0, 2, 1))
    conv_pack = plane_exchange(jnp.concatenate([in_quart, out_quart], axis=2))
    conv_pack = conv_pack.reshape(plane_rows, 4 * chan)
    tap_piece = lax.ppermute(
        conv_taps.reshape(1, 3 * tap_len),
        ("z",) + PLANE,
        [(s, (s % planes) * 4 + s // planes) for s in range(4 * planes)],
    )
    tap_rows = jnp.pad(tap_piece, ((0, 15), (0, 4 * chan - 3 * tap_len)))
    conv_pack = jnp.concatenate([conv_pack, tap_rows], axis=0)
    conv_own = lax.all_gather(conv_pack, "z", axis=0, tiled=False)

    down_quart = jnp.transpose(w_down.reshape(4, hid, rows), (0, 2, 1))
    down_quart = jnp.pad(down_quart, ((0, 0), (0, 0), (0, pad)))
    down_pack = plane_exchange(down_quart).reshape(plane_rows, hid_p)
    down_own = lax.all_gather(down_pack, "z", axis=0, tiled=True)

    gu_scaled = (gate_up.astype(f32) * gain_two).astype(bf16).reshape(rows, 2, 4, hid)
    gu_quart = jnp.pad(jnp.transpose(gu_scaled, (2, 0, 1, 3)), ((0, 0),) * 3 + ((0, pad),))
    gu_pack = plane_exchange(gu_quart.reshape(4, rows, 2 * hid_p)).reshape(plane_rows, 2 * hid_p)
    gu_own = lax.all_gather(gu_pack, "z", axis=0, tiled=True)

    inputs = mine(tokens).astype(f32)
    inv_mix = lax.rsqrt(jnp.mean(inputs * inputs, axis=-1, keepdims=True) + epsilon)
    hat_mix = inputs * inv_mix
    begin_row = mine(starts).astype(bf16)[None]
    begin_rows = jnp.pad(begin_row, ((0, 15), (0, width - seg)))
    hat_all = plane_gather(jnp.concatenate([hat_mix.astype(bf16), begin_rows], axis=0))
    begins = jnp.stack([blk[seg, :seg] for blk in hat_all]).astype(f32)
    hat_all = jnp.concatenate([blk[:seg] for blk in hat_all], axis=0)
    cot = mine(cotangent)
    cot_all = jnp.concatenate(plane_gather(cot), axis=0)

    earlier = jnp.concatenate([jnp.zeros((4, 1), f32), begins[:, :-1]], axis=1)
    keep_one = (1.0 - begins)[:, :, None]
    keep_two = ((1.0 - begins) * (1.0 - earlier))[:, :, None]
    last_keep = 1.0 - begins[:, -1:]

    conv_other = core_swap(conv_own)
    pair = [conv_own, conv_other]
    taps = jnp.concatenate(
        [
            jnp.transpose(
                p[:, plane_rows, : 3 * tap_len].reshape(planes, 3, tap_len), (1, 0, 2)
            ).reshape(3, chan)
            for p in pair
        ],
        axis=1,
    ).astype(f32)
    in_full = jnp.concatenate(
        [p[:, :plane_rows, : 3 * chan].reshape(width, 3, chan) for p in pair], axis=2
    ).reshape(width, 6 * chan)
    out_full = jnp.concatenate(
        [p[:, :plane_rows, 3 * chan :].reshape(width, chan) for p in pair], axis=1
    )
    projected = dot(hat_all, in_full, ((1,), (0,))).reshape(4, seg, 6 * chan)
    b_part = projected[:, :, : 2 * chan]
    c_part = projected[:, :, 2 * chan : 4 * chan]
    x_part = projected[:, :, 4 * chan :]
    mixed_in = (b_part * x_part).astype(bf16)
    tails = jnp.stack(
        [(mixed_in[:, -2] * last_keep).astype(bf16), mixed_in[:, -1]], axis=1
    )
    extended = jnp.concatenate([halo_forward(tails), mixed_in], axis=1).astype(f32)
    convolved = (
        taps[0] * extended[:, 2:]
        + taps[1] * keep_one * extended[:, 1:-1]
        + taps[2] * keep_two * extended[:, :-2]
    )
    gated = (c_part * convolved).astype(bf16).reshape(4 * seg, 2 * chan)
    mixer = dot(gated, out_full, ((1,), (1,))).astype(bf16).reshape(4, seg, width)
    middle = inputs + plane_reduce(mixer)

    inv_ffn = lax.rsqrt(jnp.mean(middle * middle, axis=-1, keepdims=True) + epsilon)
    hat_ffn = middle * inv_ffn
    hat2_all = jnp.concatenate(plane_gather(hat_ffn.astype(bf16)), axis=0)
    down_other = core_swap(down_own)
    gu_other = core_swap(gu_own)
    acts, grads = [], []
    for down, gu in ((down_own, gu_own), (down_other, gu_other)):
        grad_act = dot(cot_all, down, ((1,), (0,)))
        gate_vals = dot(hat2_all, gu, ((1,), (0,)))
        gate_part, up_part = gate_vals[:, :hid_p], gate_vals[:, hid_p:]
        sig_gate = jax.nn.sigmoid(gate_part)
        silu_gate = gate_part * sig_gate
        acts.append((silu_gate * up_part).astype(bf16))
        grad_gate = grad_act * up_part * sig_gate * (1.0 + gate_part * (1.0 - sig_gate))
        grads.append(jnp.concatenate([grad_gate, grad_act * silu_gate], axis=1).astype(bf16))
    grad_hat2 = (dot(grads[0], gu_own, ((1,), (1,))) + dot(grads[1], gu_other, ((1,), (1,)))).astype(bf16)
    ffn_out = (dot(acts[0], down_own, ((1,), (1,))) + dot(acts[1], down_other, ((1,), (1,)))).astype(bf16)

    def weight_grad(left, own_right, other_right):
        theirs = core_swap(dot(left, other_right, ((0,), (0,))).astype(bf16))
        return (dot(left, own_right, ((0,), (0,))) + theirs.astype(f32)).astype(bf16)

    grad_down = weight_grad(cot_all, acts[0], acts[1])
    grad_down = lax.psum_scatter(grad_down, "z", scatter_dimension=0, tiled=True)
    grad_gu = weight_grad(hat2_all, grads[0], grads[1])
    grad_gu = lax.psum_scatter(grad_gu, "z", scatter_dimension=0, tiled=True)

    grad_hat2 = plane_reduce(grad_hat2.reshape(4, seg, width))
    inner = jnp.mean(grad_hat2 * hat_ffn, axis=-1, keepdims=True)
    grad_middle = cot.astype(f32) + inv_ffn * (grad_hat2 - hat_ffn * inner)
    output_vals = (middle + plane_reduce(ffn_out.reshape(4, seg, width))).astype(bf16)

    grad_mixer = jnp.concatenate(plane_gather(grad_middle.astype(bf16)), axis=0)
    grad_gated = dot(grad_mixer, out_full, ((1,), (0,))).reshape(4, seg, 2 * chan)
    grad_out = dot(grad_mixer, gated, ((0,), (0,)))
    grad_c = grad_gated * convolved
    grad_conv = grad_gated * c_part
    grad_taps = jnp.stack(
        [
            jnp.sum(grad_conv * extended[:, 2:], axis=(0, 1)),
            jnp.sum(grad_conv * keep_one * extended[:, 1:-1], axis=(0, 1)),
            jnp.sum(grad_conv * keep_two * extended[:, :-2], axis=(0, 1)),
        ]
    )
    term_zero = taps[0] * grad_conv
    term_one = taps[1] * keep_one * grad_conv
    term_two = taps[2] * keep_two * grad_conv
    grad_ext = (
        jnp.pad(term_zero, ((0, 0), (2, 0), (0, 0)))
        + jnp.pad(term_one, ((0, 0), (1, 1), (0, 0)))
        + jnp.pad(term_two, ((0, 0), (0, 2), (0, 0)))
    )
    back = halo_backward(grad_ext[:, :2])
    tail_gate = jnp.stack([last_keep, jnp.ones((4, 1), f32)], axis=1)
    grad_mixed = jnp.concatenate(
        [grad_ext[:, 2:-2], grad_ext[:, -2:] + back * tail_gate], axis=1
    )
    grad_mixed = grad_mixed.astype(bf16).astype(f32)
    grad_proj = jnp.concatenate(
        [grad_mixed * x_part, grad_c, grad_mixed * b_part], axis=2
    ).astype(bf16).reshape(4 * seg, 6 * chan)
    grad_hat1 = dot(grad_proj, in_full, ((1,), (1,))).astype(bf16)
    grad_in = dot(hat_all, grad_proj, ((0,), (0,))).reshape(width, 3, 2, chan)

    def conv_half(which):
        body = jnp.concatenate(
            [
                grad_in[:, :, which].reshape(width, 3 * chan),
                grad_out[:, which * chan : (which + 1) * chan],
            ],
            axis=1,
        ).reshape(planes, plane_rows, 4 * chan)
        piece = grad_taps[:, which * chan : (which + 1) * chan].reshape(3, planes, tap_len)
        piece = jnp.transpose(piece, (1, 0, 2)).reshape(planes, 1, 3 * tap_len)
        piece = jnp.pad(piece, ((0, 0), (0, 15), (0, 4 * chan - 3 * tap_len)))
        return jnp.concatenate([body, piece], axis=1)

    theirs = core_swap(conv_half(1).astype(bf16))
    conv_grads = (conv_half(0) + theirs.astype(f32)).astype(bf16)
    conv_grads = lax.psum_scatter(conv_grads, "z", scatter_dimension=0, tiled=False)

    grad_hat1 = plane_reduce(grad_hat1.reshape(4, seg, width))
    inner = jnp.mean(grad_hat1 * hat_mix, axis=-1, keepdims=True)
    grad_inputs = grad_middle + inv_mix * (grad_hat1 - hat_mix * inner)

    red_down = plane_exchange(grad_down.reshape(4, rows, hid_p))[:, :, :hid]
    red_down = jnp.transpose(red_down, (0, 2, 1)).reshape(half_f, rows).astype(f32)
    red_gu = plane_exchange(grad_gu.reshape(4, rows, 2 * hid_p)).reshape(4, rows, 2, hid_p)
    red_gu = jnp.transpose(red_gu[..., :hid], (1, 2, 0, 3)).reshape(rows, 2, half_f).astype(f32)
    red_conv = plane_exchange(conv_grads[:plane_rows].reshape(4, rows, 4 * chan)).astype(f32)
    red_in = red_conv[:, :, : 3 * chan].reshape(4, rows, 3, chan)
    red_in = jnp.transpose(red_in, (1, 2, 0, 3)).reshape(rows, 3, half_c)
    red_out = jnp.transpose(red_conv[:, :, 3 * chan :], (0, 2, 1)).reshape(half_c, rows)
    red_taps = lax.ppermute(
        conv_grads[plane_rows, : 3 * tap_len].astype(f32).reshape(3, 1, tap_len),
        ("z",) + PLANE,
        [((s % planes) * 4 + s // planes, s) for s in range(4 * planes)],
    )
    gains = jnp.stack(
        [
            jnp.sum(red_in * w_in.astype(f32), axis=(1, 2)),
            jnp.sum(red_gu * gate_up.astype(f32), axis=(1, 2)),
        ]
    )
    gains = gains + core_swap(gains)
    return (
        both_cores(output_vals),
        both_cores(grad_inputs),
        red_in * gain_one,
        red_out,
        red_gu * gain_two,
        red_down,
        gains[0],
        gains[1],
        red_taps,
    )


def solution(mesh):
    seq, cores = mesh.shape["seq"], mesh.shape["mp"]
    split = Mesh(np.asarray(mesh.devices).reshape(seq // 4, 2, 2, cores), ("z", "y", "x", "mp"))
    by = ("z", "y", "x")
    weights = (
        P(by, None, "mp"),
        P("mp", by),
        P(by, None, "mp"),
        P("mp", by),
        P(by),
        P(by),
        P(None, "mp", by),
    )
    return jax.shard_map(
        per_device,
        mesh=split,
        in_specs=(P(by, None), P(by)) + weights + (P(by, None),),
        out_specs=(P(by, None), P(by, None)) + weights,
        check_vma=False,
    )
```

time: 2160 us -> 810 us (0.38)
  waiting for transfers between devices: 1750 us -> 269 us
  local copies, waits for them, and re-layouts: 36.5 us -> 169 us
  blocking collectives: 122 us -> 0 us
  starting transfers between devices: 8.12 us -> 75.4 us
  other arithmetic: 43.6 us -> 97.4 us
    reduce_scatter x4 -> x3, waiting for transfers between devices: 1220 us -> 20 us  [the longest x1 19.9 us: per_device(): grad_gu = lax.psum_scatter(grad_gu, 'z', scatter_dimension=0, tiled=True)]
    all_gather x4 -> x3, waiting for transfers between devices: 415 us -> 0.01 us  [the longest x1 0.01 us: per_device(): conv_own = lax.all_gather(conv_pack, 'z', axis=0, tiled=False)]
    ppermute x2 -> x65, waiting for transfers between devices: 3.23 us -> 249 us  [the longest x22 146 us: plane_swap(): return lax.ppermute(value, 'y', SWAP)]
    unnamed x2 -> x0, blocking collectives: 87.1 us -> none
    psum x3 -> x0, waiting for transfers between devices: 75.4 us -> none  [the longest x1 33.4 us: per_device(): lax.psum(jnp.dot(act_vals, down_full, preferred_element_type=jnp.float32)...]
    ppermute x2 -> x65, starting transfers between devices: 7.64 us -> 74.5 us  [the longest x22 22.4 us: plane_swap(): return lax.ppermute(value, 'y', SWAP)]
    slice x3 -> x73, local copies, waits for them, and re-layouts: 8.17 us -> 46.8 us  [the longest x4 7.93 us: per_device(): p[:, :plane_rows, :3 * chan].reshape(width, 3, chan)]
    unnamed x13 -> x6, waiting for transfers between devices: 37.1 us -> 0.1 us
  transfers between devices with their start and end apart: 14 -> 71, of which waited for: 14 -> 31; matrix products, arithmetic and copies ran while one was open for 8% -> 48% of each run, Pallas kernels for 0% -> 0%
where the time goes in v1:
time: 810 us; the launch traced here: 800 us
  waiting for transfers between devices  269 us (33%)
  matrix products  174 us (21%)
  local copies, waits for them, and re-layouts  169 us (21%)
  other arithmetic  97.4 us (12%)
  starting transfers between devices  75.4 us (9%)
  between operations  16.4 us (2%)
    dot_general x18, matrix products, dot(): lax.dot_general(left, right, ((dims[0], dims[1]), ((), ())), preferred_el...  174 us
    ppermute x22, waiting for transfers between devices, plane_swap(): return lax.ppermute(value, 'y', SWAP)  146 us
    ppermute x22, waiting for transfers between devices, plane_swap(): return lax.ppermute(value, 'x', SWAP)  96.9 us
    unnamed x184, local copies, waits for them, and re-layouts  37.2 us
    concatenate x6, local copies, waits for them, and re-layouts, conv_half(): jnp.concatenate([grad_in[:, :, which].reshape(width, 3 * chan), grad_out[...  22.7 us
    ppermute x22, starting transfers between devices, plane_swap(): return lax.ppermute(value, 'y', SWAP)  22.4 us
    ppermute x11, starting transfers between devices, core_swap(): return lax.ppermute(value, 'mp', SWAP)  21.5 us
    reduce_scatter x1, waiting for transfers between devices, per_device(): grad_gu = lax.psum_scatter(grad_gu, 'z', scatter_dimension=0, tiled=True)  19.9 us
  transfers between devices with their start and end apart: 71, of which 31 were waited for; matrix products, arithmetic and copies ran while one was open for 48% of the time, Pallas kernels for 0%

profile of v1, /device:TPU:25, one launch (start us, length us, event | category | flops | bytes accessed | tf_op | source)
XLA Modules:
  0.0 800.3 jit_solution(9227062494151798314)
XLA Ops:
  15.1 3.7 collective-permute-start.7
  18.8 3.0 collective-permute-done.6
  44.0 3.5 reshape.346
  55.9 21.9 %collective-permute-done.21 = bf16[96,1792]{1,0:T(8,128)(2,1)S(1)} collective-permute-done((bf16[96,1792]{1,0:T(8,128)(2,1)S(1)}, bf16[96,1792]{1,0:T(8,128)(2,1)S(1)}, u32[]{:S(2)}, u32[]{:S(2)}) %collective-permute-start.21) | collective-permute-done | bytes 344096 | tf_op jit(solution)/shard_map/ppermute | solution.py:28
  94.2 7.0 collective-permute-done.2
  101.2 11.9 %fusion.5 = bf16[1536,1536]{1,0:T(8,128)(2,1)} fusion(bf16[208,1536]{1,0:T(8,128)(2,1)S(1)} %collective-permute-done.3, bf16[192,1536]{1,0:T(8,128)(2,1)} %collective-permute-done.2, bf16[384,1536]{1,0:T(8,128)(2,1)S(1)} %slice.990, bf16[384,1536]{1,0:T(8,128)(2,1)S(1)} %slice.989, bf16[384,1536]{1,0:T(8,128)(2,1)S(1)} %copy-done.16), kind=kLoop, calls=%fused_computation.26 | loop fusion | flops 23592960 | bytes 9486336 | tf_op jit(solution)/shard_map/concatenate | solution.py:146
  113.7 3.0 copy.140
  116.7 3.0 reshape.336
  124.1 3.0 copy.141
  127.1 3.0 reshape.337
  131.5 9.2 %fusion.104 = f32[4,384,1152]{2,1,0:T(8,128)S(1)} fusion(bf16[4,384,1536]{2,1,0:T(8,128)(2,1)} %bitcast.242, bf16[1536,1152,1]{0,1,2:T(8,128)(2,1)} %bitcast.290), kind=kOutput, calls=%fused_computation.335 | convolution fusion | flops 5435817984 | bytes 15335424 | tf_op jit(solution)/shard_map/dot_general | solution.py:15
  140.7 3.0 copy-done.5
  149.2 4.3 multiply_convert_fusion.7
  158.4 24.6 %collective-permute-done.11 = bf16[2,192,1536]{2,1,0:T(8,128)(2,1)S(1)} collective-permute-done((bf16[2,192,1536]{2,1,0:T(8,128)(2,1)S(1)}, bf16[2,192,1536]{2,1,0:T(8,128)(2,1)S(1)}, u32[]{:S(2)}, u32[]{:S(2)}) %collective-permute-start.11) | collective-permute-done | bytes 1179680 | tf_op jit(solution)/shard_map/ppermute | solution.py:28
  188.7 8.6 %collective-permute-done.12 = bf16[192,1536]{1,0:T(8,128)(2,1)S(1)} collective-permute-done((bf16[192,1536]{1,0:T(8,128)(2,1)S(1)}, bf16[192,1536]{1,0:T(8,128)(2,1)S(1)}, u32[]{:S(2)}, u32[]{:S(2)}) %collective-permute-start.12) | collective-permute-done | bytes 589856 | tf_op jit(solution)/shard_map/ppermute | solution.py:26
  201.2 21.3 %collective-permute-done.32 = bf16[384,1536]{1,0:T(8,128)(2,1)S(1)} collective-permute-done((bf16[384,1536]{1,0:T(8,128)(2,1)S(1)}, bf16[384,1536]{1,0:T(8,128)(2,1)S(1)}, u32[]{:S(2)}, u32[]{:S(2)}) %collective-permute-start.32) | collective-permute-done | bytes 1179680 | tf_op jit(solution)/shard_map/ppermute | solution.py:26
  226.1 34.4 %collective-permute-done.34 = bf16[192,1536]{1,0:T(8,128)(2,1)S(1)} collective-permute-done((bf16[192,1536]{1,0:T(8,128)(2,1)S(1)}, bf16[192,1536]{1,0:T(8,128)(2,1)S(1)}, u32[]{:S(2)}, u32[]{:S(2)}) %collective-permute-start.34) | collective-permute-done | bytes 589856 | tf_op jit(solution)/shard_map/ppermute | solution.py:28
  263.3 3.7 collective-permute-start.26
  270.4 3.1 constant_dynamic-update-slice_fusion.4
  275.8 6.8 collective-permute-done.18
  283.4 13.1 %fusion.105 = f32[1536,1792]{1,0:T(8,128)} fusion(bf16[1536,1536]{1,0:T(8,128)(2,1)} %constant_dynamic-update-slice_fusion.2, bf16[1536,1792]{1,0:T(8,128)(2,1)S(1)} %copy-done.69), kind=kOutput, calls=%fused_computation.336 | convolution fusion | flops 8455716864 | bytes 21233664 | tf_op jit(solution)/shard_map/dot_general | solution.py:15
  296.6 12.3 %multiply_convert_fusion.3 = (bf16[1536,896]{1,0:T(8,128)(2,1)}, bf16[1536,896]{1,0:T(8,128)(2,1)}, bf16[1536,896]{1,0:T(8,128)(2,1)}) fusion(f32[1536,1792]{1,0:T(8,128)} %fusion.105, bf16[1536,1536]{1,0:T(8,128)(2,1)} %constant_dynamic-update-slice_fusion.7, bf16[1536,896]{1,0:T(8,128)(2,1)S(1)} %copy-done.71), kind=kOutput, calls=%fused_computation.16 | convolution fusion | flops 4248502272 | bytes 26738688 | tf_op jit(solution)/shard_map/dot_general | solution.py:15
  308.9 13.3 %fusion.8 = f32[1536,1536]{1,0:T(8,128)} fusion(bf16[1536,1792]{1,0:T(8,128)(2,1)S(1)} %copy-done.69, bf16[1536,896]{1,0:T(8,128)(2,1)} %get-tuple-element.67, bf16[1536,896]{1,0:T(8,128)(2,1)} %get-tuple-element.66), kind=kOutput, calls=%fused_computation.31 | convolution fusion | flops 8466726912 | bytes 20447232 | tf_op jit(solution)/shard_map/dot_general | solution.py:15
  322.2 11.3 %fusion.107 = f32[1536,1792]{1,0:T(8,128)} fusion(bf16[1536,1536]{1,0:T(8,128)(2,1)S(1)} %bitcast.314, bf16[1536,1792]{1,0:T(8,128)(2,1)S(1)} %collective-permute-done.25), kind=kOutput, calls=%fused_computation.338 | convolution fusion | flops 8455716864 | bytes 21233664 | tf_op jit(solution)/shard_map/dot_general | solution.py:15
  333.5 13.4 %multiply_convert_fusion.1 = (bf16[1536,896]{1,0:T(8,128)(2,1)S(1)}, bf16[1536,896]{1,0:T(8,128)(2,1)}, bf16[1536,896]{1,0:T(8,128)(2,1)}) fusion(f32[1536,1792]{1,0:T(8,128)} %fusion.107, bf16[1536,1536]{1,0:T(8,128)(2,1)} %constant_dynamic-update-slice_fusion.7, bf16[1536,896]{1,0:T(8,128)(2,1)} %collective-permute-done.26), kind=kOutput, calls=%fused_computation.14 | convolution fusion | flops 4248502272 | bytes 26738688 | tf_op jit(solution)/shard_map/dot_general | solution.py:15
  346.9 14.2 %add_convert_fusion.1 = bf16[1536,1536]{1,0:T(8,128)(2,1)S(1)} fusion(f32[1536,1536]{1,0:T(8,128)} %fusion.8, bf16[1536,1792]{1,0:T(8,128)(2,1)} %copy-done.70, bf16[1536,896]{1,0:T(8,128)(2,1)} %get-tuple-element.65, bf16[1536,896]{1,0:T(8,128)(2,1)S(1)} %get-tuple-element.64), kind=kOutput, calls=%fused_computation.1 | convolution fusion | flops 8471445504 | bytes 25165824 | tf_op jit(solution)/shard_map/dot_general | solution.py:15
  363.8 23.6 %collective-permute-done.36 = bf16[2,192,1536]{2,1,0:T(8,128)(2,1)S(1)} collective-permute-done((bf16[2,192,1536]{2,1,0:T(8,128)(2,1)S(1)}, bf16[2,192,1536]{2,1,0:T(8,128)(2,1)S(1)}, u32[]{:S(2)}, u32[]{:S(2)}) %collective-permute-start.36) | collective-permute-done | bytes 1179680 | tf_op jit(solution)/shard_map/ppermute | solution.py:28
  390.3 8.8 %convolution_convert_fusion.3 = bf16[1536,896]{1,0:T(8,128)(2,1)} fusion(bf16[1536,1536]{1,0:T(8,128)(2,1)} %constant_dynamic-update-slice_fusion.7, bf16[1536,896]{1,0:T(8,128)(2,1)S(1)} %copy-done.77), kind=kOutput, calls=%fused_computation.30 | convolution fusion | flops 4229234688 | bytes 10223616 | tf_op jit(solution)/shard_map/dot_general | solution.py:15
  399.1 3.1 collective-permute-start.59
  408.6 22.0 %collective-permute-done.40 = bf16[384,1536]{1,0:T(8,128)(2,1)} collective-permute-done((bf16[384,1536]{1,0:T(8,128)(2,1)}, bf16[384,1536]{1,0:T(8,128)(2,1)}, u32[]{:S(2)}, u32[]{:S(2)}) %collective-permute-start.40) | collective-permute-done | bytes 1179680 | tf_op jit(solution)/shard_map/ppermute | solution.py:26
  434.5 9.3 %add_convert_fusion.3 = bf16[1536,896]{1,0:T(8,128)(2,1)} fusion(bf16[1536,896]{1,0:T(8,128)(2,1)} %collective-permute-done.59, bf16[1536,1536]{1,0:T(8,128)(2,1)} %constant_dynamic-update-slice_fusion.7, bf16[1536,896]{1,0:T(8,128)(2,1)} %get-tuple-element.69), kind=kOutput, calls=%fused_computation.12 | convolution fusion | flops 4231987200 | bytes 12976128 | tf_op jit(solution)/shard_map/dot_general | solution.py:15
  452.4 3.7 collective-permute-done.43
  457.0 4.6 fusion.33
  461.7 3.3 multiply_reduce_fusion.2
  470.2 3.4 fusion.108
  474.4 4.8 collective-permute-start.44
  500.4 5.8 copy.154
  506.1 8.9 %fusion.6 = f32[1536,3,2,192]{0,3,2,1:T(8,128)S(1)} fusion(bf16[3,2,192,1536]{3,2,1,0:T(8,128)(2,1)} %bitcast.268, bf16[1536,1536]{1,0:T(8,128)(2,1)} %fusion.5), kind=kOutput, calls=%fused_computation.28 | convolution fusion | flops 5435817984 | bytes 15335424 | tf_op jit(solution)/shard_map/dot_general | solution.py:15
  519.3 4.1 concatenate.157
  523.4 4.7 copy.159
  528.1 3.8 fusion.14
  531.9 3.4 collective-permute-start.51
  535.3 13.2 %convolution_convert_fusion = bf16[1536,1792]{1,0:T(8,128)(2,1)} fusion(bf16[1536,1536]{1,0:T(8,128)(2,1)} %constant_dynamic-update-slice_fusion.2, bf16[1536,896]{1,0:T(8,128)(2,1)} %get-tuple-element.65, bf16[1536,896]{1,0:T(8,128)(2,1)S(1)} %copy-done.79), kind=kOutput, calls=%fused_computation.3 | convolution fusion | flops 8469479424 | bytes 15728640 | tf_op jit(solution)/shard_map/dot_general | solution.py:15
  548.6 7.7 fusion.106
  562.0 4.0 slice.1139
  566.1 5.3 concatenate.153
  571.3 4.0 copy.155
  575.4 4.6 copy.163
  579.9 5.0 fusion.1
  585.0 8.9 %add_convert_fusion.2 = bf16[1536,1536]{1,0:T(8,128)(2,1)S(1)} fusion(f32[1536,1536]{1,0:T(8,128)} %fusion.106, bf16[1536,896]{1,0:T(8,128)(2,1)} %get-tuple-element.68, bf16[1536,896]{1,0:T(8,128)(2,1)} %collective-permute-done.26), kind=kOutput, calls=%fused_computation.2 | convolution fusion | flops 4232577024 | bytes 19660800 | tf_op jit(solution)/shard_map/dot_general | solution.py:15
  599.5 6.4 convolution_convert_fusion.1
  611.1 12.7 %add_convert_fusion = bf16[1536,1792]{1,0:T(8,128)(2,1)} fusion(bf16[1536,1792]{1,0:T(8,128)(2,1)} %collective-permute-done.55, bf16[1536,1536]{1,0:T(8,128)(2,1)S(1)} %bitcast.316, bf16[1536,896]{1,0:T(8,128)(2,1)S(1)} %copy-done.75, bf16[1536,896]{1,0:T(8,128)(2,1)S(1)} %copy-done.74), kind=kOutput, calls=%fused_computation | convolution fusion | flops 8474984448 | bytes 21233664 | tf_op jit(solution)/shard_map/dot_general | solution.py:15
  629.6 18.3 %collective-permute-done.46 = bf16[2,192,1536]{2,1,0:T(8,128)(2,1)} collective-permute-done((bf16[2,192,1536]{2,1,0:T(8,128)(2,1)}, bf16[2,192,1536]{2,1,0:T(8,128)(2,1)}, u32[]{:S(2)}, u32[]{:S(2)}) %collective-permute-start.46) | collective-permute-done | bytes 1179680 | tf_op jit(solution)/shard_map/ppermute | solution.py:28
  647.9 3.0 collective-permute-done.48
  654.8 8.7 %collective-permute-done.28 = bf16[192,1536]{1,0:T(8,128)(2,1)S(1)} collective-permute-done((bf16[192,1536]{1,0:T(8,128)(2,1)S(1)}, bf16[192,1536]{1,0:T(8,128)(2,1)S(1)}, u32[]{:S(2)}, u32[]{:S(2)}) %collective-permute-start.28) | collective-permute-done | bytes 589856 | tf_op jit(solution)/shard_map/ppermute | solution.py:26
  665.6 10.6 %collective-permute-done.47 = bf16[192,1536]{1,0:T(8,128)(2,1)S(1)} collective-permute-done((bf16[192,1536]{1,0:T(8,128)(2,1)S(1)}, bf16[192,1536]{1,0:T(8,128)(2,1)S(1)}, u32[]{:S(2)}, u32[]{:S(2)}) %collective-permute-start.47) | collective-permute-done | bytes 589856 | tf_op jit(solution)/shard_map/ppermute | solution.py:26
  679.8 3.4 fusion.21
  684.5 5.8 collective-permute-done.31
  693.3 4.3 broadcast_select_fusion.3
  705.8 4.5 collective-permute-done.62
  725.2 19.9 %reduce-scatter.6.cloned.1.call-done = bf16[384,1792]{1,0:T(8,128)(2,1)} async-done(((bf16[1536,1792]{1,0:T(8,128)(2,1)}), bf16[384,1792]{1,0:T(8,128)(2,1)}) %reduce-scatter.6.cloned.1.call-update) | async-done | bytes 1376272 | tf_op jit(solution)/shard_map/reduce_scatter | solution.py:215
  757.7 7.6 collective-permute-done.58
  775.8 4.5 reshape.362
  780.3 6.2 fusion.13
  (532 shorter events, 238.4 us)
Async XLA Ops:
  7.2 74.1 %all-gather.9.cloned.1.call-start = ((), (), s32[]{:S(2)}) async-start(), calls=%async_computation.8 | async-start | bytes 3072000 | tf_op jit(solution)/shard_map/all_gather | solution.py:127
  12.3 9.5 %collective-permute-start.6 = (bf16[96,768]{0,1:T(8,128)(2,1)S(1)}, bf16[96,768]{0,1:T(8,128)(2,1)S(1)}, u32[]{:S(2)}, u32[]{:S(2)}) collective-permute-start(bf16[96,768]{0,1:T(8,128)(2,1)S(1)} %get-tuple-element.151), channel_id=1, source_target_pairs={{0,4},{4,0},{1,5},{5,1},{2,6},{6,2},{3,7},{7,3},{8,12},{12,8},{9,1... | collective-permute-start | bytes 442376 | tf_op jit(solution)/shard_map/ppermute | solution.py:28
  13.6 8.2 %collective-permute-start.5 = (bf16[96,768]{0,1:T(8,128)(2,1)S(1)}, bf16[96,768]{0,1:T(8,128)(2,1)S(1)}, u32[]{:S(2)}, u32[]{:S(2)}) collective-permute-start(bf16[96,768]{0,1:T(8,128)(2,1)S(1)} %get-tuple-element.152), channel_id=1, source_target_pairs={{0,6},{2,4},{4,2},{6,0},{1,7},{3,5},{5,3},{7,1},{8,14},{10,12},{12... | collective-permute-start | bytes 442376 | tf_op jit(solution)/shard_map/ppermute | solution.py:29
  14.8 8.5 %collective-permute-start.4 = (bf16[96,768]{0,1:T(8,128)(2,1)S(1)}, bf16[96,768]{0,1:T(8,128)(2,1)S(1)}, u32[]{:S(2)}, u32[]{:S(2)}) collective-permute-start(bf16[96,768]{0,1:T(8,128)(2,1)S(1)} %get-tuple-element.150), channel_id=1, source_target_pairs={{0,2},{2,0},{1,3},{3,1},{4,6},{6,4},{5,7},{7,5},{8,10},{10,8},{9,1... | collective-permute-start | bytes 442376 | tf_op jit(solution)/shard_map/ppermute | solution.py:26
  15.1 9.3 %collective-permute-start.7 = (bf16[1,144]{1,0:T(2,128)(2,1)S(1)}, bf16[1,144]{1,0:T(2,128)(2,1)S(1)}, u32[]{:S(2)}, u32[]{:S(2)}) collective-permute-start(bf16[1,144]{1,0:T(2,128)(2,1)S(1)} %reshape.335), channel_id=1, source_target_pairs={{0,0},{2,8},{4,16},{6,24},{8,2},{10,10},{12,18},{14,26},{16,4},{18... | collective-permute-start | bytes 872 | tf_op jit(solution)/shard_map/ppermute | solution.py:120
  25.3 238.0 %all-gather.7.cloned.1.call-start = ((), (), s32[]{:S(2)}) async-start(), calls=%async_computation.4 | async-start | bytes 3440640 | tf_op jit(solution)/shard_map/all_gather | solution.py:132
  27.3 7.0 collective-permute-start.24
  31.9 46.2 %collective-permute-start.1 = (bf16[400,1536]{1,0:T(8,128)(2,1)}, bf16[400,1536]{1,0:T(8,128)(2,1)}, u32[]{:S(2)}, u32[]{:S(2)}) collective-permute-start(bf16[400,1536]{1,0:T(8,128)(2,1)} %fusion.27), channel_id=1, source_target_pairs={{0,4},{4,0},{1,5},{5,1},{2,6},{6,2},{3,7},{7,3},{8,12},{12,8},{9,1... | collective-permute-start | bytes 3686408 | tf_op jit(solution)/shard_map/ppermute | solution.py:28
  33.1 50.9 %collective-permute-start = (bf16[400,1536]{1,0:T(8,128)(2,1)}, bf16[400,1536]{1,0:T(8,128)(2,1)}, u32[]{:S(2)}, u32[]{:S(2)}) collective-permute-start(bf16[400,1536]{1,0:T(8,128)(2,1)} %fusion.27), channel_id=1, source_target_pairs={{0,2},{2,0},{1,3},{3,1},{4,6},{6,4},{5,7},{7,5},{8,10},{10,8},{9,1... | collective-permute-start | bytes 3686408 | tf_op jit(solution)/shard_map/ppermute | solution.py:26
  37.4 229.6 %all-gather.5.cloned.1.call-start = ((), (), s32[]{:S(2)}) async-start(), calls=%async_computation.3 | async-start | bytes 6881280 | tf_op jit(solution)/shard_map/all_gather | solution.py:137
  53.2 24.6 %collective-permute-start.21 = (bf16[96,1792]{1,0:T(8,128)(2,1)S(1)}, bf16[96,1792]{1,0:T(8,128)(2,1)S(1)}, u32[]{:S(2)}, u32[]{:S(2)}) collective-permute-start(bf16[96,1792]{1,0:T(8,128)(2,1)S(1)} %get-tuple-element.125), channel_id=1, source_target_pairs={{0,4},{4,0},{1,5},{5,1},{2,6},{6,2},{3,7},{7,3},{8,12},{12,8},{9,1... | collective-permute-start | bytes 1032200 | tf_op jit(solution)/shard_map/ppermute | solution.py:28
  54.4 23.4 %collective-permute-start.20 = (bf16[96,1792]{1,0:T(8,128)(2,1)S(1)}, bf16[96,1792]{1,0:T(8,128)(2,1)S(1)}, u32[]{:S(2)}, u32[]{:S(2)}) collective-permute-start(bf16[96,1792]{1,0:T(8,128)(2,1)S(1)} %get-tuple-element.126), channel_id=1, source_target_pairs={{0,6},{2,4},{4,2},{6,0},{1,7},{3,5},{5,3},{7,1},{8,14},{10,12},{12... | collective-permute-start | bytes 1032200 | tf_op jit(solution)/shard_map/ppermute | solution.py:29
  55.6 22.2 %collective-permute-start.19 = (bf16[96,1792]{1,0:T(8,128)(2,1)S(1)}, bf16[96,1792]{1,0:T(8,128)(2,1)S(1)}, u32[]{:S(2)}, u32[]{:S(2)}) collective-permute-start(bf16[96,1792]{1,0:T(8,128)(2,1)S(1)} %get-tuple-element.124), channel_id=1, source_target_pairs={{0,2},{2,0},{1,3},{3,1},{4,6},{6,4},{5,7},{7,5},{8,10},{10,8},{9,1... | collective-permute-start | bytes 1032200 | tf_op jit(solution)/shard_map/ppermute | solution.py:26
  80.1 13.9 %collective-permute-start.3 = (bf16[208,1536]{1,0:T(8,128)(2,1)}, bf16[208,1536]{1,0:T(8,128)(2,1)S(1)}, u32[]{:S(2)}, u32[]{:S(2)}) collective-permute-start(bf16[208,1536]{1,0:T(8,128)(2,1)} %slice.992), channel_id=1, source_target_pairs={{0,2},{2,0},{1,3},{3,1},{4,6},{6,4},{5,7},{7,5},{8,10},{10,8},{9,1... | collective-permute-start | bytes 1916936 | tf_op jit(solution)/shard_map/ppermute | solution.py:26
  81.3 41.1 %collective-permute-start.8 = (bf16[4,400,768]{2,1,0:T(8,128)(2,1)}, bf16[4,400,768]{2,1,0:T(8,128)(2,1)}, u32[]{:S(2)}, u32[]{:S(2)}) collective-permute-start(bf16[4,400,768]{2,1,0:T(8,128)(2,1)} %bitcast.272), channel_id=1, source_target_pairs={{0,1},{1,0},{2,3},{3,2},{4,5},{5,4},{6,7},{7,6},{8,9},{9,8},{10,11... | collective-permute-start | bytes 7372808 | tf_op jit(solution)/shard_map/ppermute | solution.py:61
  85.9 15.3 %collective-permute-start.2 = (bf16[192,1536]{1,0:T(8,128)(2,1)}, bf16[192,1536]{1,0:T(8,128)(2,1)}, u32[]{:S(2)}, u32[]{:S(2)}) collective-permute-start(bf16[192,1536]{1,0:T(8,128)(2,1)} %slice.991), channel_id=1, source_target_pairs={{0,4},{4,0},{1,5},{5,1},{2,6},{6,2},{3,7},{7,3},{8,12},{12,8},{9,1... | collective-permute-start | bytes 1769480 | tf_op jit(solution)/shard_map/ppermute | solution.py:28
  88.6 609.0 %reduce-scatter.8.cloned.1.call-start = ((), (), s32[]{:S(2)}) async-start(), calls=%async_computation.7 | async-start | bytes 3440640 | tf_op jit(solution)/shard_map/reduce_scatter | solution.py:213
  156.5 26.5 %collective-permute-start.11 = (bf16[2,192,1536]{2,1,0:T(8,128)(2,1)S(1)}, bf16[2,192,1536]{2,1,0:T(8,128)(2,1)S(1)}, u32[]{:S(2)}, u32[]{:S(2)}) collective-permute-start(bf16[2,192,1536]{2,1,0:T(8,128)(2,1)S(1)} %stack.359), channel_id=1, source_target_pairs={{0,4},{4,0},{1,5},{5,1},{2,6},{6,2},{3,7},{7,3},{8,12},{12,8},{9,1... | collective-permute-start | bytes 3538952 | tf_op jit(solution)/shard_map/ppermute | solution.py:28
  158.0 26.2 %collective-permute-start.13 = (bf16[2,192,1536]{2,1,0:T(8,128)(2,1)S(1)}, bf16[2,192,1536]{2,1,0:T(8,128)(2,1)S(1)}, u32[]{:S(2)}, u32[]{:S(2)}) collective-permute-start(bf16[2,192,1536]{2,1,0:T(8,128)(2,1)S(1)} %pad_maximum_fusion.22), channel_id=1, source_target_pairs={{0,2},{2,0},{1,3},{3,1},{4,6},{6,4},{5,7},{7,5},{8,10},{10,8},{9,1... | collective-permute-start | bytes 3538952 | tf_op jit(solution)/shard_map/ppermute | solution.py:26
  184.5 12.7 %collective-permute-start.12 = (bf16[192,1536]{1,0:T(8,128)(2,1)S(1)}, bf16[192,1536]{1,0:T(8,128)(2,1)S(1)}, u32[]{:S(2)}, u32[]{:S(2)}) collective-permute-start(bf16[192,1536]{1,0:T(8,128)(2,1)S(1)} %get-tuple-element.96), channel_id=1, source_target_pairs={{0,2},{2,0},{1,3},{3,1},{4,6},{6,4},{5,7},{7,5},{8,10},{10,8},{9,1... | collective-permute-start | bytes 1769480 | tf_op jit(solution)/shard_map/ppermute | solution.py:26
  184.9 12.4 %collective-permute-start.14 = (bf16[192,1536]{1,0:T(8,128)(2,1)S(1)}, bf16[192,1536]{1,0:T(8,128)(2,1)S(1)}, u32[]{:S(2)}, u32[]{:S(2)}) collective-permute-start(bf16[192,1536]{1,0:T(8,128)(2,1)S(1)} %get-tuple-element.97), channel_id=1, source_target_pairs={{0,4},{4,0},{1,5},{5,1},{2,6},{6,2},{3,7},{7,3},{8,12},{12,8},{9,1... | collective-permute-start | bytes 1769480 | tf_op jit(solution)/shard_map/ppermute | solution.py:28
  186.4 36.2 %collective-permute-start.32 = (bf16[384,1536]{1,0:T(8,128)(2,1)S(1)}, bf16[384,1536]{1,0:T(8,128)(2,1)S(1)}, u32[]{:S(2)}, u32[]{:S(2)}) collective-permute-start(bf16[384,1536]{1,0:T(8,128)(2,1)S(1)} %get-tuple-element.57), channel_id=1, source_target_pairs={{0,2},{2,0},{1,3},{3,1},{4,6},{6,4},{5,7},{7,5},{8,10},{10,8},{9,1... | collective-permute-start | bytes 3538952 | tf_op jit(solution)/shard_map/ppermute | solution.py:26
  187.5 35.4 %collective-permute-start.33 = (bf16[384,1536]{1,0:T(8,128)(2,1)S(1)}, bf16[384,1536]{1,0:T(8,128)(2,1)S(1)}, u32[]{:S(2)}, u32[]{:S(2)}) collective-permute-start(bf16[384,1536]{1,0:T(8,128)(2,1)S(1)} %get-tuple-element.57), channel_id=1, source_target_pairs={{0,4},{4,0},{1,5},{5,1},{2,6},{6,2},{3,7},{7,3},{8,12},{12,8},{9,1... | collective-permute-start | bytes 3538952 | tf_op jit(solution)/shard_map/ppermute | solution.py:28
  199.8 61.5 %collective-permute-start.15 = (bf16[384,1536]{1,0:T(8,128)(2,1)}, bf16[384,1536]{1,0:T(8,128)(2,1)S(1)}, u32[]{:S(2)}, u32[]{:S(2)}) collective-permute-start(bf16[384,1536]{1,0:T(8,128)(2,1)} %get-tuple-element.59), channel_id=1, source_target_pairs={{0,2},{2,0},{1,3},{3,1},{4,6},{6,4},{5,7},{7,5},{8,10},{10,8},{9,1... | collective-permute-start | bytes 3538952 | tf_op jit(solution)/shard_map/ppermute | solution.py:26
  200.9 66.1 %collective-permute-start.16 = (bf16[384,1536]{1,0:T(8,128)(2,1)}, bf16[384,1536]{1,0:T(8,128)(2,1)}, u32[]{:S(2)}, u32[]{:S(2)}) collective-permute-start(bf16[384,1536]{1,0:T(8,128)(2,1)} %get-tuple-element.59), channel_id=1, source_target_pairs={{0,4},{4,0},{1,5},{5,1},{2,6},{6,2},{3,7},{7,3},{8,12},{12,8},{9,1... | collective-permute-start | bytes 3538952 | tf_op jit(solution)/shard_map/ppermute | solution.py:28
  222.6 37.9 %collective-permute-start.34 = (bf16[192,1536]{1,0:T(8,128)(2,1)S(1)}, bf16[192,1536]{1,0:T(8,128)(2,1)S(1)}, u32[]{:S(2)}, u32[]{:S(2)}) collective-permute-start(bf16[192,1536]{1,0:T(8,128)(2,1)S(1)} %slice.1091), channel_id=1, source_target_pairs={{0,4},{4,0},{1,5},{5,1},{2,6},{6,2},{3,7},{7,3},{8,12},{12,8},{9,1... | collective-permute-start | bytes 1769480 | tf_op jit(solution)/shard_map/ppermute | solution.py:28
  223.0 39.5 %collective-permute-start.35 = (bf16[192,1536]{1,0:T(8,128)(2,1)S(1)}, bf16[192,1536]{1,0:T(8,128)(2,1)S(1)}, u32[]{:S(2)}, u32[]{:S(2)}) collective-permute-start(bf16[192,1536]{1,0:T(8,128)(2,1)S(1)} %slice.1092), channel_id=1, source_target_pairs={{0,2},{2,0},{1,3},{3,1},{4,6},{6,4},{5,7},{7,5},{8,10},{10,8},{9,1... | collective-permute-start | bytes 1769480 | tf_op jit(solution)/shard_map/ppermute | solution.py:26
  262.2 11.7 %collective-permute-start.17 = (bf16[192,1536]{1,0:T(8,128)(2,1)}, bf16[192,1536]{1,0:T(8,128)(2,1)}, u32[]{:S(2)}, u32[]{:S(2)}) collective-permute-start(bf16[192,1536]{1,0:T(8,128)(2,1)} %slice.1059), channel_id=1, source_target_pairs={{0,4},{4,0},{1,5},{5,1},{2,6},{6,2},{3,7},{7,3},{8,12},{12,8},{9,1... | collective-permute-start | bytes 1769480 | tf_op jit(solution)/shard_map/ppermute | solution.py:28
  263.3 70.2 %collective-permute-start.26 = (bf16[1536,896]{1,0:T(8,128)(2,1)}, bf16[1536,896]{1,0:T(8,128)(2,1)}, u32[]{:S(2)}, u32[]{:S(2)}) collective-permute-start(bf16[1536,896]{1,0:T(8,128)(2,1)} %all-gather.7.cloned.1.call-done), channel_id=1, source_target_pairs={{0,1},{1,0},{2,3},{3,2},{4,5},{5,4},{6,7},{7,6},{8,9},{9,8},{10,11... | collective-permute-start | bytes 8257544 | tf_op jit(solution)/shard_map/ppermute | solution.py:61
  267.0 55.1 %collective-permute-start.25 = (bf16[1536,1792]{1,0:T(8,128)(2,1)}, bf16[1536,1792]{1,0:T(8,128)(2,1)S(1)}, u32[]{:S(2)}, u32[]{:S(2)}) collective-permute-start(bf16[1536,1792]{1,0:T(8,128)(2,1)} %all-gather.5.cloned.1.call-done), channel_id=1, source_target_pairs={{0,1},{1,0},{2,3},{3,2},{4,5},{5,4},{6,7},{7,6},{8,9},{9,8},{10,11... | collective-permute-start | bytes 16515080 | tf_op jit(solution)/shard_map/ppermute | solution.py:61
  268.1 14.5 %collective-permute-start.18 = (bf16[192,1536]{1,0:T(8,128)(2,1)S(1)}, bf16[192,1536]{1,0:T(8,128)(2,1)S(1)}, u32[]{:S(2)}, u32[]{:S(2)}) collective-permute-start(bf16[192,1536]{1,0:T(8,128)(2,1)S(1)} %slice.1060), channel_id=1, source_target_pairs={{0,2},{2,0},{1,3},{3,1},{4,6},{6,4},{5,7},{7,5},{8,10},{10,8},{9,1... | collective-permute-start | bytes 1769480 | tf_op jit(solution)/shard_map/ppermute | solution.py:26
  361.2 26.2 %collective-permute-start.36 = (bf16[2,192,1536]{2,1,0:T(8,128)(2,1)S(1)}, bf16[2,192,1536]{2,1,0:T(8,128)(2,1)S(1)}, u32[]{:S(2)}, u32[]{:S(2)}) collective-permute-start(bf16[2,192,1536]{2,1,0:T(8,128)(2,1)S(1)} %stack.361), channel_id=1, source_target_pairs={{0,4},{4,0},{1,5},{5,1},{2,6},{6,2},{3,7},{7,3},{8,12},{12,8},{9,1... | collective-permute-start | bytes 3538952 | tf_op jit(solution)/shard_map/ppermute | solution.py:28
  362.6 25.9 %collective-permute-start.38 = (bf16[2,192,1536]{2,1,0:T(8,128)(2,1)S(1)}, bf16[2,192,1536]{2,1,0:T(8,128)(2,1)S(1)}, u32[]{:S(2)}, u32[]{:S(2)}) collective-permute-start(bf16[2,192,1536]{2,1,0:T(8,128)(2,1)S(1)} %pad_maximum_fusion.24), channel_id=1, source_target_pairs={{0,2},{2,0},{1,3},{3,1},{4,6},{6,4},{5,7},{7,5},{8,10},{10,8},{9,1... | collective-permute-start | bytes 3538952 | tf_op jit(solution)/shard_map/ppermute | solution.py:26
  388.8 13.3 %collective-permute-start.37 = (bf16[192,1536]{1,0:T(8,128)(2,1)S(1)}, bf16[192,1536]{1,0:T(8,128)(2,1)S(1)}, u32[]{:S(2)}, u32[]{:S(2)}) collective-permute-start(bf16[192,1536]{1,0:T(8,128)(2,1)S(1)} %get-tuple-element.84), channel_id=1, source_target_pairs={{0,2},{2,0},{1,3},{3,1},{4,6},{6,4},{5,7},{7,5},{8,10},{10,8},{9,1... | collective-permute-start | bytes 1769480 | tf_op jit(solution)/shard_map/ppermute | solution.py:26
  390.0 12.2 %collective-permute-start.39 = (bf16[192,1536]{1,0:T(8,128)(2,1)S(1)}, bf16[192,1536]{1,0:T(8,128)(2,1)S(1)}, u32[]{:S(2)}, u32[]{:S(2)}) collective-permute-start(bf16[192,1536]{1,0:T(8,128)(2,1)S(1)} %get-tuple-element.85), channel_id=1, source_target_pairs={{0,4},{4,0},{1,5},{5,1},{2,6},{6,2},{3,7},{7,3},{8,12},{12,8},{9,1... | collective-permute-start | bytes 1769480 | tf_op jit(solution)/shard_map/ppermute | solution.py:28
  399.1 35.5 %collective-permute-start.59 = (bf16[1536,896]{1,0:T(8,128)(2,1)}, bf16[1536,896]{1,0:T(8,128)(2,1)}, u32[]{:S(2)}, u32[]{:S(2)}) collective-permute-start(bf16[1536,896]{1,0:T(8,128)(2,1)} %convolution_convert_fusion.3), channel_id=1, source_target_pairs={{0,1},{1,0},{2,3},{3,2},{4,5},{5,4},{6,7},{7,6},{8,9},{9,8},{10,11... | collective-permute-start | bytes 8257544 | tf_op jit(solution)/shard_map/ppermute | solution.py:61
  406.3 24.2 %collective-permute-start.40 = (bf16[384,1536]{1,0:T(8,128)(2,1)}, bf16[384,1536]{1,0:T(8,128)(2,1)}, u32[]{:S(2)}, u32[]{:S(2)}) collective-permute-start(bf16[384,1536]{1,0:T(8,128)(2,1)} %get-tuple-element.55), channel_id=1, source_target_pairs={{0,2},{2,0},{1,3},{3,1},{4,6},{6,4},{5,7},{7,5},{8,10},{10,8},{9,1... | collective-permute-start | bytes 3538952 | tf_op jit(solution)/shard_map/ppermute | solution.py:26
  406.7 37.3 %collective-permute-start.41 = (bf16[384,1536]{1,0:T(8,128)(2,1)}, bf16[384,1536]{1,0:T(8,128)(2,1)}, u32[]{:S(2)}, u32[]{:S(2)}) collective-permute-start(bf16[384,1536]{1,0:T(8,128)(2,1)} %get-tuple-element.55), channel_id=1, source_target_pairs={{0,4},{4,0},{1,5},{5,1},{2,6},{6,2},{3,7},{7,3},{8,12},{12,8},{9,1... | collective-permute-start | bytes 3538952 | tf_op jit(solution)/shard_map/ppermute | solution.py:28
  432.5 18.0 %collective-permute-start.42 = (bf16[192,1536]{1,0:T(8,128)(2,1)}, bf16[192,1536]{1,0:T(8,128)(2,1)}, u32[]{:S(2)}, u32[]{:S(2)}) collective-permute-start(bf16[192,1536]{1,0:T(8,128)(2,1)} %slice.1103), channel_id=1, source_target_pairs={{0,4},{4,0},{1,5},{5,1},{2,6},{6,2},{3,7},{7,3},{8,12},{12,8},{9,1... | collective-permute-start | bytes 1769480 | tf_op jit(solution)/shard_map/ppermute | solution.py:28
  443.9 267.5 %reduce-scatter.4.cloned.1.call-start = ((), (), s32[]{:S(2)}) async-start(), calls=%async_computation.5 | async-start | bytes 3932160 | tf_op jit(solution)/shard_map/reduce_scatter | solution.py:269
  445.1 11.0 %collective-permute-start.43 = (bf16[192,1536]{1,0:T(8,128)(2,1)S(1)}, bf16[192,1536]{1,0:T(8,128)(2,1)S(1)}, u32[]{:S(2)}, u32[]{:S(2)}) collective-permute-start(bf16[192,1536]{1,0:T(8,128)(2,1)S(1)} %slice.1104), channel_id=1, source_target_pairs={{0,2},{2,0},{1,3},{3,1},{4,6},{6,4},{5,7},{7,5},{8,10},{10,8},{9,1... | collective-permute-start | bytes 1769480 | tf_op jit(solution)/shard_map/ppermute | solution.py:26
  474.4 17.1 %collective-permute-start.44 = (f32[4,2,384]{2,1,0:T(2,128)}, f32[4,2,384]{2,1,0:T(2,128)S(1)}, u32[]{:S(2)}, u32[]{:S(2)}) collective-permute-start(f32[4,2,384]{2,1,0:T(2,128)} %get-tuple-element.53), channel_id=1, source_target_pairs={{0,1},{1,0},{2,3},{3,2},{4,5},{5,4},{6,7},{7,6},{8,9},{9,8},{10,11... | collective-permute-start | bytes 36872 | tf_op jit(solution)/shard_map/ppermute | solution.py:61
  479.8 11.8 %collective-permute-start.45 = (f32[2,384]{1,0:T(2,128)}, f32[2,384]{1,0:T(2,128)}, u32[]{:S(2)}, u32[]{:S(2)}) collective-permute-start(f32[2,384]{1,0:T(2,128)} %fusion.58), channel_id=1, source_target_pairs={{8,1},{16,9},{24,17},{10,3},{18,11},{26,19},{12,5},{20,13},{28,21}... | collective-permute-start | bytes 9224 | tf_op jit(solution)/shard_map/ppermute | solution.py:84
  531.9 43.5 %collective-permute-start.51 = (bf16[4,400,768]{2,1,0:T(8,128)(2,1)}, bf16[4,400,768]{2,1,0:T(8,128)(2,1)}, u32[]{:S(2)}, u32[]{:S(2)}) collective-permute-start(bf16[4,400,768]{2,1,0:T(8,128)(2,1)} %fusion.14), channel_id=1, source_target_pairs={{0,1},{1,0},{2,3},{3,2},{4,5},{5,4},{6,7},{7,6},{8,9},{9,8},{10,11... | collective-permute-start | bytes 7372808 | tf_op jit(solution)/shard_map/ppermute | solution.py:61
  548.4 62.5 %collective-permute-start.55 = (bf16[1536,1792]{1,0:T(8,128)(2,1)}, bf16[1536,1792]{1,0:T(8,128)(2,1)}, u32[]{:S(2)}, u32[]{:S(2)}) collective-permute-start(bf16[1536,1792]{1,0:T(8,128)(2,1)} %convolution_convert_fusion), channel_id=1, source_target_pairs={{0,1},{1,0},{2,3},{3,2},{4,5},{5,4},{6,7},{7,6},{8,9},{9,8},{10,11... | collective-permute-start | bytes 16515080 | tf_op jit(solution)/shard_map/ppermute | solution.py:61
  584.9 160.2 %reduce-scatter.6.cloned.1.call-start = ((), (), s32[]{:S(2)}) async-start(), calls=%async_computation.6 | async-start | bytes 6881280 | tf_op jit(solution)/shard_map/reduce_scatter | solution.py:215
  595.1 28.8 %collective-permute-start.27 = (bf16[2,192,1536]{2,1,0:T(8,128)(2,1)}, bf16[2,192,1536]{2,1,0:T(8,128)(2,1)}, u32[]{:S(2)}, u32[]{:S(2)}) collective-permute-start(bf16[2,192,1536]{2,1,0:T(8,128)(2,1)} %stack.360), channel_id=1, source_target_pairs={{0,4},{4,0},{1,5},{5,1},{2,6},{6,2},{3,7},{7,3},{8,12},{12,8},{9,1... | collective-permute-start | bytes 3538952 | tf_op jit(solution)/shard_map/ppermute | solution.py:28
  598.1 27.5 %collective-permute-start.29 = (bf16[2,192,1536]{2,1,0:T(8,128)(2,1)}, bf16[2,192,1536]{2,1,0:T(8,128)(2,1)}, u32[]{:S(2)}, u32[]{:S(2)}) collective-permute-start(bf16[2,192,1536]{2,1,0:T(8,128)(2,1)} %pad_maximum_fusion.23), channel_id=1, source_target_pairs={{0,2},{2,0},{1,3},{3,1},{4,6},{6,4},{5,7},{7,5},{8,10},{10,8},{9,1... | collective-permute-start | bytes 3538952 | tf_op jit(solution)/shard_map/ppermute | solution.py:26
  607.1 40.8 %collective-permute-start.46 = (bf16[2,192,1536]{2,1,0:T(8,128)(2,1)}, bf16[2,192,1536]{2,1,0:T(8,128)(2,1)}, u32[]{:S(2)}, u32[]{:S(2)}) collective-permute-start(bf16[2,192,1536]{2,1,0:T(8,128)(2,1)} %stack.362), channel_id=1, source_target_pairs={{0,4},{4,0},{1,5},{5,1},{2,6},{6,2},{3,7},{7,3},{8,12},{12,8},{9,1... | collective-permute-start | bytes 3538952 | tf_op jit(solution)/shard_map/ppermute | solution.py:28
  610.1 40.8 %collective-permute-start.48 = (bf16[2,192,1536]{2,1,0:T(8,128)(2,1)}, bf16[2,192,1536]{2,1,0:T(8,128)(2,1)}, u32[]{:S(2)}, u32[]{:S(2)}) collective-permute-start(bf16[2,192,1536]{2,1,0:T(8,128)(2,1)} %pad_maximum_fusion.26), channel_id=1, source_target_pairs={{0,2},{2,0},{1,3},{3,1},{4,6},{6,4},{5,7},{7,5},{8,10},{10,8},{9,1... | collective-permute-start | bytes 3538952 | tf_op jit(solution)/shard_map/ppermute | solution.py:26
  627.5 36.0 %collective-permute-start.28 = (bf16[192,1536]{1,0:T(8,128)(2,1)S(1)}, bf16[192,1536]{1,0:T(8,128)(2,1)S(1)}, u32[]{:S(2)}, u32[]{:S(2)}) collective-permute-start(bf16[192,1536]{1,0:T(8,128)(2,1)S(1)} %get-tuple-element.90), channel_id=1, source_target_pairs={{0,2},{2,0},{1,3},{3,1},{4,6},{6,4},{5,7},{7,5},{8,10},{10,8},{9,1... | collective-permute-start | bytes 1769480 | tf_op jit(solution)/shard_map/ppermute | solution.py:26
  628.5 35.0 %collective-permute-start.30 = (bf16[192,1536]{1,0:T(8,128)(2,1)S(1)}, bf16[192,1536]{1,0:T(8,128)(2,1)S(1)}, u32[]{:S(2)}, u32[]{:S(2)}) collective-permute-start(bf16[192,1536]{1,0:T(8,128)(2,1)S(1)} %get-tuple-element.91), channel_id=1, source_target_pairs={{0,4},{4,0},{1,5},{5,1},{2,6},{6,2},{3,7},{7,3},{8,12},{12,8},{9,1... | collective-permute-start | bytes 1769480 | tf_op jit(solution)/shard_map/ppermute | solution.py:28
  652.8 23.4 %collective-permute-start.47 = (bf16[192,1536]{1,0:T(8,128)(2,1)S(1)}, bf16[192,1536]{1,0:T(8,128)(2,1)S(1)}, u32[]{:S(2)}, u32[]{:S(2)}) collective-permute-start(bf16[192,1536]{1,0:T(8,128)(2,1)S(1)} %get-tuple-element.78), channel_id=1, source_target_pairs={{0,2},{2,0},{1,3},{3,1},{4,6},{6,4},{5,7},{7,5},{8,10},{10,8},{9,1... | collective-permute-start | bytes 1769480 | tf_op jit(solution)/shard_map/ppermute | solution.py:26
  653.7 22.4 %collective-permute-start.49 = (bf16[192,1536]{1,0:T(8,128)(2,1)S(1)}, bf16[192,1536]{1,0:T(8,128)(2,1)S(1)}, u32[]{:S(2)}, u32[]{:S(2)}) collective-permute-start(bf16[192,1536]{1,0:T(8,128)(2,1)S(1)} %get-tuple-element.79), channel_id=1, source_target_pairs={{0,4},{4,0},{1,5},{5,1},{2,6},{6,2},{3,7},{7,3},{8,12},{12,8},{9,1... | collective-permute-start | bytes 1769480 | tf_op jit(solution)/shard_map/ppermute | solution.py:28
  683.3 10.0 %collective-permute-start.50 = (f32[384,1536]{1,0:T(8,128)}, f32[384,1536]{1,0:T(8,128)}, u32[]{:S(2)}, u32[]{:S(2)}) collective-permute-start(f32[384,1536]{1,0:T(8,128)} %get-tuple-element.102), channel_id=1, source_target_pairs={{0,1},{1,0},{2,3},{3,2},{4,5},{5,4},{6,7},{7,6},{8,9},{9,8},{10,11... | collective-permute-start | bytes 7077896 | tf_op jit(solution)/shard_map/ppermute | solution.py:61
  700.5 9.7 %collective-permute-start.62 = (bf16[96,896]{1,0:T(8,128)(2,1)S(1)}, bf16[96,896]{1,0:T(8,128)(2,1)S(1)}, u32[]{:S(2)}, u32[]{:S(2)}) collective-permute-start(bf16[96,896]{1,0:T(8,128)(2,1)S(1)} %get-tuple-element.163), channel_id=1, source_target_pairs={{0,4},{4,0},{1,5},{5,1},{2,6},{6,2},{3,7},{7,3},{8,12},{12,8},{9,1... | collective-permute-start | bytes 516104 | tf_op jit(solution)/shard_map/ppermute | solution.py:28
  701.7 8.6 %collective-permute-start.61 = (bf16[96,896]{1,0:T(8,128)(2,1)S(1)}, bf16[96,896]{1,0:T(8,128)(2,1)S(1)}, u32[]{:S(2)}, u32[]{:S(2)}) collective-permute-start(bf16[96,896]{1,0:T(8,128)(2,1)S(1)} %get-tuple-element.164), channel_id=1, source_target_pairs={{0,6},{2,4},{4,2},{6,0},{1,7},{3,5},{5,3},{7,1},{8,14},{10,12},{12... | collective-permute-start | bytes 516104 | tf_op jit(solution)/shard_map/ppermute | solution.py:29
  701.7 9.5 %collective-permute-start.60 = (bf16[96,896]{1,0:T(8,128)(2,1)S(1)}, bf16[96,896]{1,0:T(8,128)(2,1)S(1)}, u32[]{:S(2)}, u32[]{:S(2)}) collective-permute-start(bf16[96,896]{1,0:T(8,128)(2,1)S(1)} %get-tuple-element.162), channel_id=1, source_target_pairs={{0,2},{2,0},{1,3},{3,1},{4,6},{6,4},{5,7},{7,5},{8,10},{10,8},{9,1... | collective-permute-start | bytes 516104 | tf_op jit(solution)/shard_map/ppermute | solution.py:26
  714.3 8.2 %collective-permute-start.54 = (bf16[96,768]{0,1:T(8,128)(2,1)S(1)}, bf16[96,768]{0,1:T(8,128)(2,1)S(1)}, u32[]{:S(2)}, u32[]{:S(2)}) collective-permute-start(bf16[96,768]{0,1:T(8,128)(2,1)S(1)} %get-tuple-element.139), channel_id=1, source_target_pairs={{0,4},{4,0},{1,5},{5,1},{2,6},{6,2},{3,7},{7,3},{8,12},{12,8},{9,1... | collective-permute-start | bytes 442376 | tf_op jit(solution)/shard_map/ppermute | solution.py:28
  715.5 9.4 %collective-permute-start.52 = (bf16[96,768]{0,1:T(8,128)(2,1)S(1)}, bf16[96,768]{0,1:T(8,128)(2,1)S(1)}, u32[]{:S(2)}, u32[]{:S(2)}) collective-permute-start(bf16[96,768]{0,1:T(8,128)(2,1)S(1)} %get-tuple-element.138), channel_id=1, source_target_pairs={{0,2},{2,0},{1,3},{3,1},{4,6},{6,4},{5,7},{7,5},{8,10},{10,8},{9,1... | collective-permute-start | bytes 442376 | tf_op jit(solution)/shard_map/ppermute | solution.py:26
  719.8 71.2 %collective-permute-start.64 = (f32[3,1,48]{2,0,1:T(4,128)S(1)}, f32[3,1,48]{2,0,1:T(4,128)S(1)}, u32[]{:S(2)}, u32[]{:S(2)}) collective-permute-start(f32[3,1,48]{2,0,1:T(4,128)S(1)} %reshape.364), channel_id=1, source_target_pairs={{0,0},{8,2},{16,4},{24,6},{2,8},{10,10},{18,12},{26,14},{4,16},{12... | collective-permute-start | bytes 1736 | tf_op jit(solution)/shard_map/ppermute | solution.py:283
  748.5 16.8 %collective-permute-start.58 = (bf16[96,1792]{1,0:T(8,128)(2,1)}, bf16[96,1792]{1,0:T(8,128)(2,1)}, u32[]{:S(2)}, u32[]{:S(2)}) collective-permute-start(bf16[96,1792]{1,0:T(8,128)(2,1)} %get-tuple-element.113), channel_id=1, source_target_pairs={{0,4},{4,0},{1,5},{5,1},{2,6},{6,2},{3,7},{7,3},{8,12},{12,8},{9,1... | collective-permute-start | bytes 1032200 | tf_op jit(solution)/shard_map/ppermute | solution.py:28
  749.8 15.5 %collective-permute-start.57 = (bf16[96,1792]{1,0:T(8,128)(2,1)}, bf16[96,1792]{1,0:T(8,128)(2,1)}, u32[]{:S(2)}, u32[]{:S(2)}) collective-permute-start(bf16[96,1792]{1,0:T(8,128)(2,1)} %get-tuple-element.114), channel_id=1, source_target_pairs={{0,6},{2,4},{4,2},{6,0},{1,7},{3,5},{5,3},{7,1},{8,14},{10,12},{12... | collective-permute-start | bytes 1032200 | tf_op jit(solution)/shard_map/ppermute | solution.py:29
  751.0 15.3 %collective-permute-start.56 = (bf16[96,1792]{1,0:T(8,128)(2,1)}, bf16[96,1792]{1,0:T(8,128)(2,1)}, u32[]{:S(2)}, u32[]{:S(2)}) collective-permute-start(bf16[96,1792]{1,0:T(8,128)(2,1)} %get-tuple-element.112), channel_id=1, source_target_pairs={{0,2},{2,0},{1,3},{3,1},{4,6},{6,4},{5,7},{7,5},{8,10},{10,8},{9,1... | collective-permute-start | bytes 1032200 | tf_op jit(solution)/shard_map/ppermute | solution.py:26
  (95 other events, 726.2 us)
Sparse Core Ops, SparseCore 0:
  25.4 51.9 all-gather.8
  79.5 55.7 all-gather.6
  136.9 100.7 all-gather.4
  444.0 57.3 reduce-scatter.7
  585.1 59.3 reduce-scatter.3
  646.6 98.5 reduce-scatter.5

commit v2 on v1

v2 whole, which is shorter than its diff:
```python
import functools

import jax
import jax.numpy as jnp
import numpy as np
from jax import lax
from jax.experimental import pallas as pl
from jax.experimental.pallas import tpu as pltpu
from jax.sharding import Mesh, PartitionSpec as P

epsilon = 1e-05
f32 = jnp.float32
bf16 = jnp.bfloat16
PLANE = ("y", "x")
SWAP = ((0, 1), (1, 0))
LANES = 128
VMEM_LIMIT = 50 * 1024 * 1024


def nn(left, right):
    return lax.dot_general(left, right, (((1,), (0,)), ((), ())), preferred_element_type=f32)


def nt(left, right):
    return lax.dot_general(left, right, (((1,), (1,)), ((), ())), preferred_element_type=f32)


def tn(left, right):
    return lax.dot_general(left, right, (((0,), (0,)), ((), ())), preferred_element_type=f32)


def after(value, *others):
    return lax.optimization_barrier((value,) + others)[0]


def by_xor(stack, bits):
    places = np.arange(stack.shape[0])
    for level, bit in enumerate(bits):
        turned = jnp.stack([stack[int(p)] for p in places ^ (1 << level)])
        stack = jnp.where(bit, turned, stack)
    return stack


def plane_bits():
    return [lax.axis_index("x") == 1, lax.axis_index("y") == 1]


def plane_swap(value, offset):
    if offset == 1:
        return lax.ppermute(value, "x", SWAP)
    if offset == 2:
        return lax.ppermute(value, "y", SWAP)
    return lax.ppermute(value, PLANE, [(i, i ^ 3) for i in range(4)])


def core_swap(value):
    return lax.ppermute(value, "mp", SWAP)


def exchange_first(relative):
    return [relative[0]] + [plane_swap(relative[r], r) for r in (1, 2, 3)]


def exchange_second(got):
    return by_xor(jnp.stack(got), plane_bits())


def plane_exchange(stack):
    return exchange_second(exchange_first(by_xor(stack, plane_bits())))


def gather_first(own):
    return plane_swap(own, 1), plane_swap(own, 2)


def gather_second(own, from_x, from_y):
    half = own.shape[0] // 32 * 16
    return [own, from_x, from_y, plane_swap(from_x[:half], 2), plane_swap(from_y[half:], 1)]


def plane_gather(own):
    return gather_second(own, *gather_first(own))


def reduce_first(parts):
    to_x, to_y = parts[0], parts[1]
    return plane_swap(to_x, 1), plane_swap(to_y, 2)


def reduce_second(parts, low_in, top_in):
    _, _, _, mine_x, mine_y = parts
    top_on = (mine_x.astype(f32) + top_in[1].astype(f32)).astype(bf16)
    low_on = (mine_y.astype(f32) + low_in[1].astype(f32)).astype(bf16)
    return plane_swap(top_on, 1), plane_swap(low_on, 2)


def reduce_end(parts, low_in, top_in, top_last, low_last):
    own = parts[2].astype(f32)
    half = top_last.shape[0]
    top = own[:half] + top_in[0].astype(f32) + top_last.astype(f32)
    low = own[half:] + low_in[0].astype(f32) + low_last.astype(f32)
    return jnp.concatenate([top, low], axis=0)


def plane_reduce(parts, *held):
    low_in, top_in = reduce_first(parts)
    top_last, low_last = reduce_second(parts, low_in, top_in)
    if held:
        top_last, low_last = lax.optimization_barrier((top_last, low_last) + held)[:2]
    return reduce_end(parts, low_in, top_in, top_last, low_last)


def halo_forward(tails):
    planes = lax.axis_size("z")
    got = core_swap(tails)
    jump = [(2 * z + 1, 2 * z + 2) for z in range(planes - 1)]
    ordered = by_xor(jnp.moveaxis(tails, 1, 0), plane_bits())
    before = lax.ppermute(ordered[3], ("z", "mp"), jump)
    ordered = by_xor(jnp.moveaxis(got, 1, 0), plane_bits())
    shifted = by_xor(jnp.concatenate([before[None], ordered[:3]], axis=0), plane_bits())
    return jnp.where(lax.axis_index("mp") == 1, got, jnp.moveaxis(shifted, 0, 1))


def halo_backward(heads):
    planes = lax.axis_size("z")
    got = core_swap(heads)
    jump = [(2 * z + 2, 2 * z + 1) for z in range(planes - 1)]
    ordered = by_xor(jnp.moveaxis(heads, 1, 0), plane_bits())
    behind = lax.ppermute(ordered[0], ("z", "mp"), jump)
    ordered = by_xor(jnp.moveaxis(got, 1, 0), plane_bits())
    shifted = by_xor(jnp.concatenate([ordered[1:], behind[None]], axis=0), plane_bits())
    return jnp.where(lax.axis_index("mp") == 1, jnp.moveaxis(shifted, 0, 1), got)


def both_cores(own):
    other = core_swap(own)
    first = lax.axis_index("mp") == 0
    return jnp.concatenate([jnp.where(first, own, other), jnp.where(first, other, own)], axis=0)


def taps_turn(back):
    planes = lax.axis_size("z")
    pairs = [(s, (s % planes) * 4 + s // planes) for s in range(4 * planes)]
    return [(b, a) for a, b in pairs] if back else pairs


def call(body, out_shapes, *args, grid=None, in_specs=None, out_specs=None, prefetch=0, flops=0, aliases=None):
    whole = pl.BlockSpec(memory_space=pltpu.VMEM)
    if in_specs is None:
        in_specs = [whole] * (len(args) - prefetch)
    if out_specs is None:
        out_specs = [whole] * len(out_shapes)
    moved = sum(a.size * a.dtype.itemsize for a in args)
    moved += sum(o.size * o.dtype.itemsize for o in out_shapes)
    return pl.pallas_call(
        body,
        out_shape=out_shapes,
        grid_spec=pltpu.PrefetchScalarGridSpec(
            num_scalar_prefetch=prefetch,
            grid=grid or (),
            in_specs=in_specs,
            out_specs=out_specs,
        ),
        input_output_aliases=aliases or {},
        compiler_params=pltpu.CompilerParams(vmem_limit_bytes=VMEM_LIMIT),
        cost_estimate=pl.CostEstimate(flops=flops // 1000, bytes_accessed=moved // 1000, transcendentals=0),
    )(*args)


def out(shape, dtype):
    return jax.ShapeDtypeStruct(shape, dtype)


def spans(seg):
    half = seg // 2
    return ((0, 0, 0, seg), (1, 1, 0, seg), (2, 2, 0, seg), (3, 3, 0, half), (4, 3, half, seg - half))


def split_shapes(seg, width):
    half = seg // 2
    return [
        out((2, half, width), bf16),
        out((2, half, width), bf16),
        out((seg, width), bf16),
        out((half, width), bf16),
        out((half, width), bf16),
    ]


def split_store(refs, place, value):
    to_x, to_y, own, mine_x, mine_y = refs
    value = value.astype(bf16)
    half = value.shape[0] // 2
    top, low = value[:half], value[half:]
    if place == 0:
        own[...] = value
    elif place == 1:
        mine_x[...] = top
        to_x[0] = low
    elif place == 2:
        to_y[0] = top
        mine_y[...] = low
    else:
        to_y[1] = top
        to_x[1] = low


def conv_project(hats, pack, seg):
    planes, _, rows_taps, cols = pack.shape
    rows, chan = rows_taps - 16, cols // 4
    width = planes * rows

    def body(*refs):
        hat_refs, pack_ref, b_ref, c_ref, x_ref, u_ref = refs[:5], *refs[5:]
        for half in range(2):
            weights = pack_ref[:, half, :rows, :].reshape(width, cols)
            for place, segment, low, count in spans(seg):
                proj = nn(hat_refs[place][:count, :], weights)
                b_val, c_val, x_val = (
                    proj[:, :chan],
                    proj[:, chan : 2 * chan],
                    proj[:, 3 * chan :],
                )
                at = (half, segment, pl.ds(low, count))
                b_ref[at] = b_val
                c_ref[at] = c_val
                x_ref[at] = x_val
                u_ref[at] = (b_val * x_val).astype(bf16)

    shape = (2, 4, seg, chan)
    return call(
        body,
        [out(shape, f32)] * 3 + [out(shape, bf16)],
        *hats,
        pack,
        flops=2 * 4 * seg * width * cols * 2,
    )


def rows_of(shape):
    return lax.broadcasted_iota(jnp.int32, shape, 0)


def earlier_rows(value, halo):
    row = rows_of(value.shape)
    one = jnp.where(row == 0, halo[1:2], pltpu.roll(value, 1, 0))
    two = jnp.where(row == 0, halo[0:1], jnp.where(row == 1, halo[1:2], pltpu.roll(value, 2, 0)))
    return one, two


def conv_mix(u_vals, halo, c_part, keeps, taps, pack, seg):
    planes, _, rows_taps, cols = pack.shape
    rows, chan = rows_taps - 16, cols // 4
    width = planes * rows

    def body(u_ref, halo_ref, c_ref, keep_ref, taps_ref, pack_ref, v_ref, y_ref, *split):
        outs = [
            pack_ref[:, half, :rows, 2 * chan : 3 * chan].reshape(width, chan) for half in range(2)
        ]
        for segment in range(4):
            keep_one, keep_two = keep_ref[0, segment], keep_ref[1, segment]
            total = None
            for half in range(2):
                u_val = u_ref[half, segment].astype(f32)
                one, two = earlier_rows(u_val, halo_ref[half, segment])
                tap = taps_ref[half]
                v_val = tap[0:1] * u_val + tap[1:2] * keep_one * one + tap[2:3] * keep_two * two
                y_val = (c_ref[half, segment] * v_val).astype(bf16)
                v_ref[half, segment] = v_val
                y_ref[half, segment] = y_val
                term = nt(y_val, outs[half])
                total = term if total is None else total + term
            split_store(split, segment, total)

    shape = (2, 4, seg, chan)
    results = call(
        body,
        [out(shape, f32), out(shape, bf16)] + split_shapes(seg, width),
        u_vals,
        halo,
        c_part,
        keeps,
        taps,
        pack,
        flops=2 * 4 * seg * width * 2 * chan,
    )
    return results[0], results[1], results[2:]


def conv_back(grad_mixer, u_vals, halo, c_part, v_vals, keeps, taps, pack, seg):
    planes, _, rows_taps, cols = pack.shape
    rows, chan = rows_taps - 16, cols // 4
    width = planes * rows

    def body(*refs):
        mix_refs = refs[:5]
        u_ref, halo_ref, c_ref, v_ref, keep_ref, taps_ref, pack_ref = refs[5:12]
        dc_ref, dv_ref, sums_ref, heads_ref = refs[12:]
        for half in range(2):
            outs = pack_ref[:, half, :rows, 2 * chan : 3 * chan].reshape(width, chan)
            for place, segment, low, count in spans(seg):
                at = (half, segment, pl.ds(low, count))
                grad_y = nn(mix_refs[place][:count, :], outs)
                dc_ref[at] = (grad_y * v_ref[at]).astype(bf16)
                dv_ref[at] = grad_y * c_ref[at]
            sums = [jnp.zeros((1, chan), f32)] * 3
            tap = taps_ref[half]
            for segment in range(4):
                keep_one, keep_two = keep_ref[0, segment], keep_ref[1, segment]
                u_val = u_ref[half, segment].astype(f32)
                one, two = earlier_rows(u_val, halo_ref[half, segment])
                grad_v = dv_ref[half, segment]
                once, twice = keep_one * grad_v, keep_two * grad_v
                for k, term in enumerate((grad_v * u_val, once * one, twice * two)):
                    sums[k] = sums[k] + jnp.sum(term, axis=0, keepdims=True)
                heads_ref[half, segment, 0:1] = tap[2:3] * twice[0:1]
                heads_ref[half, segment, 1:2] = tap[1:2] * once[0:1] + tap[2:3] * twice[1:2]
            for k in range(3):
                sums_ref[half, k : k + 1] = sums[k]

    shape = (2, 4, seg, chan)
    return call(
        body,
        [out(shape, bf16), out(shape, f32), out((2, 3, chan), f32), out((2, 4, 2, chan), f32)],
        *grad_mixer,
        u_vals,
        halo,
        c_part,
        v_vals,
        keeps,
        taps,
        pack,
        flops=2 * 4 * seg * width * 2 * chan,
    )


def conv_grads(grad_c, grad_v, back, b_part, x_part, keeps, taps, seg):
    chan = grad_v.shape[-1]

    def body(dc_ref, dv_ref, back_ref, b_ref, x_ref, keep_ref, taps_ref, dp_ref):
        row = rows_of((seg, chan))
        for segment in range(4):
            keep_one, keep_two = keep_ref[0, segment], keep_ref[1, segment]
            for half in range(2):
                tap = taps_ref[half]
                grad_val = dv_ref[half, segment]
                once = jnp.where(row == seg - 1, 0.0, pltpu.roll(keep_one * grad_val, seg - 1, 0))
                twice = jnp.where(row >= seg - 2, 0.0, pltpu.roll(keep_two * grad_val, seg - 2, 0))
                grad_u = tap[0:1] * grad_val + tap[1:2] * once + tap[2:3] * twice
                ends = back_ref[half, segment]
                grad_u = grad_u + jnp.where(
                    row == seg - 2, ends[0:1], jnp.where(row == seg - 1, ends[1:2], 0.0)
                )
                grad_u = grad_u.astype(bf16).astype(f32)
                dp_ref[half, segment * seg : (segment + 1) * seg, :] = jnp.concatenate(
                    [
                        grad_u * x_ref[half, segment],
                        dc_ref[half, segment].astype(f32),
                        jnp.zeros((seg, chan), f32),
                        grad_u * b_ref[half, segment],
                    ],
                    axis=1,
                ).astype(bf16)

    return call(
        body,
        [out((2, 4 * seg, 4 * chan), bf16)],
        grad_c,
        grad_v,
        back,
        b_part,
        x_part,
        keeps,
        taps,
    )[0]


def ffn_pack(gate, up, down, gain, place, cuts, chan_hid):
    rows = gate.shape[0]
    hid = chan_hid

    def body(place_ref, gate_ref, up_ref, down_ref, gain_ref, *outs):
        scale = gain_ref[...]
        for q in range(4):
            for (low, high), out_ref in zip(cuts, outs):
                tiles = high - low
                for t in range(tiles):
                    start = (low + t) * LANES
                    count = min(hid - start, LANES)
                    values = [
                        ref[:, q * hid + start : q * hid + start + count]
                        for ref in (gate_ref, up_ref, down_ref)
                    ]
                    values[0] = (values[0].astype(f32) * scale).astype(bf16)
                    values[1] = (values[1].astype(f32) * scale).astype(bf16)
                    if count < LANES:
                        fill = jnp.zeros((rows, LANES - count), bf16)
                        values = [jnp.concatenate([v, fill], axis=1) for v in values]
                    for value, column in zip(values, (2 * t, 2 * t + 1, 2 * tiles + t)):
                        out_ref[q ^ place_ref[0], :, column * LANES : (column + 1) * LANES] = value

    whole = pl.BlockSpec(memory_space=pltpu.VMEM)
    return call(
        body,
        [out((4, rows, 3 * LANES * (high - low)), bf16) for low, high in cuts],
        place,
        gate,
        up,
        down,
        gain,
        in_specs=[whole] * 4,
        out_specs=[whole] * 2,
        prefetch=1,
    )


def ffn_pass(hats, cots, pack, size, seg, segments, earlier=None):
    planes, _, rows, _ = pack.shape
    width = planes * rows
    tiles = size // LANES
    blocks = [span for span in spans(seg) if span[1] in segments]
    hats, cots = ([values[span[0]] for span in blocks] for values in (hats, cots))
    count_in = len(blocks)
    first = blocks[0][1]
    held_rows = len(segments) * seg

    def body(*refs):
        hat_refs, cot_refs = refs[:count_in], refs[count_in : 2 * count_in]
        gu_ref, down_ref = refs[2 * count_in : 2 * count_in + 2]
        a_ref, dg_ref = refs[-2:]
        downs = jnp.concatenate(
            [down_ref[:, half].reshape(width, LANES) for half in range(2)], axis=1
        )
        gus = [gu_ref[:, half].reshape(width, 2 * LANES) for half in range(2)]
        for hat_ref, cot_ref, (_, segment, low, count) in zip(hat_refs, cot_refs, blocks):
            at = pl.ds((segment - first) * seg + low, count)
            grad_act = nn(cot_ref[:count, :], downs)
            for half in range(2):
                vals = nn(hat_ref[:count, :], gus[half])
                gate, up = vals[:, :LANES], vals[:, LANES:]
                grad = grad_act[:, half * LANES : (half + 1) * LANES]
                sig = 1.0 / (1.0 + jnp.exp(-gate))
                silu = gate * sig
                a_ref[half, at, :] = (silu * up).astype(bf16)
                dg_ref[half, at, :LANES] = (grad * up * (sig + silu * (1.0 - sig))).astype(bf16)
                dg_ref[half, at, LANES:] = (grad * silu).astype(bf16)

    def held(value):
        return pl.BlockSpec(value.shape, lambda t: (0, 0))

    tokens = 4 * seg
    place = first * seg // held_rows
    args = [*hats, *cots, pack, pack]
    specs = [held(v) for v in (*hats, *cots)] + [
        pl.BlockSpec((planes, 2, rows, 2 * LANES), lambda t: (0, 0, 0, t)),
        pl.BlockSpec((planes, 2, rows, LANES), lambda t: (0, 0, 0, 2 * tiles + t)),
    ]
    aliases = None
    if earlier is not None:
        aliases = {len(args): 0, len(args) + 1: 1}
        args += list(earlier)
        specs += [pl.BlockSpec(memory_space=pl.ANY)] * 2
    return call(
        body,
        [out((2, tokens, size), bf16), out((2, tokens, 2 * size), bf16)],
        *args,
        grid=(tiles,),
        in_specs=specs,
        out_specs=[
            pl.BlockSpec((2, held_rows, LANES), lambda t: (0, place, t)),
            pl.BlockSpec((2, held_rows, 2 * LANES), lambda t: (0, place, t)),
        ],
        flops=2 * held_rows * width * 6 * size,
        aliases=aliases,
    )


def turned_back(lefts, packs, place, rows, seg):
    planes = packs[0].shape[0]
    width = planes * rows
    group = max(1, 2 * planes // 4)
    wide = group * rows

    def body(*refs):
        count = len(lefts)
        left_refs, pack_refs, split = refs[:count], refs[count : 2 * count], refs[2 * count :]
        weights = [
            [ref[:, half].reshape(wide, ref.shape[-1]) for half in range(2)] for ref in pack_refs
        ]
        for segment in range(4):
            total = None
            for left_ref, pair in zip(left_refs, weights):
                for half in range(2):
                    term = nt(left_ref[half, segment * seg : (segment + 1) * seg, :], pair[half])
                    total = term if total is None else total + term
            split_store(split, segment, total)

    cols = [left.shape[-1] for left in lefts]
    half_seg = seg // 2
    return call(
        body,
        split_shapes(seg, width),
        *lefts,
        *packs,
        grid=(planes // group,),
        in_specs=[pl.BlockSpec(left.shape, lambda i: (0, 0, 0)) for left in lefts]
        + [
            pl.BlockSpec((group, 2, rows, c), functools.partial(lambda p, i: (i, 0, 0, p), place))
            for c in cols
        ],
        out_specs=[
            pl.BlockSpec((2, half_seg, wide), lambda i: (0, 0, i)),
            pl.BlockSpec((2, half_seg, wide), lambda i: (0, 0, i)),
            pl.BlockSpec((seg, wide), lambda i: (0, i)),
            pl.BlockSpec((half_seg, wide), lambda i: (0, i)),
            pl.BlockSpec((half_seg, wide), lambda i: (0, i)),
        ],
        flops=2 * 4 * seg * width * 2 * sum(cols),
    )


def weight_grad(which, lefts, right, others, other_right, at, cols, extra, seg):
    width = lefts[0].shape[1]
    wide = 384
    first, second = right.shape[-1], other_right.shape[-1]

    def body(which_ref, *refs):
        left_refs, other_refs, right_ref, other_ref = refs[:5], refs[5:10], refs[10], refs[11]
        out_ref = refs[-1]

        def gathered(places):
            return jnp.concatenate(
                [places[place][:count, :] for place, _, _, count in spans(seg)], axis=0
            )

        def put(low, high, value):
            if extra is not None:
                value = value + refs[12][:, low:high].astype(f32)
            out_ref[:, low:high] = value.astype(bf16)

        put(0, first, tn(gathered(left_refs), right_ref[0]))
        put(at, at + second, tn(gathered(other_refs), other_ref[0]))

    def column(value):
        return pl.BlockSpec((value.shape[0], wide), lambda i, w: (0, i))

    def chosen(value):
        return pl.BlockSpec((1,) + value.shape[1:], lambda i, w: (w[0], 0, 0))

    tile = pl.BlockSpec((wide, cols), lambda i, w: (i, 0))
    args = [*lefts, *others, right, other_right]
    specs = [column(v) for v in (*lefts, *others)] + [chosen(right), chosen(other_right)]
    if extra is not None:
        args.append(extra)
        specs.append(tile)
    return call(
        body,
        [out((width, cols), bf16)],
        which,
        *args,
        grid=(width // wide,),
        in_specs=specs,
        out_specs=[tile],
        prefetch=1,
        flops=2 * 4 * seg * width * cols,
    )[0]


def per_device(
    tokens, starts, w_in, w_out, gate_up, w_down, gain_mix, gain_ffn, conv_taps, cotangent
):
    core = lax.axis_index("mp")
    planes = lax.axis_size("z")
    rows, _, half_c = w_in.shape
    half_f = w_down.shape[0]
    width = tokens.shape[1]
    seg = tokens.shape[0] // 2
    chan, hid = half_c // 4, half_f // 4
    plane_rows = 4 * rows
    tap_len = conv_taps.shape[2]
    tiles = -(-hid // LANES)
    cuts = ((0, tiles // 2 + 1), (tiles // 2 + 1, tiles))
    sizes = [LANES * (high - low) for low, high in cuts]
    own_half = core.astype(jnp.int32).reshape(1)
    other_half = 1 - own_half

    def mine(value):
        return lax.dynamic_slice_in_dim(value, core * seg, seg, axis=0)

    gain_one = gain_mix.astype(f32)[:, None, None]
    gain_two = gain_ffn.astype(f32)[:, None, None]
    in_scaled = (w_in.astype(f32) * gain_one).astype(bf16)
    out_turned = w_out.T

    def conv_columns(q):
        at = slice(q * chan, (q + 1) * chan)
        return [in_scaled[:, 0, at], in_scaled[:, 1, at], out_turned[:, at], in_scaled[:, 2, at]]

    conv_quart = jnp.stack([jnp.concatenate(conv_columns(q), axis=1) for q in range(4)])
    conv_quart = by_xor(conv_quart, plane_bits())
    tap_piece = lax.ppermute(conv_taps.reshape(1, -1), ("z",) + PLANE, taps_turn(False))
    tap_rows = jnp.pad(tap_piece, ((0, 15), (0, 4 * chan - 3 * tap_len)))
    conv_got = exchange_first(conv_quart)

    def over_all(value):
        value = lax.all_gather(value, ("z", "mp"), axis=0, tiled=False)
        return value.reshape((planes, 2) + value.shape[1:])

    inputs = mine(tokens).astype(f32)
    inv_mix = lax.rsqrt(jnp.mean(inputs * inputs, axis=-1, keepdims=True) + epsilon)
    hat_mix = inputs * inv_mix
    begin_row = mine(starts).astype(bf16)[None]
    begin_rows = jnp.pad(begin_row, ((0, 15), (0, width - seg)))
    hat_own = jnp.concatenate([hat_mix.astype(bf16), begin_rows], axis=0)
    hat_own = after(hat_own, conv_quart)
    hat_x, hat_y = gather_first(hat_own)
    conv_pack = exchange_second(after(conv_got, hat_own)).reshape(plane_rows, 4 * chan)
    conv_pack = jnp.concatenate([conv_pack, tap_rows], axis=0)
    conv_all = over_all(conv_pack)
    cot = mine(cotangent)

    place = (2 * lax.axis_index("y") + lax.axis_index("x")).astype(jnp.int32).reshape(1)
    packs = ffn_pack(
        gate_up[:, 0], gate_up[:, 1], w_down.T, gain_two[:, 0], place, cuts, hid
    )
    first_quart, second_quart = packs
    hats = gather_second(hat_own, hat_x, hat_y)
    first_got = exchange_first(first_quart)
    first_pack = exchange_second(after(first_got, hat_x, hat_y)).reshape(plane_rows, -1)
    cot, second_quart = lax.optimization_barrier((cot, second_quart, first_pack, *hats[3:]))[:2]
    second_got = exchange_first(second_quart)
    cot_x, cot_y = gather_first(cot)

    begins = jnp.stack(
        [hats[0][seg, :seg], hats[1][seg, :seg], hats[2][seg, :seg], hats[4][-16, :seg]]
    ).astype(f32)
    earlier = jnp.concatenate([jnp.zeros((4, 1), f32), begins[:, :-1]], axis=1)
    keeps = jnp.stack([1.0 - begins, (1.0 - begins) * (1.0 - earlier)])[..., None]
    last_keep = 1.0 - begins[:, -1:]
    taps = conv_all[:, :, plane_rows, : 3 * tap_len].reshape(planes, 2, 3, tap_len)
    taps = jnp.transpose(taps, (1, 2, 0, 3)).reshape(2, 3, chan).astype(f32)

    b_part, c_part, x_part, mixed_in = conv_project(hats, conv_all, seg)
    tails = mixed_in[:, :, seg - 2 :]
    tail_gate = jnp.stack([last_keep, jnp.ones((4, 1), f32)], axis=1)
    halo = halo_forward((tails * tail_gate).astype(bf16)).astype(f32)
    convolved, gated, mixer = conv_mix(mixed_in, halo, c_part, keeps, taps, conv_all, seg)
    first_in = reduce_first(mixer)
    second_got, cot_x, cot_y = lax.optimization_barrier((second_got, cot_x, cot_y, *mixer))[:3]
    cots = gather_second(cot, cot_x, cot_y)
    second_pack = exchange_second(second_got).reshape(plane_rows, -1)
    ffn_all = [over_all(first_pack), over_all(second_pack)]
    first_in = lax.optimization_barrier((*first_in, second_pack))[:2]
    middle = inputs + reduce_end(mixer, *first_in, *reduce_second(mixer, *first_in))

    inv_ffn = lax.rsqrt(jnp.mean(middle * middle, axis=-1, keepdims=True) + epsilon)
    hat_ffn = middle * inv_ffn
    hats_two = plane_gather(hat_ffn.astype(bf16))

    def other_grad(lefts, right, others, other_right, at, cols):
        theirs = weight_grad(other_half, lefts, right, others, other_right, at, cols, None, seg)
        return core_swap(theirs), theirs

    def own_grad(lefts, right, others, other_right, at, cols, theirs):
        return weight_grad(own_half, lefts, right, others, other_right, at, cols, theirs, seg)

    def over_z(value, *held):
        value = after(value, *held)
        return lax.psum_scatter(value, "z", scatter_dimension=0, tiled=True)

    def cut_grads(acts, grads, size):
        given = (hats_two, grads, cots, acts, 2 * size, 3 * size)
        return own_grad(*given, other_grad(*given))

    done_one = ffn_pass(hats_two, cots, ffn_all[0], sizes[0], seg, (0, 1, 2))
    acts_one, grads_one = ffn_pass(hats_two, cots, ffn_all[0], sizes[0], seg, (3,), done_one)
    given = (hats_two, grads_one, cots, acts_one, 2 * sizes[0], 3 * sizes[0])
    theirs = other_grad(*given)
    second_all = after(ffn_all[1], theirs[1])
    acts_two, grads_two = ffn_pass(hats_two, cots, second_all, sizes[1], seg, (0, 1, 2, 3))
    sum_one = own_grad(*given, after(theirs[0], acts_two))
    red_one = over_z(sum_one)
    grad_hat2 = turned_back(
        [grads_one, after(grads_two, sum_one)], [ffn_all[0], second_all], 0, plane_rows, seg
    )
    acts_two, grads_two = lax.optimization_barrier((acts_two, grads_two, *grad_hat2))[:2]
    given = (hats_two, grads_two, cots, acts_two, 2 * sizes[1], 3 * sizes[1])
    sum_two = own_grad(*given, other_grad(*given)[0])
    red_two = over_z(sum_two)
    first_in = reduce_first(grad_hat2)
    first_in = lax.optimization_barrier((*first_in, sum_two))[:2]
    last_in = reduce_second(grad_hat2, *first_in)
    last_in = lax.optimization_barrier((*last_in, red_one))[:2]
    grad_hat2 = reduce_end(grad_hat2, *first_in, *last_in)
    inner = jnp.mean(grad_hat2 * hat_ffn, axis=-1, keepdims=True)
    grad_middle = cot.astype(f32) + inv_ffn * (grad_hat2 - hat_ffn * inner)

    mixer_own = grad_middle.astype(bf16)
    mixer_x, mixer_y = gather_first(mixer_own)
    ffn_out = turned_back(
        [acts_one, after(acts_two, mixer_own)], [ffn_all[0], second_all], 2, plane_rows, seg
    )
    mixer_x, mixer_y = lax.optimization_barrier((mixer_x, mixer_y, *ffn_out))[:2]
    grad_mixer = gather_second(mixer_own, mixer_x, mixer_y)
    ffn_out = lax.optimization_barrier((*ffn_out, *grad_mixer))[:5]
    grad_c, grad_v, tap_sums, heads = conv_back(
        grad_mixer, mixed_in, halo, c_part, convolved, keeps, taps, conv_all, seg
    )
    back = halo_backward(heads) * tail_gate
    grad_proj = conv_grads(grad_c, grad_v, back, b_part, x_part, keeps, taps, seg)
    gated = gated.reshape(2, 4 * seg, chan)
    given = (hats, grad_proj, grad_mixer, gated, 2 * chan, 4 * chan)
    theirs, sent = other_grad(given[0], after(grad_proj, red_two), *given[2:])
    grad_hat1 = turned_back([after(grad_proj, sent)], [conv_all], 0, plane_rows, seg)
    sum_conv = own_grad(*given, after(theirs, *grad_hat1))
    red_conv = over_z(sum_conv)
    first_in = reduce_first(grad_hat1)
    first_in = lax.optimization_barrier((*first_in, sum_conv))[:2]
    grad_hat1 = reduce_end(grad_hat1, *first_in, *reduce_second(grad_hat1, *first_in))
    inner = jnp.mean(grad_hat1 * hat_mix, axis=-1, keepdims=True)
    grad_inputs = grad_middle + inv_mix * (grad_hat1 - hat_mix * inner)
    output_vals = (middle + plane_reduce(ffn_out)).astype(bf16)

    tap_sums = jnp.where(core == 0, tap_sums, tap_sums[::-1])
    tap_sum = tap_sums[0] + core_swap(tap_sums[1])
    tap_sum = lax.psum(tap_sum, "z").reshape(3, planes, tap_len)
    tap_sum = lax.dynamic_index_in_dim(tap_sum, lax.axis_index("z"), axis=1, keepdims=True)
    tap_grad = lax.ppermute(tap_sum, ("z",) + PLANE, taps_turn(True))

    def owned(value):
        return plane_exchange(value.reshape(4, rows, -1))

    cut_parts = [owned(after(value, sum_conv)) for value in (red_one, red_two)]
    raw_gu = jnp.concatenate(
        [
            part[:, :, : 2 * size].reshape(4, rows, -1, 2, LANES)
            for part, size in zip(cut_parts, sizes)
        ],
        axis=2,
    )
    raw_gu = jnp.transpose(raw_gu, (1, 3, 0, 2, 4)).reshape(rows, 2, 4, tiles * LANES)
    raw_gu = raw_gu[..., :hid].reshape(rows, 2, half_f).astype(f32)
    raw_down = jnp.concatenate(
        [part[:, :, 2 * size :] for part, size in zip(cut_parts, sizes)], axis=2
    )[:, :, :hid]
    out_down = jnp.transpose(raw_down, (0, 2, 1)).reshape(half_f, rows).astype(f32)
    output_vals, grad_inputs = both_cores(output_vals), both_cores(grad_inputs)
    red_conv = after(red_conv, output_vals, grad_inputs, raw_gu, out_down, tap_grad)
    conv_grad = owned(red_conv).astype(f32)

    def conv_cols(k):
        return jnp.concatenate(
            [conv_grad[q, :, k * chan : (k + 1) * chan] for q in range(4)], axis=1
        )

    raw_in = jnp.stack([conv_cols(k) for k in (0, 1, 3)], axis=1)
    gains = jnp.stack(
        [
            jnp.sum(raw_in * w_in.astype(f32), axis=(1, 2)),
            jnp.sum(raw_gu * gate_up.astype(f32), axis=(1, 2)),
        ]
    )
    gains = gains + core_swap(gains)
    return (
        output_vals,
        grad_inputs,
        raw_in * gain_one,
        conv_cols(2).T,
        raw_gu * gain_two,
        out_down,
        gains[0],
        gains[1],
        tap_grad,
    )


def solution(mesh):
    seq, cores = mesh.shape["seq"], mesh.shape["mp"]
    split = Mesh(np.asarray(mesh.devices).reshape(seq // 4, 2, 2, cores), ("z", "y", "x", "mp"))
    by = ("z", "y", "x")
    weights = (
        P(by, None, "mp"),
        P("mp", by),
        P(by, None, "mp"),
        P("mp", by),
        P(by),
        P(by),
        P(None, "mp", by),
    )
    return jax.shard_map(
        per_device,
        mesh=split,
        in_specs=(P(by, None), P(by)) + weights + (P(by, None),),
        out_specs=(P(by, None), P(by, None)) + weights,
        check_vma=False,
    )
```

time: 810 us -> 639 us (0.79)
  Pallas kernels: 0 us -> 207 us
  matrix products: 174 us -> 0 us
  local copies, waits for them, and re-layouts: 169 us -> 75.8 us
  waiting for transfers between devices: 269 us -> 179 us
  other arithmetic: 97.4 us -> 62.4 us
  starting transfers between devices: 75.4 us -> 85.5 us
    pallas_call x0 -> x17, Pallas kernels: none -> 207 us  [call(): pl.pallas_call(body, out_shape=out_shapes, grid_spec=pltpu.PrefetchScalar...]
    dot_general x18 -> x0, matrix products: 174 us -> none  [dot(): lax.dot_general(left, right, ((dims[0], dims[1]), ((), ())), preferred_el...]
    ppermute x22, waiting for transfers between devices: 146 us -> 58.6 us  [plane_swap(): return lax.ppermute(value, 'y', SWAP)]
    ppermute x6, waiting for transfers between devices: 0.02 us -> 36.5 us  [plane_swap(): return lax.ppermute(value, PLANE, [(i, i ^ 3) for i in range(4)])]
    slice x73 -> x42, local copies, waits for them, and re-layouts: 46.8 us -> 13 us  [the longest x4 4.87 us: gather_second(): from_y[half:]]
    concatenate x10 -> x0, local copies, waits for them, and re-layouts: 26.6 us -> none  [the longest x6 22.7 us: conv_half(): jnp.concatenate([grad_in[:, :, which].reshape(width, 3 * chan), grad_out[...]
    ppermute x22, waiting for transfers between devices: 96.9 us -> 71.8 us  [plane_swap(): return lax.ppermute(value, 'x', SWAP)]
    concatenate x6 -> x1, other arithmetic: 17.3 us -> 1.11 us  [per_device(): hat_own = jnp.concatenate([hat_mix.astype(bf16), begin_rows], axis=0)]
  transfers between devices with their start and end apart: 71 -> 69, of which waited for: 31 -> 29; matrix products, arithmetic and copies ran while one was open for 48% -> 16% of each run, Pallas kernels for 0% -> 31%
where the time goes in v2:
time: 639 us; the launch traced here: 632 us
  Pallas kernels  207 us (32%)
  waiting for transfers between devices  179 us (28%)
  starting transfers between devices  85.5 us (13%)
  local copies, waits for them, and re-layouts  75.8 us (12%)
  other arithmetic  62.4 us (10%)
  between operations  15.6 us (2%)
  blocking collectives  6.49 us (1%)
    pallas_call x17, Pallas kernels, call(): pl.pallas_call(body, out_shape=out_shapes, grid_spec=pltpu.PrefetchScalar...  207 us
    ppermute x22, waiting for transfers between devices, plane_swap(): return lax.ppermute(value, 'x', SWAP)  71.8 us
    ppermute x22, waiting for transfers between devices, plane_swap(): return lax.ppermute(value, 'y', SWAP)  58.6 us
    ppermute x6, waiting for transfers between devices, plane_swap(): return lax.ppermute(value, PLANE, [(i, i ^ 3) for i in range(4)])  36.5 us
    unnamed x169, local copies, waits for them, and re-layouts  32.7 us
    ppermute x9, starting transfers between devices, core_swap(): return lax.ppermute(value, 'mp', SWAP)  29.7 us
    ppermute x22, starting transfers between devices, plane_swap(): return lax.ppermute(value, 'y', SWAP)  21 us
    ppermute x22, starting transfers between devices, plane_swap(): return lax.ppermute(value, 'x', SWAP)  16.1 us
  transfers between devices with their start and end apart: 69, of which 29 were waited for; matrix products, arithmetic and copies ran while one was open for 16% of the time, Pallas kernels for 31%

profile of v2, /device:TPU:25, one launch (start us, length us, event | category | flops | bytes accessed | tf_op | source)
XLA Modules:
  0.0 631.8 jit_solution(17157406403072230072)
XLA Ops:
  8.2 3.7 collective-permute-start.7
  25.3 2.2 collective-permute-start.1
  37.3 24.3 %collective-permute-done.27 = bf16[96,1536]{1,0:T(8,128)(2,1)S(1)} collective-permute-done((bf16[96,1536]{1,0:T(8,128)(2,1)S(1)}, bf16[96,1536]{1,0:T(8,128)(2,1)S(1)}, u32[]{:S(2)}, u32[]{:S(2)}) %collective-permute-start.27) | collective-permute-done | bytes 294944 | tf_op jit(solution)/shard_map/ppermute | solution.py:53
  61.5 5.3 collective-permute-done.26
  76.9 9.7 %collective-permute-done.2.refs_3_ = bf16[192,1536]{1,0:T(8,128)(2,1)S(1)} collective-permute-done((bf16[192,1536]{1,0:T(8,128)(2,1)S(1)}, bf16[192,1536]{1,0:T(8,128)(2,1)S(1)}, u32[]{:S(2)}, u32[]{:S(2)}) %collective-permute-start.2) | collective-permute-done | bytes 589856 | tf_op jit(solution)/shard_map/ppermute | solution.py:52
  94.8 14.8 %shard_map.169 = (f32[2,4,384,192]{3,2,1,0:T(8,128)}, f32[2,4,384,192]{3,2,1,0:T(8,128)}, f32[2,4,384,192]{3,2,1,0:T(8,128)}, bf16[2,4,384,192]{3,2,1,0:T(8,128)(2,1)}) custom-call(bf16[400,1536]{1,0:T(8,128)(2,1)S(1)} %copy-done.5, bf16[400,1536]{1,0:T(8,128)(2,1)} %collective-permute-done.refs_1_, bf16[400,1536]{1,0:T(8,128)(2,1)} %collective-permute-done.1.refs_2_, ...), custom_call_target="tpu_custom_call" | custom-call | flops 7247757 | bytes 18087 | tf_op jit(solution)/shard_map/pallas_call | solution.py:155
  110.5 4.2 collective-permute-start.8
  120.4 8.7 %shard_map.170 = (f32[2,4,384,192]{3,2,1,0:T(8,128)}, bf16[2,4,384,192]{3,2,1,0:T(8,128)(2,1)}, bf16[2,192,1536]{2,1,0:T(8,128)(2,1)S(1)}, bf16[2,192,1536]{2,1,...) custom-call(bf16[2,4,384,192]{3,2,1,0:T(8,128)(2,1)} %get-tuple-element, ...), custom_call_target="tpu_custom_call" | custom-call | flops 1811939 | bytes 16740 | tf_op jit(solution)/shard_map/pallas_call | solution.py:155
  130.8 2.5 maximum_select_fusion.7
  134.8 21.5 %collective-permute-done.10 = bf16[2,192,1536]{2,1,0:T(8,128)(2,1)S(1)} collective-permute-done((bf16[2,192,1536]{2,1,0:T(8,128)(2,1)S(1)}, bf16[2,192,1536]{2,1,0:T(8,128)(2,1)S(1)}, u32[]{:S(2)}, u32[]{:S(2)}) %collective-permute-start.10) | collective-permute-done | bytes 1179680 | tf_op jit(solution)/shard_map/ppermute | solution.py:50
  159.2 9.5 %collective-permute-done.13 = bf16[192,1536]{1,0:T(8,128)(2,1)S(1)} collective-permute-done((bf16[192,1536]{1,0:T(8,128)(2,1)S(1)}, bf16[192,1536]{1,0:T(8,128)(2,1)S(1)}, u32[]{:S(2)}, u32[]{:S(2)}) %collective-permute-start.13) | collective-permute-done | bytes 589856 | tf_op jit(solution)/shard_map/ppermute | solution.py:52
  172.5 1.9 slice.707
  174.4 1.9 slice.708
  177.7 14.0 %collective-permute-done.16.refs_2_ = bf16[384,1536]{1,0:T(8,128)(2,1)S(1)} collective-permute-done((bf16[384,1536]{1,0:T(8,128)(2,1)S(1)}, bf16[384,1536]{1,0:T(8,128)(2,1)S(1)}, u32[]{:S(2)}, u32[]{:S(2)}) %collective-permute-start.16) | collective-permute-done | bytes 1179680 | tf_op jit(solution)/shard_map/ppermute | solution.py:52
  193.7 2.2 collective-permute-start.15
  196.0 16.7 %shard_map.172 = (bf16[2,1536,512]{2,1,0:T(8,128)(2,1)}, bf16[2,1536,1024]{2,1,0:T(8,128)(2,1)}) custom-call(bf16[384,1536]{1,0:T(8,128)(2,1)S(1)} %multiply_convert_fusion.refs_0_, bf16[384,1536]{1,0:T(8,128)(2,1)S(1)} %collective-permute-done.14.refs_1_, bf16[384,1536]{1,0:T(8,128)(2,1)S(1)} %collective-permute-done.16.refs_2_, ...), custom_call_target="tpu_custom_call" | custom-call | flops 10871635 | bytes 35389 | tf_op jit(solution)/shard_map/pallas_call | solution.py:155
  212.7 5.5 collective-permute-done.17.refs_1_.refs_4_
  218.1 8.8 %shard_map.173 = (bf16[2,1536,512]{2,1,0:T(8,128)(2,1)}, bf16[2,1536,1024]{2,1,0:T(8,128)(2,1)}) custom-call(bf16[192,1536]{1,0:T(8,128)(2,1)} %collective-permute-done.15.refs_0_.refs_3_, bf16[192,1536]{1,0:T(8,128)(2,1)} %collective-permute-done.17.refs_1_.refs_4_, ...), custom_call_target="tpu_custom_call", output_to_operand_aliasing={{0}: (6, {}), {1}: (7, {})} | custom-call | flops 3623878 | bytes 40108 | tf_op jit(solution)/shard_map/pallas_call | solution.py:155
  227.0 12.5 %shard_map.174 = bf16[1536,1536]{1,0:T(8,128)(2,1)} custom-call(s32[1]{0:T(128)S(6)} %sub.32.which_ref, bf16[384,1536]{1,0:T(8,128)(2,1)S(1)} %multiply_convert_fusion.refs_0_, bf16[384,1536]{1,0:T(8,128)(2,1)} %copy-done.3, bf16[384,1536]{1,0:T(8,128)(2,1)} %copy-done.2, bf16[192,1536]{1,0:T(8,128)(2,1)} %collective-permute-done.15.refs_0_.refs_3_, ...), custom_call_target="tpu_custom_call" | custom-call | flops 7247757 | bytes 23592 | tf_op jit(solution)/shard_map/pallas_call | solution.py:155
  239.5 11.8 %collective-permute-start.28 = (bf16[1536,1536]{1,0:T(8,128)(2,1)}, bf16[1536,1536]{1,0:T(8,128)(2,1)}, u32[]{:S(2)}, u32[]{:S(2)}) collective-permute-start(bf16[1536,1536]{1,0:T(8,128)(2,1)} %shard_map.174), channel_id=1, source_target_pairs={{0,1},{1,0},{2,3},{3,2},{4,5},{5,4},{6,7},{7,6},{8,9},{9,8},{10,11... | collective-permute-start | bytes 14155784 | tf_op jit(solution)/shard_map/ppermute | solution.py:57
  251.3 17.5 %shard_map.175 = (bf16[2,1536,384]{2,1,0:T(8,128)(2,1)}, bf16[2,1536,768]{2,1,0:T(8,128)(2,1)}) custom-call(bf16[384,1536]{1,0:T(8,128)(2,1)S(1)} %multiply_convert_fusion.refs_0_, bf16[384,1536]{1,0:T(8,128)(2,1)} %copy-done.3, bf16[384,1536]{1,0:T(8,128)(2,1)} %copy-done.2, bf16[192,1536]{1,0:T(8,128)(2,1)} %collective-permute-done.15.refs_0_.refs_3_, ...), custom_call_target="tpu_custom_call" | custom-call | flops 10871635 | bytes 30670 | tf_op jit(solution)/shard_map/pallas_call | solution.py:155
  268.8 13.1 %shard_map.176 = bf16[1536,1536]{1,0:T(8,128)(2,1)} custom-call(s32[1]{0:T(128)} %bitcast.69.which_ref, bf16[384,1536]{1,0:T(8,128)(2,1)S(1)} %multiply_convert_fusion.refs_0_, bf16[384,1536]{1,0:T(8,128)(2,1)} %copy-done.3, bf16[384,1536]{1,0:T(8,128)(2,1)} %copy-done.2, bf16[192,1536]{1,0:T(8,128)(2,1)} %collective-permute-done.15.refs_0_.refs_3_, ...), custom_call_target="tpu_custom_call" | custom-call | flops 7247757 | bytes 28311 | tf_op jit(solution)/shard_map/pallas_call | solution.py:155
  282.3 24.6 %shard_map.177 = (bf16[2,192,1536]{2,1,0:T(8,128)(2,1)}, bf16[2,192,1536]{2,1,0:T(8,128)(2,1)}, bf16[384,1536]{1,0:T(8,128)(2,1)}, bf16[192,1536]{1,0:T(8,128)(2,1)S(1)}, bf16[192,1536]{1,0:T(8,128)(2,1)S(1)}) custom-call(bf16[2,1536,1024]{2,1,0:T(8,128)(2,1)} %get-tuple-element.122.refs_10_.refs_0_, ...), custom_call_target="tpu_custom_call" | custom-call | flops 16911432 | bytes 32243 | tf_op jit(solution)/shard_map/pallas_call | solution.py:155
  306.9 10.8 %shard_map.178 = bf16[1536,1152]{1,0:T(8,128)(2,1)} custom-call(s32[1]{0:T(128)S(6)} %sub.32.which_ref, bf16[384,1536]{1,0:T(8,128)(2,1)S(1)} %multiply_convert_fusion.refs_0_, bf16[384,1536]{1,0:T(8,128)(2,1)} %copy-done.3, bf16[384,1536]{1,0:T(8,128)(2,1)} %copy-done.2, bf16[192,1536]{1,0:T(8,128)(2,1)} %collective-permute-done.15.refs_0_.refs_3_, ...), custom_call_target="tpu_custom_call" | custom-call | flops 5435817 | bytes 20054 | tf_op jit(solution)/shard_map/pallas_call | solution.py:155
  319.4 4.7 collective-permute-done.31.refs_12_
  324.2 1.8 copy-done.52
  326.0 11.4 %shard_map.179 = bf16[1536,1152]{1,0:T(8,128)(2,1)} custom-call(s32[1]{0:T(128)} %bitcast.69.which_ref, bf16[384,1536]{1,0:T(8,128)(2,1)S(1)} %multiply_convert_fusion.refs_0_, bf16[384,1536]{1,0:T(8,128)(2,1)} %copy-done.3, bf16[384,1536]{1,0:T(8,128)(2,1)} %copy-done.2, bf16[192,1536]{1,0:T(8,128)(2,1)} %collective-permute-done.15.refs_0_.refs_3_, ...), custom_call_target="tpu_custom_call" | custom-call | flops 5435817 | bytes 23592 | tf_op jit(solution)/shard_map/pallas_call | solution.py:155
  337.4 8.2 %collective-permute-done.29 = bf16[2,192,1536]{2,1,0:T(8,128)(2,1)} collective-permute-done((bf16[2,192,1536]{2,1,0:T(8,128)(2,1)}, bf16[2,192,1536]{2,1,0:T(8,128)(2,1)}, u32[]{:S(2)}, u32[]{:S(2)}) %collective-permute-start.29) | collective-permute-done | bytes 1179680 | tf_op jit(solution)/shard_map/ppermute | solution.py:50
  352.6 8.8 %collective-permute-done.33 = bf16[192,1536]{1,0:T(8,128)(2,1)S(1)} collective-permute-done((bf16[192,1536]{1,0:T(8,128)(2,1)S(1)}, bf16[192,1536]{1,0:T(8,128)(2,1)S(1)}, u32[]{:S(2)}, u32[]{:S(2)}) %collective-permute-start.33) | collective-permute-done | bytes 589856 | tf_op jit(solution)/shard_map/ppermute | solution.py:52
  363.0 7.7 %reduce-scatter.4.cloned.1.call-done = bf16[384,1536]{1,0:T(8,128)(2,1)} async-done(((bf16[1536,1536]{1,0:T(8,128)(2,1)}), bf16[384,1536]{1,0:T(8,128)(2,1)}) %reduce-scatter.4.cloned.1.call-update) | async-done | bytes 1179664 | tf_op jit(solution)/shard_map/reduce_scatter | solution.py:669
  370.7 2.5 fusion.17
  374.7 1.9 fusion.43.refs_0_.refs_5_
  379.1 15.5 %shard_map.180 = (bf16[2,192,1536]{2,1,0:T(8,128)(2,1)}, bf16[2,192,1536]{2,1,0:T(8,128)(2,1)}, bf16[384,1536]{1,0:T(8,128)(2,1)}, bf16[192,1536]{1,0:T(8,128)(2,1)S(1)}, bf16[192,1536]{1,0:T(8,128)(2,1)S(1)}) custom-call(bf16[2,1536,512]{2,1,0:T(8,128)(2,1)} %get-tuple-element.117.refs_11_.refs_0_, ...), custom_call_target="tpu_custom_call" | custom-call | flops 8455716 | bytes 26738 | tf_op jit(solution)/shard_map/pallas_call | solution.py:155
  394.6 9.2 %collective-permute-done.35.refs_2_.refs_7_ = bf16[384,1536]{1,0:T(8,128)(2,1)S(1)} collective-permute-done((bf16[384,1536]{1,0:T(8,128)(2,1)S(1)}, bf16[384,1536]{1,0:T(8,128)(2,1)S(1)}, u32[]{:S(2)}, u32[]{:S(2)}) %collective-permute-start.35) | collective-permute-done | bytes 1179680 | tf_op jit(solution)/shard_map/ppermute | solution.py:52
  407.9 11.8 %collective-permute-done.37.refs_4_.refs_9_ = bf16[192,1536]{1,0:T(8,128)(2,1)S(1)} collective-permute-done((bf16[192,1536]{1,0:T(8,128)(2,1)}, bf16[192,1536]{1,0:T(8,128)(2,1)S(1)}, u32[]{:S(2)}, u32[]{:S(2)}) %collective-permute-start.37) | collective-permute-done | bytes 589856 | tf_op jit(solution)/shard_map/ppermute | solution.py:50
  425.6 11.8 %shard_map.181 = (bf16[2,4,384,192]{3,2,1,0:T(8,128)(2,1)}, f32[2,4,384,192]{3,2,1,0:T(8,128)}, f32[2,3,192]{2,1,0:T(4,128)S(1)}, f32[2,4,2,192]{3,2,1,0:T(2,128)S(1)}) custom-call(bf16[384,1536]{1,0:T(8,128)(2,1)S(1)} %fusion.43.refs_0_.refs_5_, bf16[384,1536]{1,0:T(8,128)(2,1)S(1)} %copy-done.7, bf16[384,1536]{1,0:T(8,128)(2,1)} %copy-done.41, ...), custom_call_target="tpu_custom_call" | custom-call | flops 1811939 | bytes 19117 | tf_op jit(solution)/shard_map/pallas_call | solution.py:155
  437.5 2.8 collective-permute-start.57
  444.1 8.6 %shard_map.182.refs_10_.refs_0_ = bf16[2,1536,768]{2,1,0:T(8,128)(2,1)} custom-call(bf16[2,4,384,192]{3,2,1,0:T(8,128)(2,1)S(1)} %copy-done.23, f32[2,4,384,192]{3,2,1,0:T(8,128)} %get-tuple-element.154.dv_ref, f32[2,4,2,192]{3,2,1,0:T(2,128)S(1)} %copy_multiply_fusion.back_ref, f32[2,4,384,192]{3,2,1,0:T(8,128)} %get-tuple-element.156.b_ref, ...), custom_call_target="tpu_custom_call" | custom-call | bytes 13005 | tf_op jit(solution)/shard_map/pallas_call | solution.py:155
  457.0 9.2 %shard_map.183 = bf16[1536,768]{1,0:T(8,128)(2,1)} custom-call(s32[1]{0:T(128)S(6)} %sub.32.which_ref, bf16[400,1536]{1,0:T(8,128)(2,1)} %fusion.10.refs_0_, bf16[400,1536]{1,0:T(8,128)(2,1)} %collective-permute-done.refs_1_, bf16[400,1536]{1,0:T(8,128)(2,1)} %collective-permute-done.1.refs_2_, bf16[192,1536]{1,0:T(8,128)(2,1)S(1)} %copy-done.12, ...), custom_call_target="tpu_custom_call" | custom-call | flops 3623878 | bytes 17891 | tf_op jit(solution)/shard_map/pallas_call | solution.py:155
  466.2 3.5 collective-permute-start.47
  469.7 6.5 %psum.7 = f32[3,4,48]{2,1,0:T(4,128)S(1)} all-reduce(f32[3,4,48]{2,1,0:T(4,128)S(1)} %reshape.284), channel_id=1, replica_groups=mesh['z'=4,'y'=2,'x'=2,'mp'=2] {'z'}, use_global_device_ids=true, to_apply=%region_7.8 | all-reduce | flops 576 | bytes 4608 | tf_op jit(solution)/shard_map/psum | solution.py:726
  480.5 6.4 %collective-permute-start.58 = (f32[3,1,48]{2,1,0:T(1,128)S(1)}, f32[3,1,48]{2,1,0:T(1,128)S(1)}, u32[]{:S(2)}, u32[]{:S(2)}) collective-permute-start(f32[3,1,48]{2,1,0:T(1,128)S(1)} %constant_dynamic-slice_fusion), channel_id=1, source_target_pairs={{0,0},{8,2},{16,4},{24,6},{2,8},{10,10},{18,12},{26,14},{4,16},{12... | collective-permute-start | bytes 1736 | tf_op jit(solution)/shard_map/ppermute | solution.py:728
  486.9 12.0 %shard_map.184 = (bf16[2,192,1536]{2,1,0:T(8,128)(2,1)}, bf16[2,192,1536]{2,1,0:T(8,128)(2,1)}, bf16[384,1536]{1,0:T(8,128)(2,1)}, bf16[192,1536]{1,0:T(8,128)(2,1)S(1)}, bf16[192,1536]{1,0:T(8,128)(2,1)S(1)}) custom-call(bf16[2,1536,768]{2,1,0:T(8,128)(2,1)} %shard_map.182.refs_10_.refs_0_, bf16[4,2,400,768]{3,2,1,0:T(8,128)(2,1)} %bitcast.320), custom_call_target="tpu_custom_call" | custom-call | flops 7247757 | bytes 14352 | tf_op jit(solution)/shard_map/pallas_call | solution.py:155
  502.0 3.3 fusion.15
  505.3 9.6 %shard_map.185 = bf16[1536,768]{1,0:T(8,128)(2,1)} custom-call(s32[1]{0:T(128)} %bitcast.69.which_ref, bf16[400,1536]{1,0:T(8,128)(2,1)} %fusion.10.refs_0_, bf16[400,1536]{1,0:T(8,128)(2,1)} %collective-permute-done.refs_1_, bf16[400,1536]{1,0:T(8,128)(2,1)} %collective-permute-done.1.refs_2_, bf16[192,1536]{1,0:T(8,128)(2,1)S(1)} %copy-done.13, ...), custom_call_target="tpu_custom_call" | custom-call | flops 3623878 | bytes 20250 | tf_op jit(solution)/shard_map/pallas_call | solution.py:155
  514.9 8.8 %collective-permute-done.45 = bf16[2,192,1536]{2,1,0:T(8,128)(2,1)} collective-permute-done((bf16[2,192,1536]{2,1,0:T(8,128)(2,1)}, bf16[2,192,1536]{2,1,0:T(8,128)(2,1)}, u32[]{:S(2)}, u32[]{:S(2)}) %collective-permute-start.45) | collective-permute-done | bytes 1179680 | tf_op jit(solution)/shard_map/ppermute | solution.py:50
  523.8 2.0 fusion.21
  525.8 2.0 fusion.20
  534.3 9.9 %collective-permute-done.54 = bf16[96,1152]{1,0:T(8,128)(2,1)S(1)} collective-permute-done((bf16[96,1152]{1,0:T(8,128)(2,1)S(1)}, bf16[96,1152]{1,0:T(8,128)(2,1)S(1)}, u32[]{:S(2)}, u32[]{:S(2)}) %collective-permute-start.54) | collective-permute-done | bytes 221216 | tf_op jit(solution)/shard_map/ppermute | solution.py:50
  545.9 3.3 collective-permute-done.55
  553.3 2.0 collective-permute-done.51
  555.3 6.5 %collective-permute-done.52 = bf16[96,1536]{1,0:T(8,128)(2,1)S(1)} collective-permute-done((bf16[96,1536]{1,0:T(8,128)(2,1)}, bf16[96,1536]{1,0:T(8,128)(2,1)S(1)}, u32[]{:S(2)}, u32[]{:S(2)}) %collective-permute-start.52) | collective-permute-done | bytes 294944 | tf_op jit(solution)/shard_map/ppermute | solution.py:53
  563.6 2.2 fusion.13
  568.0 4.3 fusion.7
  572.2 5.5 collective-permute-start.42
  583.6 2.5 reshape.283
  586.1 2.0 copy.131
  588.1 3.0 reshape.304
  591.3 3.3 copy.130
  594.6 4.4 reshape.303
  602.0 2.8 broadcast_select_fusion.1
  604.8 2.5 pad_maximum_fusion
  612.2 3.6 copy.133
  616.0 2.5 collective-permute-done.60
  (441 shorter events, 138.5 us)
Async XLA Ops:
  7.2 86.4 %all-gather.9.cloned.1.call-start = ((), (), s32[]{:S(2)}) async-start(), calls=%async_computation.8 | async-start | bytes 5529600 | tf_op jit(solution)/shard_map/all_gather | solution.py:606
  8.2 16.2 %collective-permute-start.7 = (bf16[1,144]{1,0:T(2,128)(2,1)S(1)}, bf16[1,144]{1,0:T(2,128)(2,1)S(1)}, u32[]{:S(2)}, u32[]{:S(2)}) collective-permute-start(bf16[1,144]{1,0:T(2,128)(2,1)S(1)} %reshape.272), channel_id=1, source_target_pairs={{0,0},{2,8},{4,16},{6,24},{8,2},{10,10},{12,18},{14,26},{16,4},{18... | collective-permute-start | bytes 872 | tf_op jit(solution)/shard_map/ppermute | solution.py:601
  15.7 7.1 %collective-permute-start.6 = (bf16[96,768]{1,0:T(8,128)(2,1)S(1)}, bf16[96,768]{1,0:T(8,128)(2,1)S(1)}, u32[]{:S(2)}, u32[]{:S(2)}) collective-permute-start(bf16[96,768]{1,0:T(8,128)(2,1)S(1)} %get-tuple-element.296), channel_id=1, source_target_pairs={{0,6},{2,4},{4,2},{6,0},{1,7},{3,5},{5,3},{7,1},{8,14},{10,12},{12... | collective-permute-start | bytes 442376 | tf_op jit(solution)/shard_map/ppermute | solution.py:53
  15.8 8.2 %collective-permute-start.5 = (bf16[96,768]{1,0:T(8,128)(2,1)S(1)}, bf16[96,768]{1,0:T(8,128)(2,1)S(1)}, u32[]{:S(2)}, u32[]{:S(2)}) collective-permute-start(bf16[96,768]{1,0:T(8,128)(2,1)S(1)} %get-tuple-element.297), channel_id=1, source_target_pairs={{0,4},{4,0},{1,5},{5,1},{2,6},{6,2},{3,7},{7,3},{8,12},{12,8},{9,1... | collective-permute-start | bytes 442376 | tf_op jit(solution)/shard_map/ppermute | solution.py:52
  17.3 6.6 %collective-permute-start.4 = (bf16[96,768]{1,0:T(8,128)(2,1)S(1)}, bf16[96,768]{1,0:T(8,128)(2,1)S(1)}, u32[]{:S(2)}, u32[]{:S(2)}) collective-permute-start(bf16[96,768]{1,0:T(8,128)(2,1)S(1)} %get-tuple-element.298), channel_id=1, source_target_pairs={{0,2},{2,0},{1,3},{3,1},{4,6},{6,4},{5,7},{7,5},{8,10},{10,8},{9,1... | collective-permute-start | bytes 442376 | tf_op jit(solution)/shard_map/ppermute | solution.py:50
  25.2 170.8 %all-gather.5.cloned.1.call-start = ((), (), s32[]{:S(2)}) async-start(), calls=%async_computation.3 | async-start | bytes 10616832 | tf_op jit(solution)/shard_map/all_gather | solution.py:606
  25.3 43.0 %collective-permute-start.1 = (bf16[400,1536]{1,0:T(8,128)(2,1)}, bf16[400,1536]{1,0:T(8,128)(2,1)}, u32[]{:S(2)}, u32[]{:S(2)}) collective-permute-start(bf16[400,1536]{1,0:T(8,128)(2,1)} %fusion.10.refs_0_), channel_id=1, source_target_pairs={{0,4},{4,0},{1,5},{5,1},{2,6},{6,2},{3,7},{7,3},{8,12},{12,8},{9,1... | collective-permute-start | bytes 3686408 | tf_op jit(solution)/shard_map/ppermute | solution.py:52
  27.5 40.8 %collective-permute-start = (bf16[400,1536]{1,0:T(8,128)(2,1)}, bf16[400,1536]{1,0:T(8,128)(2,1)}, u32[]{:S(2)}, u32[]{:S(2)}) collective-permute-start(bf16[400,1536]{1,0:T(8,128)(2,1)} %fusion.10.refs_0_), channel_id=1, source_target_pairs={{0,2},{2,0},{1,3},{3,1},{4,6},{6,4},{5,7},{7,5},{8,10},{10,8},{9,1... | collective-permute-start | bytes 3686408 | tf_op jit(solution)/shard_map/ppermute | solution.py:50
  34.6 26.9 %collective-permute-start.27 = (bf16[96,1536]{1,0:T(8,128)(2,1)S(1)}, bf16[96,1536]{1,0:T(8,128)(2,1)S(1)}, u32[]{:S(2)}, u32[]{:S(2)}) collective-permute-start(bf16[96,1536]{1,0:T(8,128)(2,1)S(1)} %get-tuple-element.256), channel_id=1, source_target_pairs={{0,6},{2,4},{4,2},{6,0},{1,7},{3,5},{5,3},{7,1},{8,14},{10,12},{12... | collective-permute-start | bytes 884744 | tf_op jit(solution)/shard_map/ppermute | solution.py:53
  35.9 30.9 %collective-permute-start.26 = (bf16[96,1536]{1,0:T(8,128)(2,1)S(1)}, bf16[96,1536]{1,0:T(8,128)(2,1)S(1)}, u32[]{:S(2)}, u32[]{:S(2)}) collective-permute-start(bf16[96,1536]{1,0:T(8,128)(2,1)S(1)} %get-tuple-element.257), channel_id=1, source_target_pairs={{0,4},{4,0},{1,5},{5,1},{2,6},{6,2},{3,7},{7,3},{8,12},{12,8},{9,1... | collective-permute-start | bytes 884744 | tf_op jit(solution)/shard_map/ppermute | solution.py:52
  37.2 31.0 %collective-permute-start.25 = (bf16[96,1536]{1,0:T(8,128)(2,1)S(1)}, bf16[96,1536]{1,0:T(8,128)(2,1)S(1)}, u32[]{:S(2)}, u32[]{:S(2)}) collective-permute-start(bf16[96,1536]{1,0:T(8,128)(2,1)S(1)} %get-tuple-element.258), channel_id=1, source_target_pairs={{0,2},{2,0},{1,3},{3,1},{4,6},{6,4},{5,7},{7,5},{8,10},{10,8},{9,1... | collective-permute-start | bytes 884744 | tf_op jit(solution)/shard_map/ppermute | solution.py:50
  69.9 181.4 %all-gather.7.cloned.1.call-start = ((), (), s32[]{:S(2)}) async-start(), calls=%async_computation.4 | async-start | bytes 7962624 | tf_op jit(solution)/shard_map/all_gather | solution.py:606
  72.5 14.4 %collective-permute-start.3 = (bf16[208,1536]{1,0:T(8,128)(2,1)S(1)}, bf16[208,1536]{1,0:T(8,128)(2,1)S(1)}, u32[]{:S(2)}, u32[]{:S(2)}) collective-permute-start(bf16[208,1536]{1,0:T(8,128)(2,1)S(1)} %slice.849), channel_id=1, source_target_pairs={{0,2},{2,0},{1,3},{3,1},{4,6},{6,4},{5,7},{7,5},{8,10},{10,8},{9,1... | collective-permute-start | bytes 1916936 | tf_op jit(solution)/shard_map/ppermute | solution.py:50
  73.6 13.0 %collective-permute-start.2 = (bf16[192,1536]{1,0:T(8,128)(2,1)S(1)}, bf16[192,1536]{1,0:T(8,128)(2,1)S(1)}, u32[]{:S(2)}, u32[]{:S(2)}) collective-permute-start(bf16[192,1536]{1,0:T(8,128)(2,1)S(1)} %slice.848), channel_id=1, source_target_pairs={{0,4},{4,0},{1,5},{5,1},{2,6},{6,2},{3,7},{7,3},{8,12},{12,8},{9,1... | collective-permute-start | bytes 1769480 | tf_op jit(solution)/shard_map/ppermute | solution.py:52
  86.8 42.3 %collective-permute-start.22 = (bf16[384,1536]{1,0:T(8,128)(2,1)}, bf16[384,1536]{1,0:T(8,128)(2,1)}, u32[]{:S(2)}, u32[]{:S(2)}) collective-permute-start(bf16[384,1536]{1,0:T(8,128)(2,1)} %constant_dynamic-slice_fusion.1.refs_3_.refs_5_), channel_id=1, source_target_pairs={{0,4},{4,0},{1,5},{5,1},{2,6},{6,2},{3,7},{7,3},{8,12},{12,8},{9,1... | collective-permute-start | bytes 3538952 | tf_op jit(solution)/shard_map/ppermute | solution.py:52
  87.8 41.3 %collective-permute-start.21 = (bf16[384,1536]{1,0:T(8,128)(2,1)}, bf16[384,1536]{1,0:T(8,128)(2,1)}, u32[]{:S(2)}, u32[]{:S(2)}) collective-permute-start(bf16[384,1536]{1,0:T(8,128)(2,1)} %constant_dynamic-slice_fusion.1.refs_3_.refs_5_), channel_id=1, source_target_pairs={{0,2},{2,0},{1,3},{3,1},{4,6},{6,4},{5,7},{7,5},{8,10},{10,8},{9,1... | collective-permute-start | bytes 3538952 | tf_op jit(solution)/shard_map/ppermute | solution.py:50
  90.0 39.1 %collective-permute-start.20 = (bf16[96,1152]{1,0:T(8,128)(2,1)}, bf16[96,1152]{1,0:T(8,128)(2,1)}, u32[]{:S(2)}, u32[]{:S(2)}) collective-permute-start(bf16[96,1152]{1,0:T(8,128)(2,1)} %get-tuple-element.276), channel_id=1, source_target_pairs={{0,6},{2,4},{4,2},{6,0},{1,7},{3,5},{5,3},{7,1},{8,14},{10,12},{12... | collective-permute-start | bytes 663560 | tf_op jit(solution)/shard_map/ppermute | solution.py:53
  90.8 38.3 %collective-permute-start.19 = (bf16[96,1152]{1,0:T(8,128)(2,1)}, bf16[96,1152]{1,0:T(8,128)(2,1)}, u32[]{:S(2)}, u32[]{:S(2)}) collective-permute-start(bf16[96,1152]{1,0:T(8,128)(2,1)} %get-tuple-element.277), channel_id=1, source_target_pairs={{0,4},{4,0},{1,5},{5,1},{2,6},{6,2},{3,7},{7,3},{8,12},{12,8},{9,1... | collective-permute-start | bytes 663560 | tf_op jit(solution)/shard_map/ppermute | solution.py:52
  110.5 7.5 %collective-permute-start.8 = (bf16[2,4,2,192]{3,2,0,1:T(2,128)(2,1)S(1)}, bf16[2,4,2,192]{3,2,0,1:T(2,128)(2,1)S(1)}, u32[]{:S(2)}, u32[]{:S(2)}) collective-permute-start(bf16[2,4,2,192]{3,2,0,1:T(2,128)(2,1)S(1)} %copy.110), channel_id=1, source_target_pairs={{0,1},{1,0},{2,3},{3,2},{4,5},{5,4},{6,7},{7,6},{8,9},{9,8},{10,11... | collective-permute-start | bytes 18440 | tf_op jit(solution)/shard_map/ppermute | solution.py:57
  118.8 10.3 %collective-permute-start.18 = (bf16[96,1152]{1,0:T(8,128)(2,1)}, bf16[96,1152]{1,0:T(8,128)(2,1)S(1)}, u32[]{:S(2)}, u32[]{:S(2)}) collective-permute-start(bf16[96,1152]{1,0:T(8,128)(2,1)} %get-tuple-element.278), channel_id=1, source_target_pairs={{0,2},{2,0},{1,3},{3,1},{4,6},{6,4},{5,7},{7,5},{8,10},{10,8},{9,1... | collective-permute-start | bytes 663560 | tf_op jit(solution)/shard_map/ppermute | solution.py:50
  133.3 237.4 %reduce-scatter.4.cloned.1.call-start = ((), (), s32[]{:S(2)}) async-start(), calls=%async_computation.5 | async-start | bytes 5898240 | tf_op jit(solution)/shard_map/reduce_scatter | solution.py:669
  133.5 22.8 %collective-permute-start.10 = (bf16[2,192,1536]{2,1,0:T(8,128)(2,1)S(1)}, bf16[2,192,1536]{2,1,0:T(8,128)(2,1)S(1)}, u32[]{:S(2)}, u32[]{:S(2)}) collective-permute-start(bf16[2,192,1536]{2,1,0:T(8,128)(2,1)S(1)} %get-tuple-element.99), channel_id=1, source_target_pairs={{0,2},{2,0},{1,3},{3,1},{4,6},{6,4},{5,7},{7,5},{8,10},{10,8},{9,1... | collective-permute-start | bytes 3538952 | tf_op jit(solution)/shard_map/ppermute | solution.py:50
  134.2 22.6 %collective-permute-start.11 = (bf16[2,192,1536]{2,1,0:T(8,128)(2,1)S(1)}, bf16[2,192,1536]{2,1,0:T(8,128)(2,1)S(1)}, u32[]{:S(2)}, u32[]{:S(2)}) collective-permute-start(bf16[2,192,1536]{2,1,0:T(8,128)(2,1)S(1)} %get-tuple-element.100), channel_id=1, source_target_pairs={{0,4},{4,0},{1,5},{5,1},{2,6},{6,2},{3,7},{7,3},{8,12},{12,8},{9,1... | collective-permute-start | bytes 3538952 | tf_op jit(solution)/shard_map/ppermute | solution.py:52
  157.2 11.5 %collective-permute-start.13 = (bf16[192,1536]{1,0:T(8,128)(2,1)S(1)}, bf16[192,1536]{1,0:T(8,128)(2,1)S(1)}, u32[]{:S(2)}, u32[]{:S(2)}) collective-permute-start(bf16[192,1536]{1,0:T(8,128)(2,1)S(1)} %fusion.26), channel_id=1, source_target_pairs={{0,4},{4,0},{1,5},{5,1},{2,6},{6,2},{3,7},{7,3},{8,12},{12,8},{9,1... | collective-permute-start | bytes 1769480 | tf_op jit(solution)/shard_map/ppermute | solution.py:52
  157.7 11.0 %collective-permute-start.12 = (bf16[192,1536]{1,0:T(8,128)(2,1)S(1)}, bf16[192,1536]{1,0:T(8,128)(2,1)S(1)}, u32[]{:S(2)}, u32[]{:S(2)}) collective-permute-start(bf16[192,1536]{1,0:T(8,128)(2,1)S(1)} %fusion.27), channel_id=1, source_target_pairs={{0,2},{2,0},{1,3},{3,1},{4,6},{6,4},{5,7},{7,5},{8,10},{10,8},{9,1... | collective-permute-start | bytes 1769480 | tf_op jit(solution)/shard_map/ppermute | solution.py:50
  170.9 20.8 %collective-permute-start.16 = (bf16[384,1536]{1,0:T(8,128)(2,1)S(1)}, bf16[384,1536]{1,0:T(8,128)(2,1)S(1)}, u32[]{:S(2)}, u32[]{:S(2)}) collective-permute-start(bf16[384,1536]{1,0:T(8,128)(2,1)S(1)} %multiply_convert_fusion.refs_0_), channel_id=1, source_target_pairs={{0,4},{4,0},{1,5},{5,1},{2,6},{6,2},{3,7},{7,3},{8,12},{12,8},{9,1... | collective-permute-start | bytes 3538952 | tf_op jit(solution)/shard_map/ppermute | solution.py:52
  171.1 21.7 %collective-permute-start.14 = (bf16[384,1536]{1,0:T(8,128)(2,1)S(1)}, bf16[384,1536]{1,0:T(8,128)(2,1)S(1)}, u32[]{:S(2)}, u32[]{:S(2)}) collective-permute-start(bf16[384,1536]{1,0:T(8,128)(2,1)S(1)} %multiply_convert_fusion.refs_0_), channel_id=1, source_target_pairs={{0,2},{2,0},{1,3},{3,1},{4,6},{6,4},{5,7},{7,5},{8,10},{10,8},{9,1... | collective-permute-start | bytes 3538952 | tf_op jit(solution)/shard_map/ppermute | solution.py:50
  176.4 36.3 %collective-permute-start.24 = (bf16[192,1536]{1,0:T(8,128)(2,1)}, bf16[192,1536]{1,0:T(8,128)(2,1)}, u32[]{:S(2)}, u32[]{:S(2)}) collective-permute-start(bf16[192,1536]{1,0:T(8,128)(2,1)} %slice.708), channel_id=1, source_target_pairs={{0,2},{2,0},{1,3},{3,1},{4,6},{6,4},{5,7},{7,5},{8,10},{10,8},{9,1... | collective-permute-start | bytes 1769480 | tf_op jit(solution)/shard_map/ppermute | solution.py:50
  176.4 36.2 %collective-permute-start.23 = (bf16[192,1536]{1,0:T(8,128)(2,1)}, bf16[192,1536]{1,0:T(8,128)(2,1)}, u32[]{:S(2)}, u32[]{:S(2)}) collective-permute-start(bf16[192,1536]{1,0:T(8,128)(2,1)} %slice.707), channel_id=1, source_target_pairs={{0,4},{4,0},{1,5},{5,1},{2,6},{6,2},{3,7},{7,3},{8,12},{12,8},{9,1... | collective-permute-start | bytes 1769480 | tf_op jit(solution)/shard_map/ppermute | solution.py:52
  192.6 25.5 %collective-permute-start.17 = (bf16[192,1536]{1,0:T(8,128)(2,1)}, bf16[192,1536]{1,0:T(8,128)(2,1)}, u32[]{:S(2)}, u32[]{:S(2)}) collective-permute-start(bf16[192,1536]{1,0:T(8,128)(2,1)} %slice.884), channel_id=1, source_target_pairs={{0,2},{2,0},{1,3},{3,1},{4,6},{6,4},{5,7},{7,5},{8,10},{10,8},{9,1... | collective-permute-start | bytes 1769480 | tf_op jit(solution)/shard_map/ppermute | solution.py:50
  193.7 24.4 %collective-permute-start.15 = (bf16[192,1536]{1,0:T(8,128)(2,1)}, bf16[192,1536]{1,0:T(8,128)(2,1)}, u32[]{:S(2)}, u32[]{:S(2)}) collective-permute-start(bf16[192,1536]{1,0:T(8,128)(2,1)} %slice.883), channel_id=1, source_target_pairs={{0,4},{4,0},{1,5},{5,1},{2,6},{6,2},{3,7},{7,3},{8,12},{12,8},{9,1... | collective-permute-start | bytes 1769480 | tf_op jit(solution)/shard_map/ppermute | solution.py:52
  239.5 29.3 %collective-permute-start.28 = (bf16[1536,1536]{1,0:T(8,128)(2,1)}, bf16[1536,1536]{1,0:T(8,128)(2,1)}, u32[]{:S(2)}, u32[]{:S(2)}) collective-permute-start(bf16[1536,1536]{1,0:T(8,128)(2,1)} %shard_map.174), channel_id=1, source_target_pairs={{0,1},{1,0},{2,3},{3,2},{4,5},{5,4},{6,7},{7,6},{8,9},{9,8},{10,11... | collective-permute-start | bytes 14155784 | tf_op jit(solution)/shard_map/ppermute | solution.py:57
  281.9 170.9 %reduce-scatter.6.cloned.1.call-start = ((), (), s32[]{:S(2)}) async-start(), calls=%async_computation.6 | async-start | bytes 4423680 | tf_op jit(solution)/shard_map/reduce_scatter | solution.py:669
  317.7 6.4 %collective-permute-start.31 = (bf16[1536,1152]{1,0:T(8,128)(2,1)}, bf16[1536,1152]{1,0:T(8,128)(2,1)S(1)}, u32[]{:S(2)}, u32[]{:S(2)}) collective-permute-start(bf16[1536,1152]{1,0:T(8,128)(2,1)} %shard_map.178), channel_id=1, source_target_pairs={{0,1},{1,0},{2,3},{3,2},{4,5},{5,4},{6,7},{7,6},{8,9},{9,8},{10,11... | collective-permute-start | bytes 10616840 | tf_op jit(solution)/shard_map/ppermute | solution.py:57
  317.9 27.6 %collective-permute-start.29 = (bf16[2,192,1536]{2,1,0:T(8,128)(2,1)}, bf16[2,192,1536]{2,1,0:T(8,128)(2,1)}, u32[]{:S(2)}, u32[]{:S(2)}) collective-permute-start(bf16[2,192,1536]{2,1,0:T(8,128)(2,1)} %get-tuple-element.128), channel_id=1, source_target_pairs={{0,2},{2,0},{1,3},{3,1},{4,6},{6,4},{5,7},{7,5},{8,10},{10,8},{9,1... | collective-permute-start | bytes 3538952 | tf_op jit(solution)/shard_map/ppermute | solution.py:50
  318.4 27.1 %collective-permute-start.30 = (bf16[2,192,1536]{2,1,0:T(8,128)(2,1)}, bf16[2,192,1536]{2,1,0:T(8,128)(2,1)}, u32[]{:S(2)}, u32[]{:S(2)}) collective-permute-start(bf16[2,192,1536]{2,1,0:T(8,128)(2,1)} %get-tuple-element.129), channel_id=1, source_target_pairs={{0,4},{4,0},{1,5},{5,1},{2,6},{6,2},{3,7},{7,3},{8,12},{12,8},{9,1... | collective-permute-start | bytes 3538952 | tf_op jit(solution)/shard_map/ppermute | solution.py:52
  348.0 13.4 %collective-permute-start.33 = (bf16[192,1536]{1,0:T(8,128)(2,1)S(1)}, bf16[192,1536]{1,0:T(8,128)(2,1)S(1)}, u32[]{:S(2)}, u32[]{:S(2)}) collective-permute-start(bf16[192,1536]{1,0:T(8,128)(2,1)S(1)} %fusion.24), channel_id=1, source_target_pairs={{0,4},{4,0},{1,5},{5,1},{2,6},{6,2},{3,7},{7,3},{8,12},{12,8},{9,1... | collective-permute-start | bytes 1769480 | tf_op jit(solution)/shard_map/ppermute | solution.py:52
  349.5 13.5 %collective-permute-start.32 = (bf16[192,1536]{1,0:T(8,128)(2,1)S(1)}, bf16[192,1536]{1,0:T(8,128)(2,1)S(1)}, u32[]{:S(2)}, u32[]{:S(2)}) collective-permute-start(bf16[192,1536]{1,0:T(8,128)(2,1)S(1)} %fusion.25), channel_id=1, source_target_pairs={{0,2},{2,0},{1,3},{3,1},{4,6},{6,4},{5,7},{7,5},{8,10},{10,8},{9,1... | collective-permute-start | bytes 1769480 | tf_op jit(solution)/shard_map/ppermute | solution.py:50
  350.6 256.6 %reduce-scatter.8.cloned.1.call-start = ((), (), s32[]{:S(2)}) async-start(), calls=%async_computation.7 | async-start | bytes 2949120 | tf_op jit(solution)/shard_map/reduce_scatter | solution.py:669
  376.5 27.3 %collective-permute-start.35 = (bf16[384,1536]{1,0:T(8,128)(2,1)S(1)}, bf16[384,1536]{1,0:T(8,128)(2,1)S(1)}, u32[]{:S(2)}, u32[]{:S(2)}) collective-permute-start(bf16[384,1536]{1,0:T(8,128)(2,1)S(1)} %fusion.43.refs_0_.refs_5_), channel_id=1, source_target_pairs={{0,4},{4,0},{1,5},{5,1},{2,6},{6,2},{3,7},{7,3},{8,12},{12,8},{9,1... | collective-permute-start | bytes 3538952 | tf_op jit(solution)/shard_map/ppermute | solution.py:52
  377.9 26.7 %collective-permute-start.34 = (bf16[384,1536]{1,0:T(8,128)(2,1)S(1)}, bf16[384,1536]{1,0:T(8,128)(2,1)S(1)}, u32[]{:S(2)}, u32[]{:S(2)}) collective-permute-start(bf16[384,1536]{1,0:T(8,128)(2,1)S(1)} %fusion.43.refs_0_.refs_5_), channel_id=1, source_target_pairs={{0,2},{2,0},{1,3},{3,1},{4,6},{6,4},{5,7},{7,5},{8,10},{10,8},{9,1... | collective-permute-start | bytes 3538952 | tf_op jit(solution)/shard_map/ppermute | solution.py:50
  406.3 13.4 %collective-permute-start.37 = (bf16[192,1536]{1,0:T(8,128)(2,1)}, bf16[192,1536]{1,0:T(8,128)(2,1)S(1)}, u32[]{:S(2)}, u32[]{:S(2)}) collective-permute-start(bf16[192,1536]{1,0:T(8,128)(2,1)} %slice.724), channel_id=1, source_target_pairs={{0,2},{2,0},{1,3},{3,1},{4,6},{6,4},{5,7},{7,5},{8,10},{10,8},{9,1... | collective-permute-start | bytes 1769480 | tf_op jit(solution)/shard_map/ppermute | solution.py:50
  407.5 13.2 %collective-permute-start.36 = (bf16[192,1536]{1,0:T(8,128)(2,1)}, bf16[192,1536]{1,0:T(8,128)(2,1)S(1)}, u32[]{:S(2)}, u32[]{:S(2)}) collective-permute-start(bf16[192,1536]{1,0:T(8,128)(2,1)} %slice.723), channel_id=1, source_target_pairs={{0,4},{4,0},{1,5},{5,1},{2,6},{6,2},{3,7},{7,3},{8,12},{12,8},{9,1... | collective-permute-start | bytes 1769480 | tf_op jit(solution)/shard_map/ppermute | solution.py:52
  437.5 32.1 %collective-permute-start.57 = (f32[3,192]{1,0:T(4,128)S(1)}, f32[3,192]{1,0:T(4,128)S(1)}, u32[]{:S(2)}, u32[]{:S(2)}) collective-permute-start(f32[3,192]{1,0:T(4,128)S(1)} %slice_bitcast_fusion.67), channel_id=1, source_target_pairs={{0,1},{1,0},{2,3},{3,2},{4,5},{5,4},{6,7},{7,6},{8,9},{9,8},{10,11... | collective-permute-start | bytes 6920 | tf_op jit(solution)/shard_map/ppermute | solution.py:57
  441.2 35.1 %collective-permute-start.38 = (bf16[2,192,1536]{2,1,0:T(8,128)(2,1)}, bf16[2,192,1536]{2,1,0:T(8,128)(2,1)}, u32[]{:S(2)}, u32[]{:S(2)}) collective-permute-start(bf16[2,192,1536]{2,1,0:T(8,128)(2,1)} %get-tuple-element.148), channel_id=1, source_target_pairs={{0,4},{4,0},{1,5},{5,1},{2,6},{6,2},{3,7},{7,3},{8,12},{12,8},{9,1... | collective-permute-start | bytes 3538952 | tf_op jit(solution)/shard_map/ppermute | solution.py:52
  441.6 36.5 %collective-permute-start.40 = (bf16[2,192,1536]{2,1,0:T(8,128)(2,1)}, bf16[2,192,1536]{2,1,0:T(8,128)(2,1)}, u32[]{:S(2)}, u32[]{:S(2)}) collective-permute-start(bf16[2,192,1536]{2,1,0:T(8,128)(2,1)} %get-tuple-element.150), channel_id=1, source_target_pairs={{0,2},{2,0},{1,3},{3,1},{4,6},{6,4},{5,7},{7,5},{8,10},{10,8},{9,1... | collective-permute-start | bytes 3538952 | tf_op jit(solution)/shard_map/ppermute | solution.py:50
  466.2 39.1 %collective-permute-start.47 = (bf16[1536,768]{1,0:T(8,128)(2,1)}, bf16[1536,768]{1,0:T(8,128)(2,1)}, u32[]{:S(2)}, u32[]{:S(2)}) collective-permute-start(bf16[1536,768]{1,0:T(8,128)(2,1)} %shard_map.183), channel_id=1, source_target_pairs={{0,1},{1,0},{2,3},{3,2},{4,5},{5,4},{6,7},{7,6},{8,9},{9,8},{10,11... | collective-permute-start | bytes 7077896 | tf_op jit(solution)/shard_map/ppermute | solution.py:57
  477.5 24.5 %collective-permute-start.39 = (bf16[192,1536]{1,0:T(8,128)(2,1)S(1)}, bf16[192,1536]{1,0:T(8,128)(2,1)S(1)}, u32[]{:S(2)}, u32[]{:S(2)}) collective-permute-start(bf16[192,1536]{1,0:T(8,128)(2,1)S(1)} %fusion.23), channel_id=1, source_target_pairs={{0,2},{2,0},{1,3},{3,1},{4,6},{6,4},{5,7},{7,5},{8,10},{10,8},{9,1... | collective-permute-start | bytes 1769480 | tf_op jit(solution)/shard_map/ppermute | solution.py:50
  479.3 22.7 %collective-permute-start.41 = (bf16[192,1536]{1,0:T(8,128)(2,1)S(1)}, bf16[192,1536]{1,0:T(8,128)(2,1)S(1)}, u32[]{:S(2)}, u32[]{:S(2)}) collective-permute-start(bf16[192,1536]{1,0:T(8,128)(2,1)S(1)} %fusion.22), channel_id=1, source_target_pairs={{0,4},{4,0},{1,5},{5,1},{2,6},{6,2},{3,7},{7,3},{8,12},{12,8},{9,1... | collective-permute-start | bytes 1769480 | tf_op jit(solution)/shard_map/ppermute | solution.py:52
  480.5 18.5 %collective-permute-start.58 = (f32[3,1,48]{2,1,0:T(1,128)S(1)}, f32[3,1,48]{2,1,0:T(1,128)S(1)}, u32[]{:S(2)}, u32[]{:S(2)}) collective-permute-start(f32[3,1,48]{2,1,0:T(1,128)S(1)} %constant_dynamic-slice_fusion), channel_id=1, source_target_pairs={{0,0},{8,2},{16,4},{24,6},{2,8},{10,10},{18,12},{26,14},{4,16},{12... | collective-permute-start | bytes 1736 | tf_op jit(solution)/shard_map/ppermute | solution.py:728
  499.0 24.7 %collective-permute-start.45 = (bf16[2,192,1536]{2,1,0:T(8,128)(2,1)}, bf16[2,192,1536]{2,1,0:T(8,128)(2,1)}, u32[]{:S(2)}, u32[]{:S(2)}) collective-permute-start(bf16[2,192,1536]{2,1,0:T(8,128)(2,1)} %get-tuple-element.162), channel_id=1, source_target_pairs={{0,2},{2,0},{1,3},{3,1},{4,6},{6,4},{5,7},{7,5},{8,10},{10,8},{9,1... | collective-permute-start | bytes 3538952 | tf_op jit(solution)/shard_map/ppermute | solution.py:50
  499.0 24.8 %collective-permute-start.46 = (bf16[2,192,1536]{2,1,0:T(8,128)(2,1)}, bf16[2,192,1536]{2,1,0:T(8,128)(2,1)}, u32[]{:S(2)}, u32[]{:S(2)}) collective-permute-start(bf16[2,192,1536]{2,1,0:T(8,128)(2,1)} %get-tuple-element.163), channel_id=1, source_target_pairs={{0,4},{4,0},{1,5},{5,1},{2,6},{6,2},{3,7},{7,3},{8,12},{12,8},{9,1... | collective-permute-start | bytes 3538952 | tf_op jit(solution)/shard_map/ppermute | solution.py:52
  527.9 34.6 %collective-permute-start.49 = (bf16[192,1536]{1,0:T(8,128)(2,1)}, bf16[192,1536]{1,0:T(8,128)(2,1)}, u32[]{:S(2)}, u32[]{:S(2)}) collective-permute-start(bf16[192,1536]{1,0:T(8,128)(2,1)} %fusion.20), channel_id=1, source_target_pairs={{0,4},{4,0},{1,5},{5,1},{2,6},{6,2},{3,7},{7,3},{8,12},{12,8},{9,1... | collective-permute-start | bytes 1769480 | tf_op jit(solution)/shard_map/ppermute | solution.py:52
  528.2 34.2 %collective-permute-start.48 = (bf16[192,1536]{1,0:T(8,128)(2,1)}, bf16[192,1536]{1,0:T(8,128)(2,1)}, u32[]{:S(2)}, u32[]{:S(2)}) collective-permute-start(bf16[192,1536]{1,0:T(8,128)(2,1)} %fusion.21), channel_id=1, source_target_pairs={{0,2},{2,0},{1,3},{3,1},{4,6},{6,4},{5,7},{7,5},{8,10},{10,8},{9,1... | collective-permute-start | bytes 1769480 | tf_op jit(solution)/shard_map/ppermute | solution.py:50
  530.0 14.2 %collective-permute-start.54 = (bf16[96,1152]{1,0:T(8,128)(2,1)S(1)}, bf16[96,1152]{1,0:T(8,128)(2,1)S(1)}, u32[]{:S(2)}, u32[]{:S(2)}) collective-permute-start(bf16[96,1152]{1,0:T(8,128)(2,1)S(1)} %get-tuple-element.264), channel_id=1, source_target_pairs={{0,2},{2,0},{1,3},{3,1},{4,6},{6,4},{5,7},{7,5},{8,10},{10,8},{9,1... | collective-permute-start | bytes 663560 | tf_op jit(solution)/shard_map/ppermute | solution.py:50
  530.9 14.1 %collective-permute-start.56 = (bf16[96,1152]{1,0:T(8,128)(2,1)S(1)}, bf16[96,1152]{1,0:T(8,128)(2,1)S(1)}, u32[]{:S(2)}, u32[]{:S(2)}) collective-permute-start(bf16[96,1152]{1,0:T(8,128)(2,1)S(1)} %get-tuple-element.265), channel_id=1, source_target_pairs={{0,4},{4,0},{1,5},{5,1},{2,6},{6,2},{3,7},{7,3},{8,12},{12,8},{9,1... | collective-permute-start | bytes 663560 | tf_op jit(solution)/shard_map/ppermute | solution.py:52
  531.6 17.5 %collective-permute-start.55 = (bf16[96,1152]{1,0:T(8,128)(2,1)S(1)}, bf16[96,1152]{1,0:T(8,128)(2,1)S(1)}, u32[]{:S(2)}, u32[]{:S(2)}) collective-permute-start(bf16[96,1152]{1,0:T(8,128)(2,1)S(1)} %get-tuple-element.266), channel_id=1, source_target_pairs={{0,6},{2,4},{4,2},{6,0},{1,7},{3,5},{5,3},{7,1},{8,14},{10,12},{12... | collective-permute-start | bytes 663560 | tf_op jit(solution)/shard_map/ppermute | solution.py:53
  544.2 11.1 %collective-permute-start.51 = (bf16[96,1536]{1,0:T(8,128)(2,1)}, bf16[96,1536]{1,0:T(8,128)(2,1)S(1)}, u32[]{:S(2)}, u32[]{:S(2)}) collective-permute-start(bf16[96,1536]{1,0:T(8,128)(2,1)} %get-tuple-element.244), channel_id=1, source_target_pairs={{0,2},{2,0},{1,3},{3,1},{4,6},{6,4},{5,7},{7,5},{8,10},{10,8},{9,1... | collective-permute-start | bytes 884744 | tf_op jit(solution)/shard_map/ppermute | solution.py:50
  545.0 10.3 %collective-permute-start.53 = (bf16[96,1536]{1,0:T(8,128)(2,1)}, bf16[96,1536]{1,0:T(8,128)(2,1)S(1)}, u32[]{:S(2)}, u32[]{:S(2)}) collective-permute-start(bf16[96,1536]{1,0:T(8,128)(2,1)} %get-tuple-element.245), channel_id=1, source_target_pairs={{0,4},{4,0},{1,5},{5,1},{2,6},{6,2},{3,7},{7,3},{8,12},{12,8},{9,1... | collective-permute-start | bytes 884744 | tf_op jit(solution)/shard_map/ppermute | solution.py:52
  549.2 12.6 %collective-permute-start.52 = (bf16[96,1536]{1,0:T(8,128)(2,1)}, bf16[96,1536]{1,0:T(8,128)(2,1)S(1)}, u32[]{:S(2)}, u32[]{:S(2)}) collective-permute-start(bf16[96,1536]{1,0:T(8,128)(2,1)} %get-tuple-element.246), channel_id=1, source_target_pairs={{0,6},{2,4},{4,2},{6,0},{1,7},{3,5},{5,3},{7,1},{8,14},{10,12},{12... | collective-permute-start | bytes 884744 | tf_op jit(solution)/shard_map/ppermute | solution.py:53
  572.2 26.7 %collective-permute-start.42 = (bf16[384,1536]{1,0:T(8,128)(2,1)S(1)}, bf16[384,1536]{1,0:T(8,128)(2,1)}, u32[]{:S(2)}, u32[]{:S(2)}) collective-permute-start(bf16[384,1536]{1,0:T(8,128)(2,1)S(1)} %get-tuple-element.207), channel_id=1, source_target_pairs={{0,1},{1,0},{2,3},{3,2},{4,5},{5,4},{6,7},{7,6},{8,9},{9,8},{10,11... | collective-permute-start | bytes 3538952 | tf_op jit(solution)/shard_map/ppermute | solution.py:57
  577.7 24.3 %collective-permute-start.50 = (f32[384,1536]{1,0:T(8,128)}, f32[384,1536]{1,0:T(8,128)}, u32[]{:S(2)}, u32[]{:S(2)}) collective-permute-start(f32[384,1536]{1,0:T(8,128)} %get-tuple-element.206), channel_id=1, source_target_pairs={{0,1},{1,0},{2,3},{3,2},{4,5},{5,4},{6,7},{7,6},{8,9},{9,8},{10,11... | collective-permute-start | bytes 7077896 | tf_op jit(solution)/shard_map/ppermute | solution.py:57
  609.0 6.8 %collective-permute-start.59 = (bf16[96,768]{1,0:T(8,128)(2,1)S(1)}, bf16[96,768]{1,0:T(8,128)(2,1)S(1)}, u32[]{:S(2)}, u32[]{:S(2)}) collective-permute-start(bf16[96,768]{1,0:T(8,128)(2,1)S(1)} %get-tuple-element.284), channel_id=1, source_target_pairs={{0,2},{2,0},{1,3},{3,1},{4,6},{6,4},{5,7},{7,5},{8,10},{10,8},{9,1... | collective-permute-start | bytes 442376 | tf_op jit(solution)/shard_map/ppermute | solution.py:50
  610.5 7.9 %collective-permute-start.60 = (bf16[96,768]{1,0:T(8,128)(2,1)S(1)}, bf16[96,768]{1,0:T(8,128)(2,1)S(1)}, u32[]{:S(2)}, u32[]{:S(2)}) collective-permute-start(bf16[96,768]{1,0:T(8,128)(2,1)S(1)} %get-tuple-element.286), channel_id=1, source_target_pairs={{0,6},{2,4},{4,2},{6,0},{1,7},{3,5},{5,3},{7,1},{8,14},{10,12},{12... | collective-permute-start | bytes 442376 | tf_op jit(solution)/shard_map/ppermute | solution.py:53
  (90 other events, 454.5 us)
Sparse Core Ops, SparseCore 0:
  25.3 52.0 all-gather.8
  79.7 89.2 all-gather.4
  171.1 69.8 all-gather.6
  282.0 88.6 reduce-scatter.3
  372.8 66.6 reduce-scatter.5
  528.0 49.9 reduce-scatter.7

commit v3 on v2

--- a/solution.py
+++ b/solution.py
@@ -33,6 +33,12 @@
     return lax.optimization_barrier((value,) + others)[0]
 
 
+def together(*groups):
+    flat = lax.optimization_barrier(tuple(value for group in groups for value in group))
+    ends = np.cumsum([len(group) for group in groups])
+    return [list(flat[end - len(group) : end]) for end, group in zip(ends, groups)]
+
+
 def by_xor(stack, bits):
     places = np.arange(stack.shape[0])
     for level, bit in enumerate(bits):
@@ -69,45 +75,32 @@
     return exchange_second(exchange_first(by_xor(stack, plane_bits())))
 
 
-def gather_first(own):
-    return plane_swap(own, 1), plane_swap(own, 2)
-
-
-def gather_second(own, from_x, from_y):
-    half = own.shape[0] // 32 * 16
-    return [own, from_x, from_y, plane_swap(from_x[:half], 2), plane_swap(from_y[half:], 1)]
+def gather_first(top, low):
+    return [plane_swap(part, offset) for offset in (1, 2) for part in (top, low)]
+
+
+def gather_second(near):
+    return [plane_swap(near[0], 2), plane_swap(near[3], 1)]
 
 
 def plane_gather(own):
-    return gather_second(own, *gather_first(own))
-
-
-def reduce_first(parts):
-    to_x, to_y = parts[0], parts[1]
-    return plane_swap(to_x, 1), plane_swap(to_y, 2)
-
-
-def reduce_second(parts, low_in, top_in):
-    _, _, _, mine_x, mine_y = parts
-    top_on = (mine_x.astype(f32) + top_in[1].astype(f32)).astype(bf16)
-    low_on = (mine_y.astype(f32) + low_in[1].astype(f32)).astype(bf16)
-    return plane_swap(top_on, 1), plane_swap(low_on, 2)
-
-
-def reduce_end(parts, low_in, top_in, top_last, low_last):
-    own = parts[2].astype(f32)
-    half = top_last.shape[0]
-    top = own[:half] + top_in[0].astype(f32) + top_last.astype(f32)
-    low = own[half:] + low_in[0].astype(f32) + low_last.astype(f32)
-    return jnp.concatenate([top, low], axis=0)
-
-
-def plane_reduce(parts, *held):
-    low_in, top_in = reduce_first(parts)
-    top_last, low_last = reduce_second(parts, low_in, top_in)
-    if held:
-        top_last, low_last = lax.optimization_barrier((top_last, low_last) + held)[:2]
-    return reduce_end(parts, low_in, top_in, top_last, low_last)
+    half = own.shape[0] // 2
+    near = gather_first(own[:half], own[half:])
+    return [own] + near + gather_second(near)
+
+
+def reduce_far(parts):
+    return [plane_swap(parts[0], 1), plane_swap(parts[1], 2)]
+
+
+def reduce_near(parts):
+    return [plane_swap(parts[2], 1), plane_swap(parts[3], 2)]
+
+
+def reduce_passed(parts, far):
+    low_on = (parts[6].astype(f32) + far[0].astype(f32)).astype(bf16)
+    top_on = (parts[5].astype(f32) + far[1].astype(f32)).astype(bf16)
+    return [top_on, low_on], [plane_swap(top_on, 1), plane_swap(low_on, 2)]
 
 
 def halo_forward(tails):
@@ -132,12 +125,6 @@
     return jnp.where(lax.axis_index("mp") == 1, jnp.moveaxis(shifted, 0, 1), got)
 
 
-def both_cores(own):
-    other = core_swap(own)
-    first = lax.axis_index("mp") == 0
-    return jnp.concatenate([jnp.where(first, own, other), jnp.where(first, other, own)], axis=0)
-
-
 def taps_turn(back):
     planes = lax.axis_size("z")
     pairs = [(s, (s % planes) * 4 + s // planes) for s in range(4 * planes)]
@@ -145,11 +132,14 @@
 
 
 def call(body, out_shapes, *args, grid=None, in_specs=None, out_specs=None, prefetch=0, flops=0, aliases=None):
-    whole = pl.BlockSpec(memory_space=pltpu.VMEM)
+    def whole(value):
+        zeros = (0,) * len(value.shape)
+        return pl.BlockSpec(value.shape, lambda *_: zeros)
+
     if in_specs is None:
-        in_specs = [whole] * (len(args) - prefetch)
+        in_specs = [whole(value) for value in args[prefetch:]]
     if out_specs is None:
-        out_specs = [whole] * len(out_shapes)
+        out_specs = [whole(value) for value in out_shapes]
     moved = sum(a.size * a.dtype.itemsize for a in args)
     moved += sum(o.size * o.dtype.itemsize for o in out_shapes)
     return pl.pallas_call(
@@ -157,13 +147,13 @@
         out_shape=out_shapes,
         grid_spec=pltpu.PrefetchScalarGridSpec(
             num_scalar_prefetch=prefetch,
-            grid=grid or (),
+            grid=grid or (1,),
             in_specs=in_specs,
             out_specs=out_specs,
         ),
         input_output_aliases=aliases or {},
         compiler_params=pltpu.CompilerParams(vmem_limit_bytes=VMEM_LIMIT),
-        cost_estimate=pl.CostEstimate(flops=flops // 1000, bytes_accessed=moved // 1000, transcendentals=0),
+        cost_estimate=pl.CostEstimate(flops=flops // 10000, bytes_accessed=moved // 10000, transcendentals=0),
     )(*args)
 
 
@@ -173,47 +163,57 @@
 
 def spans(seg):
     half = seg // 2
-    return ((0, 0, 0, seg), (1, 1, 0, seg), (2, 2, 0, seg), (3, 3, 0, half), (4, 3, half, seg - half))
+    parts = [(0, 0, 0, seg)]
+    for segment in (1, 2, 3):
+        parts.append((2 * segment - 1, segment, 0, half))
+        parts.append((2 * segment, segment, half, seg - half))
+    return parts
+
+
+BLOCKS = 7
 
 
 def split_shapes(seg, width):
     half = seg // 2
-    return [
-        out((2, half, width), bf16),
-        out((2, half, width), bf16),
-        out((seg, width), bf16),
-        out((half, width), bf16),
-        out((half, width), bf16),
-    ]
-
-
-def split_store(refs, place, value):
-    to_x, to_y, own, mine_x, mine_y = refs
+    return [out((seg if place == 4 else half, width), bf16) for place in range(BLOCKS)]
+
+
+def split_store(refs, segment, value):
     value = value.astype(bf16)
     half = value.shape[0] // 2
-    top, low = value[:half], value[half:]
-    if place == 0:
-        own[...] = value
-    elif place == 1:
-        mine_x[...] = top
-        to_x[0] = low
-    elif place == 2:
-        to_y[0] = top
-        mine_y[...] = low
-    else:
-        to_y[1] = top
-        to_x[1] = low
-
-
-def conv_project(hats, pack, seg):
+    if segment == 0:
+        refs[4][...] = value
+        return
+    top, low = {1: (5, 2), 2: (3, 6), 3: (1, 0)}[segment]
+    refs[top][...] = value[:half]
+    refs[low][...] = value[half:]
+
+
+def conv_project(hats, pack, seg, tap_len):
     planes, _, rows_taps, cols = pack.shape
     rows, chan = rows_taps - 16, cols // 4
     width = planes * rows
 
     def body(*refs):
-        hat_refs, pack_ref, b_ref, c_ref, x_ref, u_ref = refs[:5], *refs[5:]
+        hat_refs, pack_ref = refs[:BLOCKS], refs[BLOCKS]
+        b_ref, c_ref, x_ref, u_ref, keep_ref, taps_ref, tails_ref, gate_ref = refs[BLOCKS + 1 :]
+        for segment, place in enumerate((0, 2, 4, 6)):
+            below = hat_refs[place].shape[0] - 16
+            begins = hat_refs[place][below:, :seg].astype(f32)[0:1]
+            begins = jnp.transpose(jnp.broadcast_to(begins, (LANES, seg)))
+            before = jnp.where(rows_of((seg, LANES)) == 0, 0.0, pltpu.roll(begins, 1, 0))
+            keep_one = (1.0 - begins)[:, :1]
+            keep_ref[0, segment] = keep_one
+            keep_ref[1, segment] = ((1.0 - begins) * (1.0 - before))[:, :1]
+            gate_ref[segment, 0:1] = keep_one[seg - 1 :]
+            gate_ref[segment, 1:2] = jnp.ones((1, 1), f32)
         for half in range(2):
             weights = pack_ref[:, half, :rows, :].reshape(width, cols)
+            for plane in range(planes):
+                row = pack_ref[plane, half, rows:, :].astype(f32)[0:1]
+                for k in range(3):
+                    at = pl.ds(plane * tap_len, tap_len)
+                    taps_ref[half, k : k + 1, at] = row[:, k * tap_len : (k + 1) * tap_len]
             for place, segment, low, count in spans(seg):
                 proj = nn(hat_refs[place][:count, :], weights)
                 b_val, c_val, x_val = (
@@ -225,16 +225,23 @@
                 b_ref[at] = b_val
                 c_ref[at] = c_val
                 x_ref[at] = x_val
-                u_ref[at] = (b_val * x_val).astype(bf16)
+                u_val = b_val * x_val
+                u_ref[at] = u_val.astype(bf16)
+                if low + count == seg:
+                    last = u_val[count - 2 :].astype(bf16).astype(f32) * gate_ref[segment]
+                    tails_ref[half, segment] = last.astype(bf16)
 
     shape = (2, 4, seg, chan)
-    return call(
-        body,
-        [out(shape, f32)] * 3 + [out(shape, bf16)],
+    results = call(
+        body,
+        [out(shape, f32)] * 3
+        + [out(shape, bf16), out((2, 4, seg, 1), f32), out((2, 3, chan), f32)]
+        + [out((2, 4, 2, chan), bf16), out((4, 2, 1), f32)],
         *hats,
         pack,
         flops=2 * 4 * seg * width * cols * 2,
     )
+    return results[:4], results[4:]
 
 
 def rows_of(shape):
@@ -293,9 +300,9 @@
     width = planes * rows
 
     def body(*refs):
-        mix_refs = refs[:5]
-        u_ref, halo_ref, c_ref, v_ref, keep_ref, taps_ref, pack_ref = refs[5:12]
-        dc_ref, dv_ref, sums_ref, heads_ref = refs[12:]
+        mix_refs, refs = refs[:BLOCKS], refs[BLOCKS:]
+        u_ref, halo_ref, c_ref, v_ref, keep_ref, taps_ref, pack_ref = refs[:7]
+        dc_ref, dv_ref, sums_ref, heads_ref = refs[7:]
         for half in range(2):
             outs = pack_ref[:, half, :rows, 2 * chan : 3 * chan].reshape(width, chan)
             for place, segment, low, count in spans(seg):
@@ -399,7 +406,6 @@
                     for value, column in zip(values, (2 * t, 2 * t + 1, 2 * tiles + t)):
                         out_ref[q ^ place_ref[0], :, column * LANES : (column + 1) * LANES] = value
 
-    whole = pl.BlockSpec(memory_space=pltpu.VMEM)
     return call(
         body,
         [out((4, rows, 3 * LANES * (high - low)), bf16) for low, high in cuts],
@@ -408,8 +414,48 @@
         up,
         down,
         gain,
-        in_specs=[whole] * 4,
-        out_specs=[whole] * 2,
+        prefetch=1,
+    )
+
+
+def ffn_unpack(first, second, gate, up, gain, place, cuts, chan_hid):
+    rows, half_f = gate.shape
+    hid = chan_hid
+
+    def body(place_ref, first_ref, second_ref, gate_ref, up_ref, gain_ref, gu_ref, down_ref, sum_ref):
+        scale = gain_ref[...]
+        total = jnp.zeros((rows, LANES), f32)
+        for q in range(4):
+            for (low, high), ref in zip(cuts, (first_ref, second_ref)):
+                tiles = high - low
+                for t in range(tiles):
+                    start = (low + t) * LANES
+                    count = min(hid - start, LANES)
+                    at = q * hid + start
+                    values = [
+                        ref[q ^ place_ref[0], :, column * LANES : (column + 1) * LANES].astype(f32)
+                        for column in (2 * t, 2 * t + 1, 2 * tiles + t)
+                    ]
+                    for side, w_ref in enumerate((gate_ref, up_ref)):
+                        weight = w_ref[:, at : at + count].astype(f32)
+                        if count < LANES:
+                            fill = jnp.zeros((rows, LANES - count), f32)
+                            weight = jnp.concatenate([weight, fill], axis=1)
+                        total = total + values[side] * weight
+                        base = side * half_f + at
+                        gu_ref[:, base : base + count] = (values[side] * scale)[:, :count]
+                    down_ref[:, at : at + count] = values[2][:, :count]
+        sum_ref[...] = jnp.sum(total, axis=1, keepdims=True)
+
+    return call(
+        body,
+        [out((rows, 2 * half_f), f32), out((rows, half_f), f32), out((rows, 1), f32)],
+        place,
+        first,
+        second,
+        gate,
+        up,
+        gain,
         prefetch=1,
     )
 
@@ -496,10 +542,10 @@
             split_store(split, segment, total)
 
     cols = [left.shape[-1] for left in lefts]
-    half_seg = seg // 2
+    shapes = split_shapes(seg, width)
     return call(
         body,
-        split_shapes(seg, width),
+        shapes,
         *lefts,
         *packs,
         grid=(planes // group,),
@@ -508,61 +554,213 @@
             pl.BlockSpec((group, 2, rows, c), functools.partial(lambda p, i: (i, 0, 0, p), place))
             for c in cols
         ],
-        out_specs=[
-            pl.BlockSpec((2, half_seg, wide), lambda i: (0, 0, i)),
-            pl.BlockSpec((2, half_seg, wide), lambda i: (0, 0, i)),
-            pl.BlockSpec((seg, wide), lambda i: (0, i)),
-            pl.BlockSpec((half_seg, wide), lambda i: (0, i)),
-            pl.BlockSpec((half_seg, wide), lambda i: (0, i)),
-        ],
+        out_specs=[pl.BlockSpec((shape.shape[0], wide), lambda i: (0, i)) for shape in shapes],
         flops=2 * 4 * seg * width * 2 * sum(cols),
     )
 
 
-def weight_grad(which, lefts, right, others, other_right, at, cols, extra, seg):
+def weight_grad(lefts, right, others, other_right, at, rows, seg, extra=None):
     width = lefts[0].shape[1]
     wide = 384
+    group = wide // rows
     first, second = right.shape[-1], other_right.shape[-1]
-
-    def body(which_ref, *refs):
-        left_refs, other_refs, right_ref, other_ref = refs[:5], refs[5:10], refs[10], refs[11]
-        out_ref = refs[-1]
+    cols = max(first, at + second)
+    below = 0 if extra is None else extra.shape[2]
+
+    def body(*refs):
+        left_refs, other_refs, refs = refs[:BLOCKS], refs[BLOCKS : 2 * BLOCKS], refs[2 * BLOCKS :]
+        right_ref, other_ref, out_ref = refs[0], refs[1], refs[-1]
 
         def gathered(places):
             return jnp.concatenate(
                 [places[place][:count, :] for place, _, _, count in spans(seg)], axis=0
             )
 
-        def put(low, high, value):
-            if extra is not None:
-                value = value + refs[12][:, low:high].astype(f32)
-            out_ref[:, low:high] = value.astype(bf16)
-
-        put(0, first, tn(gathered(left_refs), right_ref[0]))
-        put(at, at + second, tn(gathered(other_refs), other_ref[0]))
+        def put(low, value):
+            value = value.astype(bf16).reshape(group, rows, value.shape[-1])
+            out_ref[:, 0, :rows, low : low + value.shape[-1]] = value
+
+        put(0, tn(gathered(left_refs), right_ref[0]))
+        put(at, tn(gathered(other_refs), other_ref[0]))
+        if extra is not None:
+            out_ref[:, 0, rows:, :] = refs[2][:, 0]
 
     def column(value):
-        return pl.BlockSpec((value.shape[0], wide), lambda i, w: (0, i))
+        return pl.BlockSpec((value.shape[0], wide), lambda h, i: (0, i))
 
     def chosen(value):
-        return pl.BlockSpec((1,) + value.shape[1:], lambda i, w: (w[0], 0, 0))
-
-    tile = pl.BlockSpec((wide, cols), lambda i, w: (i, 0))
+        return pl.BlockSpec((1,) + value.shape[1:], lambda h, i: (h, 0, 0))
+
     args = [*lefts, *others, right, other_right]
     specs = [column(v) for v in (*lefts, *others)] + [chosen(right), chosen(other_right)]
     if extra is not None:
         args.append(extra)
-        specs.append(tile)
+        specs.append(pl.BlockSpec((group, 1, below, cols), lambda h, i: (i, h, 0, 0)))
     return call(
         body,
-        [out((width, cols), bf16)],
-        which,
+        [out((width // rows, 2, rows + below, cols), bf16)],
         *args,
-        grid=(width // wide,),
+        grid=(2, width // wide),
         in_specs=specs,
-        out_specs=[tile],
+        out_specs=[
+            pl.BlockSpec((group, 1, rows + below, cols), lambda h, i: (i, h, 0, 0)),
+        ],
+        flops=2 * 4 * seg * width * cols * 2,
+    )[0]
+
+
+def sum_parts(own_ref, last_refs):
+    top_passed, low_passed, low_near, top_near = [ref[...].astype(f32) for ref in last_refs]
+    half = top_near.shape[0]
+    own = own_ref[...].astype(f32)
+    return jnp.concatenate(
+        [own[:half] + top_near + top_passed, own[half:] + low_near + low_passed], axis=0
+    )
+
+
+def halves(shape, dtype):
+    return [out((shape[0] // 2,) + shape[1:], dtype)] * 2
+
+
+def store_halves(value, refs):
+    half = value.shape[0] // 2
+    refs[0][...] = value[:half]
+    refs[1][...] = value[half:]
+
+
+def middle_norm(parts, last, tokens, core):
+    rows, width = parts[4].shape
+
+    def body(core_ref, own_ref, *refs):
+        last_refs, token_ref, mid_ref, inv_ref, hat_ref, *half_refs = refs[:4], *refs[4:]
+        middle = token_ref[...].astype(f32) + sum_parts(own_ref, last_refs)
+        inv = lax.rsqrt(jnp.mean(middle * middle, axis=-1, keepdims=True) + epsilon)
+        hat = (middle * inv).astype(bf16)
+        mid_ref[...] = middle
+        inv_ref[...] = inv
+        hat_ref[...] = hat
+        store_halves(hat, half_refs)
+
+    shape = (rows, width)
+    return on_core(
+        body,
+        [out(shape, f32), out((rows, 1), f32), out(shape, bf16)] + halves(shape, bf16),
+        core,
+        [parts[4], *last],
+        [tokens],
+    )
+
+
+def middle_back(parts, last, middle, inv, cot, core):
+    rows, width = parts[4].shape
+
+    def body(core_ref, own_ref, *refs):
+        last_refs, mid_ref, inv_ref, cot_ref, grad_ref, round_ref, *half_refs = (
+            refs[:4],
+            *refs[4:],
+        )
+        grad = sum_parts(own_ref, last_refs)
+        inv = inv_ref[...]
+        hat = mid_ref[...] * inv
+        inner = jnp.mean(grad * hat, axis=-1, keepdims=True)
+        grad = cot_ref[...].astype(f32) + inv * (grad - hat * inner)
+        grad_ref[...] = grad
+        rounded = grad.astype(bf16)
+        round_ref[...] = rounded
+        store_halves(rounded, half_refs)
+
+    shape = (rows, width)
+    return on_core(
+        body,
+        [out(shape, f32), out(shape, bf16)] + halves(shape, bf16),
+        core,
+        [parts[4], *last, middle, inv, cot],
+        [],
+    )
+
+
+def on_core(body, shapes, core, args, by_core, both=()):
+    def whole(value):
+        zeros = (0,) * len(value.shape)
+        return pl.BlockSpec(value.shape, lambda i, c: zeros)
+
+    def part(value):
+        return pl.BlockSpec((value.shape[0] // 2, value.shape[1]), lambda i, c: (c[0], 0))
+
+    return call(
+        body,
+        list(shapes) + list(both),
+        core,
+        *args,
+        *by_core,
+        in_specs=[whole(v) for v in args] + [part(v) for v in by_core],
+        out_specs=[whole(v) for v in shapes] + [part(v) for v in both],
         prefetch=1,
-        flops=2 * 4 * seg * width * cols,
+    )
+
+
+def block_out(parts, last, middle, core):
+    rows, width = middle.shape
+
+    def body(core_ref, own_ref, *refs):
+        last_refs, mid_ref, result_ref, both_ref = refs[:4], *refs[4:]
+        result = (mid_ref[...] + sum_parts(own_ref, last_refs)).astype(bf16)
+        result_ref[...] = result
+        both_ref[...] = result
+
+    return on_core(
+        body,
+        [out((rows, width), bf16)],
+        core,
+        [parts[4], *last, middle],
+        [],
+        [out((2 * rows, width), bf16)],
+    )
+
+
+def tokens_back(parts, last, grad_middle, tokens, core):
+    rows, width = grad_middle.shape
+
+    def body(core_ref, own_ref, *refs):
+        last_refs, grad_ref, token_ref, result_ref, both_ref = refs[:4], *refs[4:]
+        grad = sum_parts(own_ref, last_refs)
+        values = token_ref[...].astype(f32)
+        inv = lax.rsqrt(jnp.mean(values * values, axis=-1, keepdims=True) + epsilon)
+        hat = values * inv
+        inner = jnp.mean(grad * hat, axis=-1, keepdims=True)
+        result = grad_ref[...] + inv * (grad - hat * inner)
+        result_ref[...] = result
+        both_ref[...] = result
+
+    return on_core(
+        body,
+        [out((rows, width), f32)],
+        core,
+        [parts[4], *last, grad_middle],
+        [tokens],
+        [out((2 * rows, width), f32)],
+    )
+
+
+def fill_other(both, other, core):
+    rows, width = other.shape
+
+    def body(core_ref, other_ref, _, both_ref):
+        both_ref[...] = other_ref[...]
+
+    return call(
+        body,
+        [out(both.shape, both.dtype)],
+        core,
+        other,
+        both,
+        in_specs=[
+            pl.BlockSpec((rows, width), lambda i, c: (0, 0)),
+            pl.BlockSpec(memory_space=pl.ANY),
+        ],
+        out_specs=[pl.BlockSpec((rows, width), lambda i, c: (1 - c[0], 0))],
+        prefetch=1,
+        aliases={2: 0},
     )[0]
 
 
@@ -582,7 +780,6 @@
     cuts = ((0, tiles // 2 + 1), (tiles // 2 + 1, tiles))
     sizes = [LANES * (high - low) for low, high in cuts]
     own_half = core.astype(jnp.int32).reshape(1)
-    other_half = 1 - own_half
 
     def mine(value):
         return lax.dynamic_slice_in_dim(value, core * seg, seg, axis=0)
@@ -609,11 +806,14 @@
     inputs = mine(tokens).astype(f32)
     inv_mix = lax.rsqrt(jnp.mean(inputs * inputs, axis=-1, keepdims=True) + epsilon)
     hat_mix = inputs * inv_mix
-    begin_row = mine(starts).astype(bf16)[None]
-    begin_rows = jnp.pad(begin_row, ((0, 15), (0, width - seg)))
-    hat_own = jnp.concatenate([hat_mix.astype(bf16), begin_rows], axis=0)
-    hat_own = after(hat_own, conv_quart)
-    hat_x, hat_y = gather_first(hat_own)
+    hat_own = hat_mix.astype(bf16)
+    begin_rows = jnp.pad(mine(starts).astype(bf16)[None], ((0, 15), (0, width - seg)))
+    half_seg = seg // 2
+    hat_low = jnp.concatenate([hat_own[half_seg:], begin_rows], axis=0)
+    hat_top = hat_own[:half_seg]
+    hat_own = jnp.concatenate([hat_own, begin_rows], axis=0)
+    hat_own, hat_top, hat_low = lax.optimization_barrier((hat_own, hat_top, hat_low, conv_quart))[:3]
+    hats_near = gather_first(hat_top, hat_low)
     conv_pack = exchange_second(after(conv_got, hat_own)).reshape(plane_rows, 4 * chan)
     conv_pack = jnp.concatenate([conv_pack, tap_rows], axis=0)
     conv_all = over_all(conv_pack)
@@ -624,129 +824,132 @@
         gate_up[:, 0], gate_up[:, 1], w_down.T, gain_two[:, 0], place, cuts, hid
     )
     first_quart, second_quart = packs
-    hats = gather_second(hat_own, hat_x, hat_y)
     first_got = exchange_first(first_quart)
-    first_pack = exchange_second(after(first_got, hat_x, hat_y)).reshape(plane_rows, -1)
-    cot, second_quart = lax.optimization_barrier((cot, second_quart, first_pack, *hats[3:]))[:2]
+    hats_near, first_got = together(hats_near, first_got)
+    hats = [hat_own] + hats_near + gather_second(hats_near)
+    first_pack = exchange_second(first_got).reshape(plane_rows, -1)
+    cot, cot_top, cot_low = lax.optimization_barrier(
+        (cot, cot[:half_seg], cot[half_seg:], *hats[5:])
+    )[:3]
+    cots_near = gather_first(cot_top, cot_low)
+
+    projected, marks = conv_project(hats, conv_all, seg, tap_len)
+    projected, marks, cots_near, (second_quart,) = together(
+        projected, marks, cots_near, (second_quart,)
+    )
+    b_part, c_part, x_part, mixed_in = projected
+    keeps, taps, tails, tail_gate = marks
     second_got = exchange_first(second_quart)
-    cot_x, cot_y = gather_first(cot)
-
-    begins = jnp.stack(
-        [hats[0][seg, :seg], hats[1][seg, :seg], hats[2][seg, :seg], hats[4][-16, :seg]]
-    ).astype(f32)
-    earlier = jnp.concatenate([jnp.zeros((4, 1), f32), begins[:, :-1]], axis=1)
-    keeps = jnp.stack([1.0 - begins, (1.0 - begins) * (1.0 - earlier)])[..., None]
-    last_keep = 1.0 - begins[:, -1:]
-    taps = conv_all[:, :, plane_rows, : 3 * tap_len].reshape(planes, 2, 3, tap_len)
-    taps = jnp.transpose(taps, (1, 2, 0, 3)).reshape(2, 3, chan).astype(f32)
-
-    b_part, c_part, x_part, mixed_in = conv_project(hats, conv_all, seg)
-    tails = mixed_in[:, :, seg - 2 :]
-    tail_gate = jnp.stack([last_keep, jnp.ones((4, 1), f32)], axis=1)
-    halo = halo_forward((tails * tail_gate).astype(bf16)).astype(f32)
+    halo = halo_forward(tails).astype(f32)
     convolved, gated, mixer = conv_mix(mixed_in, halo, c_part, keeps, taps, conv_all, seg)
-    first_in = reduce_first(mixer)
-    second_got, cot_x, cot_y = lax.optimization_barrier((second_got, cot_x, cot_y, *mixer))[:3]
-    cots = gather_second(cot, cot_x, cot_y)
+    mixer, second_got = together(mixer, second_got)
+    far, near = reduce_far(mixer), reduce_near(mixer)
     second_pack = exchange_second(second_got).reshape(plane_rows, -1)
     ffn_all = [over_all(first_pack), over_all(second_pack)]
-    first_in = lax.optimization_barrier((*first_in, second_pack))[:2]
-    middle = inputs + reduce_end(mixer, *first_in, *reduce_second(mixer, *first_in))
-
-    inv_ffn = lax.rsqrt(jnp.mean(middle * middle, axis=-1, keepdims=True) + epsilon)
-    hat_ffn = middle * inv_ffn
-    hats_two = plane_gather(hat_ffn.astype(bf16))
-
-    def other_grad(lefts, right, others, other_right, at, cols):
-        theirs = weight_grad(other_half, lefts, right, others, other_right, at, cols, None, seg)
-        return core_swap(theirs), theirs
-
-    def own_grad(lefts, right, others, other_right, at, cols, theirs):
-        return weight_grad(own_half, lefts, right, others, other_right, at, cols, theirs, seg)
-
-    def over_z(value, *held):
-        value = after(value, *held)
-        return lax.psum_scatter(value, "z", scatter_dimension=0, tiled=True)
-
-    def cut_grads(acts, grads, size):
-        given = (hats_two, grads, cots, acts, 2 * size, 3 * size)
-        return own_grad(*given, other_grad(*given))
-
-    done_one = ffn_pass(hats_two, cots, ffn_all[0], sizes[0], seg, (0, 1, 2))
-    acts_one, grads_one = ffn_pass(hats_two, cots, ffn_all[0], sizes[0], seg, (3,), done_one)
-    given = (hats_two, grads_one, cots, acts_one, 2 * sizes[0], 3 * sizes[0])
-    theirs = other_grad(*given)
-    second_all = after(ffn_all[1], theirs[1])
+    far, near, mixer, _ = together(far, near, mixer, (second_pack,))
+    passed = reduce_passed(mixer, far)[1]
+    last, mixer = together(passed + near, mixer)
+    middle, inv_ffn, hat_own, hat_top, hat_low = middle_norm(mixer, last, tokens, own_half)
+
+    near = gather_first(hat_top, hat_low)
+
+    def first_cut(segment, earlier):
+        return ffn_pass(hats_two, cots, ffn_all[0], sizes[0], seg, (segment,), earlier)
+
+    hats_two, cots = [hat_own], [cot] + cots_near
+    done_one = first_cut(0, None)
+    done_one, near, cots_near = together(done_one, near, cots_near)
+    hats_two, cots = [hat_own] + near, [cot] + cots_near
+    far, cots_far = gather_second(near), gather_second(cots_near)
+    done_one = first_cut(2, first_cut(1, done_one))
+    done_one, far, cots_far = together(done_one, far, cots_far)
+    hats_two, cots = hats_two + far, cots + cots_far
+
+    def ordered(value):
+        stack = by_xor(value.reshape(4, rows, -1), plane_bits())
+        return [stack[r] for r in range(4)]
+
+    def over_owners(value):
+        value = value.reshape((2 * planes,) + value.shape[2:])
+        return lax.psum_scatter(value, ("z", "mp"), scatter_dimension=0, tiled=False)
+
+    acts_one, grads_one = first_cut(3, done_one)
+    sum_one = weight_grad(hats_two, grads_one, cots, acts_one, 2 * sizes[0], plane_rows, seg)
+    red_one = over_owners(sum_one)
+    second_all = after(ffn_all[1], sum_one)
     acts_two, grads_two = ffn_pass(hats_two, cots, second_all, sizes[1], seg, (0, 1, 2, 3))
-    sum_one = own_grad(*given, after(theirs[0], acts_two))
-    red_one = over_z(sum_one)
-    grad_hat2 = turned_back(
-        [grads_one, after(grads_two, sum_one)], [ffn_all[0], second_all], 0, plane_rows, seg
-    )
+    grad_hat2 = turned_back([grads_one, grads_two], [ffn_all[0], second_all], 0, plane_rows, seg)
+    far, near = reduce_far(grad_hat2), reduce_near(grad_hat2)
     acts_two, grads_two = lax.optimization_barrier((acts_two, grads_two, *grad_hat2))[:2]
-    given = (hats_two, grads_two, cots, acts_two, 2 * sizes[1], 3 * sizes[1])
-    sum_two = own_grad(*given, other_grad(*given)[0])
-    red_two = over_z(sum_two)
-    first_in = reduce_first(grad_hat2)
-    first_in = lax.optimization_barrier((*first_in, sum_two))[:2]
-    last_in = reduce_second(grad_hat2, *first_in)
-    last_in = lax.optimization_barrier((*last_in, red_one))[:2]
-    grad_hat2 = reduce_end(grad_hat2, *first_in, *last_in)
-    inner = jnp.mean(grad_hat2 * hat_ffn, axis=-1, keepdims=True)
-    grad_middle = cot.astype(f32) + inv_ffn * (grad_hat2 - hat_ffn * inner)
-
-    mixer_own = grad_middle.astype(bf16)
-    mixer_x, mixer_y = gather_first(mixer_own)
-    ffn_out = turned_back(
-        [acts_one, after(acts_two, mixer_own)], [ffn_all[0], second_all], 2, plane_rows, seg
-    )
-    mixer_x, mixer_y = lax.optimization_barrier((mixer_x, mixer_y, *ffn_out))[:2]
-    grad_mixer = gather_second(mixer_own, mixer_x, mixer_y)
-    ffn_out = lax.optimization_barrier((*ffn_out, *grad_mixer))[:5]
+    sum_two = weight_grad(hats_two, grads_two, cots, acts_two, 2 * sizes[1], plane_rows, seg)
+    far, near, grad_hat2, (sum_two,) = together(far, near, grad_hat2, (sum_two,))
+    red_two = over_owners(sum_two)
+    sent, passed = reduce_passed(grad_hat2, far)
+    acts_last = lax.optimization_barrier((acts_two, *sent))[0]
+    ffn_out = turned_back([acts_one, acts_last], [ffn_all[0], second_all], 2, plane_rows, seg)
+    last, ffn_out, grad_hat2 = together(passed + near, ffn_out, grad_hat2)
+    grad_middle, mix_own, mix_top, mix_low = middle_back(
+        grad_hat2, last, middle, inv_ffn, cot, own_half
+    )
+
+    near = gather_first(mix_top, mix_low)
+    near, (back_one,) = together(near, (red_one,))
+    grad_mixer = [mix_own] + near + gather_second(near)
+    ffn_out, grad_mixer = together(ffn_out, grad_mixer)
+    ffn_far = reduce_far(ffn_out)
     grad_c, grad_v, tap_sums, heads = conv_back(
         grad_mixer, mixed_in, halo, c_part, convolved, keeps, taps, conv_all, seg
     )
+    (heads,), ffn_far, ffn_out = together((heads,), ffn_far, ffn_out)
+    ffn_passed = reduce_passed(ffn_out, ffn_far)[1]
     back = halo_backward(heads) * tail_gate
     grad_proj = conv_grads(grad_c, grad_v, back, b_part, x_part, keeps, taps, seg)
+    (grad_proj,), ffn_passed, back_one = together((grad_proj,), ffn_passed, ordered(back_one))
+    first_got = exchange_first(back_one)
+    ffn_near = reduce_near(ffn_out)
     gated = gated.reshape(2, 4 * seg, chan)
-    given = (hats, grad_proj, grad_mixer, gated, 2 * chan, 4 * chan)
-    theirs, sent = other_grad(given[0], after(grad_proj, red_two), *given[2:])
-    grad_hat1 = turned_back([after(grad_proj, sent)], [conv_all], 0, plane_rows, seg)
-    sum_conv = own_grad(*given, after(theirs, *grad_hat1))
-    red_conv = over_z(sum_conv)
-    first_in = reduce_first(grad_hat1)
-    first_in = lax.optimization_barrier((*first_in, sum_conv))[:2]
-    grad_hat1 = reduce_end(grad_hat1, *first_in, *reduce_second(grad_hat1, *first_in))
-    inner = jnp.mean(grad_hat1 * hat_mix, axis=-1, keepdims=True)
-    grad_inputs = grad_middle + inv_mix * (grad_hat1 - hat_mix * inner)
-    output_vals = (middle + plane_reduce(ffn_out)).astype(bf16)
-
-    tap_sums = jnp.where(core == 0, tap_sums, tap_sums[::-1])
-    tap_sum = tap_sums[0] + core_swap(tap_sums[1])
-    tap_sum = lax.psum(tap_sum, "z").reshape(3, planes, tap_len)
-    tap_sum = lax.dynamic_index_in_dim(tap_sum, lax.axis_index("z"), axis=1, keepdims=True)
-    tap_grad = lax.ppermute(tap_sum, ("z",) + PLANE, taps_turn(True))
-
-    def owned(value):
-        return plane_exchange(value.reshape(4, rows, -1))
-
-    cut_parts = [owned(after(value, sum_conv)) for value in (red_one, red_two)]
-    raw_gu = jnp.concatenate(
-        [
-            part[:, :, : 2 * size].reshape(4, rows, -1, 2, LANES)
-            for part, size in zip(cut_parts, sizes)
-        ],
-        axis=2,
-    )
-    raw_gu = jnp.transpose(raw_gu, (1, 3, 0, 2, 4)).reshape(rows, 2, 4, tiles * LANES)
-    raw_gu = raw_gu[..., :hid].reshape(rows, 2, half_f).astype(f32)
-    raw_down = jnp.concatenate(
-        [part[:, :, 2 * size :] for part, size in zip(cut_parts, sizes)], axis=2
-    )[:, :, :hid]
-    out_down = jnp.transpose(raw_down, (0, 2, 1)).reshape(half_f, rows).astype(f32)
-    output_vals, grad_inputs = both_cores(output_vals), both_cores(grad_inputs)
-    red_conv = after(red_conv, output_vals, grad_inputs, raw_gu, out_down, tap_grad)
-    conv_grad = owned(red_conv).astype(f32)
+    tap_rows = jnp.transpose(tap_sums.reshape(2, 3, planes, tap_len), (2, 0, 1, 3))
+    tap_rows = tap_rows.reshape(planes, 2, 1, 3 * tap_len).astype(bf16)
+    tap_rows = jnp.pad(tap_rows, ((0, 0), (0, 0), (0, 15), (0, 4 * chan - 3 * tap_len)))
+    sum_conv = weight_grad(
+        hats, grad_proj, grad_mixer, gated, 2 * chan, plane_rows, seg, tap_rows
+    )
+    red_conv = over_owners(sum_conv)
+    (grad_proj,), ffn_near, _ = together((grad_proj,), ffn_near, (sum_conv,))
+    grad_hat1 = turned_back([grad_proj], [conv_all], 0, plane_rows, seg)
+    grad_hat1, first_got, back_two = together(grad_hat1, first_got, ordered(red_two))
+    far, near = reduce_far(grad_hat1), reduce_near(grad_hat1)
+    out_own, out_both = block_out(ffn_out, ffn_passed + ffn_near, middle, own_half)
+    far, near, grad_hat1, (out_own, out_both) = together(far, near, grad_hat1, (out_own, out_both))
+    sent, passed = reduce_passed(grad_hat1, far)
+    back_two, _ = together(back_two, sent)
+    second_got = exchange_first(back_two)
+    output_vals = fill_other(out_both, core_swap(after(out_own, *sent)), own_half)
+
+    out_gu, down_turned, gain_sum = ffn_unpack(
+        jnp.stack(first_got),
+        jnp.stack(second_got),
+        gate_up[:, 0],
+        gate_up[:, 1],
+        gain_two[:, 0],
+        place,
+        cuts,
+        hid,
+    )
+    out_gu = out_gu.reshape(rows, 2, half_f)
+    out_down = down_turned.T
+    conv_got = exchange_first(ordered(red_conv[:plane_rows]))
+    last, grad_hat1, conv_got, (out_gu, out_down, gain_sum, output_vals) = together(
+        passed + near, grad_hat1, conv_got, (out_gu, out_down, gain_sum, output_vals)
+    )
+    grad_own, grad_both = tokens_back(grad_hat1, last, grad_middle, tokens, own_half)
+    grad_inputs = fill_other(grad_both, core_swap(grad_own), own_half)
+    conv_grad = exchange_second(conv_got).astype(f32)
+    tap_grad = lax.ppermute(
+        red_conv[plane_rows, : 3 * tap_len].astype(f32).reshape(3, 1, tap_len),
+        ("z",) + PLANE,
+        taps_turn(True),
+    )
 
     def conv_cols(k):
         return jnp.concatenate(
@@ -757,7 +960,7 @@
     gains = jnp.stack(
         [
             jnp.sum(raw_in * w_in.astype(f32), axis=(1, 2)),
-            jnp.sum(raw_gu * gate_up.astype(f32), axis=(1, 2)),
+            gain_sum[:, 0],
         ]
     )
     gains = gains + core_swap(gains)
@@ -766,7 +969,7 @@
         grad_inputs,
         raw_in * gain_one,
         conv_cols(2).T,
-        raw_gu * gain_two,
+        out_gu,
         out_down,
         gains[0],
         gains[1],

time: 639 us -> 613 us (0.959)
  other arithmetic: 62.4 us -> 23.4 us
  starting transfers between devices: 85.5 us -> 124 us
  local copies, waits for them, and re-layouts: 75.8 us -> 43.6 us
  Pallas kernels: 207 us -> 236 us
  waiting for transfers between devices: 179 us -> 161 us
  blocking collectives: 6.49 us -> 0 us
    ppermute x22 -> x30, waiting for transfers between devices: 58.6 us -> 89.4 us  [plane_swap(): return lax.ppermute(value, 'y', SWAP)]
    pallas_call x17 -> x23, Pallas kernels: 207 us -> 236 us  [call(): pl.pallas_call(body, out_shape=out_shapes, grid_spec=pltpu.PrefetchScalar...]
    ppermute x6, waiting for transfers between devices: 36.5 us -> 9.28 us  [plane_swap(): return lax.ppermute(value, PLANE, [(i, i ^ 3) for i in range(4)])]
    ppermute x9 -> x5, starting transfers between devices: 29.7 us -> 47.6 us  [core_swap(): return lax.ppermute(value, 'mp', SWAP)]
    convert_element_type x9 -> x5, local copies, waits for them, and re-layouts: 13.4 us -> 0.27 us  [the longest x4 0.19 us: per_device(): tap_rows = tap_rows.reshape(planes, 2, 1, 3 * tap_len).astype(bf16)]
    add x6 -> x0, other arithmetic: 12.7 us -> none  [the longest x4 8.48 us: reduce_end(): top = own[:half] + top_in[0].astype(f32) + top_last.astype(f32)]
    ppermute x22 -> x30, waiting for transfers between devices: 71.8 us -> 60.7 us  [plane_swap(): return lax.ppermute(value, 'x', SWAP)]
    convert_element_type x24 -> x14, other arithmetic: 19.4 us -> 8.83 us  [the longest x4 3.74 us: reduce_passed(): low_on = (parts[6].astype(f32) + far[0].astype(f32)).astype(bf16)]
  transfers between devices with their start and end apart: 69 -> 81, of which waited for: 29 -> 33; matrix products, arithmetic and copies ran while one was open for 16% -> 7% of each run, Pallas kernels for 31% -> 38%
where the time goes in v3:
time: 613 us; the launch traced here: 602 us
  Pallas kernels  236 us (38%)
  waiting for transfers between devices  161 us (26%)
  starting transfers between devices  124 us (20%)
  local copies, waits for them, and re-layouts  43.6 us (7%)
  other arithmetic  23.4 us (4%)
  between operations  15.5 us (3%)
    pallas_call x23, Pallas kernels, call(): pl.pallas_call(body, out_shape=out_shapes, grid_spec=pltpu.PrefetchScalar...  236 us
    ppermute x30, waiting for transfers between devices, plane_swap(): return lax.ppermute(value, 'y', SWAP)  89.4 us
    ppermute x30, waiting for transfers between devices, plane_swap(): return lax.ppermute(value, 'x', SWAP)  60.7 us
    ppermute x5, starting transfers between devices, core_swap(): return lax.ppermute(value, 'mp', SWAP)  47.6 us
    ppermute x30, starting transfers between devices, plane_swap(): return lax.ppermute(value, 'x', SWAP)  23.9 us
    unnamed x162, local copies, waits for them, and re-layouts  23.2 us
    ppermute x30, starting transfers between devices, plane_swap(): return lax.ppermute(value, 'y', SWAP)  23 us
    ppermute x1, starting transfers between devices, per_device(): lax.ppermute(red_conv[plane_rows, :3 * tap_len].astype(f32).reshape(3, 1,...  15.7 us
  transfers between devices with their start and end apart: 81, of which 33 were waited for; matrix products, arithmetic and copies ran while one was open for 7% of the time, Pallas kernels for 38%

profile of v3, /device:TPU:25, one launch (start us, length us, event | category | flops | bytes accessed | tf_op | source)
XLA Modules:
  0.0 602.5 jit_solution(12001627930296799383)
XLA Ops:
  8.0 3.7 collective-permute-start.12
  16.2 1.6 collective-permute-start.10
  21.8 2.9 collective-permute-done.10
  26.7 1.8 fusion.17
  31.6 1.5 collective-permute-start.6
  33.0 1.6 collective-permute-start.3
  34.8 1.5 collective-permute-start.5
  36.3 3.4 collective-permute-done.6
  39.7 2.8 collective-permute-start
  42.4 19.1 %collective-permute-done.5 = bf16[96,1536]{1,0:T(8,128)(2,1)S(1)} collective-permute-done((bf16[96,1536]{1,0:T(8,128)(2,1)S(1)}, bf16[96,1536]{1,0:T(8,128)(2,1)S(1)}, u32[]{:S(2)}, u32[]{:S(2)}) %collective-permute-start.5) | collective-permute-done | bytes 294944 | tf_op jit(solution)/shard_map/ppermute | solution.py:58
  61.5 1.9 collective-permute-start.4
  63.4 10.9 %collective-permute-done.4 = bf16[96,1536]{1,0:T(8,128)(2,1)S(1)} collective-permute-done((bf16[96,1536]{1,0:T(8,128)(2,1)S(1)}, bf16[96,1536]{1,0:T(8,128)(2,1)S(1)}, u32[]{:S(2)}, u32[]{:S(2)}) %collective-permute-start.4) | collective-permute-done | bytes 294944 | tf_op jit(solution)/shard_map/ppermute | solution.py:56
  78.2 1.8 collective-permute-start.8
  81.1 1.5 constant_dynamic-slice_fusion.2.refs_1_.refs_7_.refs_6_
  84.3 10.0 %collective-permute-done.7.refs_5_ = bf16[192,1536]{1,0:T(8,128)(2,1)} collective-permute-done((bf16[192,1536]{1,0:T(8,128)(2,1)S(1)}, bf16[192,1536]{1,0:T(8,128)(2,1)}, u32[]{:S(2)}, u32[]{:S(2)}) %collective-permute-start.7) | collective-permute-done | bytes 589856 | tf_op jit(solution)/shard_map/ppermute | solution.py:58
  95.1 1.6 collective-permute-start.15
  103.7 15.3 %shard_map.170 = (f32[2,4,384,192]{3,2,1,0:T(8,128)}, f32[2,4,384,192]{3,2,1,0:T(8,128)}, f32[2,4,384,192]{3,2,1,0:T(8,128)}, bf16[2,4,384,192]{3,2,1,0:T(8,128)...) custom-call(bf16[400,1536]{1,0:T(8,128)(2,1)} %pad_maximum_fusion.re, ...), custom_call_target="tpu_custom_call" | custom-call | flops 724775 | bytes 1811 | tf_op jit(solution)/shard_map/pallas_call | solution.py:145
  119.1 2.6 collective-permute-done.16.refs_3_.refs_11_
  121.6 1.5 collective-permute-done.14.refs_3_.refs_9_
  123.1 2.3 collective-permute-start.17
  129.2 9.6 %shard_map.171 = (f32[2,4,384,192]{3,2,1,0:T(8,128)}, bf16[2,4,384,192]{3,2,1,0:T(8,128)(2,1)}, bf16[192,1536]{1,0:T(8,128)(2,1)S(1)}, bf16[192,1536]{1,0:T(8,12...) custom-call(bf16[2,4,384,192]{3,2,1,0:T(8,128)(2,1)} %get-tuple-elem, ...), custom_call_target="tpu_custom_call" | custom-call | flops 181193 | bytes 1674 | tf_op jit(solution)/shard_map/pallas_call | solution.py:145
  143.6 1.5 collective-permute-start.25
  145.0 10.6 %collective-permute-done.22 = bf16[192,1536]{1,0:T(8,128)(2,1)S(1)} collective-permute-done((bf16[192,1536]{1,0:T(8,128)(2,1)}, bf16[192,1536]{1,0:T(8,128)(2,1)S(1)}, u32[]{:S(2)}, u32[]{:S(2)}) %collective-permute-start.22) | collective-permute-done | bytes 589856 | tf_op jit(solution)/shard_map/ppermute | solution.py:56
  155.7 12.5 %collective-permute-done.24.refs_2_ = bf16[192,1536]{1,0:T(8,128)(2,1)S(1)} collective-permute-done((bf16[192,1536]{1,0:T(8,128)(2,1)}, bf16[192,1536]{1,0:T(8,128)(2,1)S(1)}, u32[]{:S(2)}, u32[]{:S(2)}) %collective-permute-start.24) | collective-permute-done | bytes 589856 | tf_op jit(solution)/shard_map/ppermute | solution.py:56
  170.9 10.9 %collective-permute-done.27.refs_1_ = bf16[192,1536]{1,0:T(8,128)(2,1)S(1)} collective-permute-done((bf16[192,1536]{1,0:T(8,128)(2,1)S(1)}, bf16[192,1536]{1,0:T(8,128)(2,1)S(1)}, u32[]{:S(2)}, u32[]{:S(2)}) %collective-permute-start.27) | collective-permute-done | bytes 589856 | tf_op jit(solution)/shard_map/ppermute | solution.py:58
  181.8 5.0 shard_map.172
  191.8 8.1 %shard_map.173 = (bf16[2,1536,512]{2,1,0:T(8,128)(2,1)}, bf16[2,1536,1024]{2,1,0:T(8,128)(2,1)}) custom-call(bf16[384,1536]{1,0:T(8,128)(2,1)S(1)} %copy-done.1, bf16[384,1536]{1,0:T(8,128)(2,1)S(1)} %constant_dynamic-slice_fusion.2.refs_1_.refs_7_.refs_6_, bf16[4,2,384,1536]{3,2,1,0:T(8,128)(2,1)} %bitcast.232, bf16[4,2,384,1536]{3,2,1,0:T(8,128)(2,1)} %bitcast.233), custom_call_target="tpu_custom_call" | custom-call | flops 362387 | bytes 3067 | tf_op jit(solution)/shard_map/pallas_call | solution.py:145
  200.4 11.5 %collective-permute-done.31.refs_1_.refs_4_ = bf16[192,1536]{1,0:T(8,128)(2,1)} collective-permute-done((bf16[192,1536]{1,0:T(8,128)(2,1)}, bf16[192,1536]{1,0:T(8,128)(2,1)}, u32[]{:S(2)}, u32[]{:S(2)}) %collective-permute-start.31) | collective-permute-done | bytes 589856 | tf_op jit(solution)/shard_map/ppermute | solution.py:58
  216.0 8.5 %shard_map.174 = (bf16[2,1536,512]{2,1,0:T(8,128)(2,1)}, bf16[2,1536,1024]{2,1,0:T(8,128)(2,1)}) custom-call(bf16[192,1536]{1,0:T(8,128)(2,1)} %collective-permute-done.28.refs_0_.refs_1_, bf16[192,1536]{1,0:T(8,128)(2,1)} %collective-permute-done.29.refs_1_.refs_2_, ...), custom_call_target="tpu_custom_call", output_to_operand_aliasing={{0}: (6, {}), {1}: (7, {})} | custom-call | flops 362387 | bytes 4010 | tf_op jit(solution)/shard_map/pallas_call | solution.py:145
  224.5 8.4 %shard_map.175 = (bf16[2,1536,512]{2,1,0:T(8,128)(2,1)}, bf16[2,1536,1024]{2,1,0:T(8,128)(2,1)}) custom-call(bf16[192,1536]{1,0:T(8,128)(2,1)} %collective-permute-done.30.refs_0_.refs_3_, bf16[192,1536]{1,0:T(8,128)(2,1)} %collective-permute-done.31.refs_1_.refs_4_, ...), custom_call_target="tpu_custom_call", output_to_operand_aliasing={{0}: (6, {}), {1}: (7, {})} | custom-call | flops 362387 | bytes 4010 | tf_op jit(solution)/shard_map/pallas_call | solution.py:145
  232.9 4.6 collective-permute-done.35.refs_3_.refs_13_
  237.5 8.7 %shard_map.176 = (bf16[2,1536,512]{2,1,0:T(8,128)(2,1)}, bf16[2,1536,1024]{2,1,0:T(8,128)(2,1)}) custom-call(bf16[192,1536]{1,0:T(8,128)(2,1)S(1)} %collective-permute-done.32.refs_0_.refs_5_, bf16[192,1536]{1,0:T(8,128)(2,1)S(1)} %collective-permute-done.33.refs_1_.refs_6_, ...), custom_call_target="tpu_custom_call", output_to_operand_aliasing={{0}: (6, {}), {1}: (7, {})} | custom-call | flops 362387 | bytes 4010 | tf_op jit(solution)/shard_map/pallas_call | solution.py:145
  246.2 22.7 %shard_map.177 = bf16[4,2,384,1536]{3,2,1,0:T(8,128)(2,1)} custom-call(bf16[384,1536]{1,0:T(8,128)(2,1)} %get-tuple-element.307.refs_0_, bf16[192,1536]{1,0:T(8,128)(2,1)} %collective-permute-done.28.refs_0_.refs_1_, bf16[192,1536]{1,0:T(8,128)(2,1)} %collective-permute-done.29.refs_1_.refs_2_, bf16[192,1536]{1,0:T(8,128)(2,1)} %collective-permute-done.30.refs_0_.refs_3_, ...), custom_call_target="tpu_custom_call" | custom-call | flops 1449551 | bytes 2831 | tf_op jit(solution)/shard_map/pallas_call | solution.py:145
  269.9 17.2 %shard_map.178 = (bf16[2,1536,384]{2,1,0:T(8,128)(2,1)}, bf16[2,1536,768]{2,1,0:T(8,128)(2,1)}) custom-call(bf16[384,1536]{1,0:T(8,128)(2,1)} %get-tuple-element.307.refs_0_, bf16[192,1536]{1,0:T(8,128)(2,1)} %collective-permute-done.28.refs_0_.refs_1_, bf16[192,1536]{1,0:T(8,128)(2,1)} %collective-permute-done.29.refs_1_.refs_2_, ...), custom_call_target="tpu_custom_call" | custom-call | flops 1087163 | bytes 3067 | tf_op jit(solution)/shard_map/pallas_call | solution.py:145
  287.2 25.3 %shard_map.179 = (bf16[192,1536]{1,0:T(8,128)(2,1)S(1)}, bf16[192,1536]{1,0:T(8,128)(2,1)S(1)}, bf16[192,1536]{1,0:T(8,128)(2,1)S(1)}, bf16[192,1536]{1,0:T(8,12...) custom-call(bf16[2,1536,1024]{2,1,0:T(8,128)(2,1)} %get-tuple-element.341.refs_, ...), custom_call_target="tpu_custom_call" | custom-call | flops 1691143 | bytes 3224 | tf_op jit(solution)/shard_map/pallas_call | solution.py:145
  316.2 19.8 %shard_map.180 = bf16[4,2,384,1152]{3,2,1,0:T(8,128)(2,1)} custom-call(bf16[384,1536]{1,0:T(8,128)(2,1)} %get-tuple-element.307.refs_0_, bf16[192,1536]{1,0:T(8,128)(2,1)} %collective-permute-done.28.refs_0_.refs_1_, bf16[192,1536]{1,0:T(8,128)(2,1)} %collective-permute-done.29.refs_1_.refs_2_, bf16[192,1536]{1,0:T(8,128)(2,1)} %collective-permute-done.30.refs_0_.refs_3_, ...), custom_call_target="tpu_custom_call" | custom-call | flops 1087163 | bytes 2359 | tf_op jit(solution)/shard_map/pallas_call | solution.py:145
  339.7 14.8 %shard_map.181 = (bf16[192,1536]{1,0:T(8,128)(2,1)}, bf16[192,1536]{1,0:T(8,128)(2,1)}, bf16[192,1536]{1,0:T(8,128)(2,1)S(1)}, bf16[192,1536]{1,0:T(8,128)(2,1)S...) custom-call(bf16[2,1536,512]{2,1,0:T(8,128)(2,1)} %get-tuple-element.346.refs_15_.refs_, ...), custom_call_target="tpu_custom_call" | custom-call | flops 845571 | bytes 2673 | tf_op jit(solution)/shard_map/pallas_call | solution.py:145
  356.2 5.9 shard_map.182
  365.3 6.2 %collective-permute-done.44.refs_3_.refs_10_ = bf16[192,1536]{1,0:T(8,128)(2,1)S(1)} collective-permute-done((bf16[192,1536]{1,0:T(8,128)(2,1)}, bf16[192,1536]{1,0:T(8,128)(2,1)S(1)}, u32[]{:S(2)}, u32[]{:S(2)}) %collective-permute-start.44) | collective-permute-done | bytes 589856 | tf_op jit(solution)/shard_map/ppermute | solution.py:58
  372.7 10.7 %collective-permute-done.45.refs_4_.refs_11_ = bf16[192,1536]{1,0:T(8,128)(2,1)S(1)} collective-permute-done((bf16[192,1536]{1,0:T(8,128)(2,1)}, bf16[192,1536]{1,0:T(8,128)(2,1)S(1)}, u32[]{:S(2)}, u32[]{:S(2)}) %collective-permute-start.45) | collective-permute-done | bytes 589856 | tf_op jit(solution)/shard_map/ppermute | solution.py:58
  386.3 10.4 %collective-permute-done.46.refs_5_.refs_12_ = bf16[192,1536]{1,0:T(8,128)(2,1)S(1)} collective-permute-done((bf16[192,1536]{1,0:T(8,128)(2,1)S(1)}, bf16[192,1536]{1,0:T(8,128)(2,1)S(1)}, u32[]{:S(2)}, u32[]{:S(2)}) %collective-permute-start.46) | collective-permute-done | bytes 589856 | tf_op jit(solution)/shard_map/ppermute | solution.py:58
  400.0 11.6 %shard_map.183 = (bf16[2,4,384,192]{3,2,1,0:T(8,128)(2,1)}, f32[2,4,384,192]{3,2,1,0:T(8,128)}, f32[2,3,192]{2,1,0:T(4,128)S(1)}, f32[2,4,2,192]{3,2,1,0:T(2,128)S(1)}) custom-call(bf16[384,1536]{1,0:T(8,128)(2,1)} %get-tuple-element.395.refs_0_.refs_7_, bf16[192,1536]{1,0:T(8,128)(2,1)S(1)} %collective-permute-done.42.refs_1_.refs_8_, ...), custom_call_target="tpu_custom_call" | custom-call | flops 181193 | bytes 1911 | tf_op jit(solution)/shard_map/pallas_call | solution.py:145
  412.3 16.2 %collective-permute-start.50 = (f32[2,4,2,192]{3,2,1,0:T(2,128)S(1)}, f32[2,4,2,192]{3,2,1,0:T(2,128)S(1)}, u32[]{:S(2)}, u32[]{:S(2)}) collective-permute-start(f32[2,4,2,192]{3,2,1,0:T(2,128)S(1)} %get-tuple-element.413), channel_id=1, source_target_pairs={{0,1},{1,0},{2,3},{3,2},{4,5},{5,4},{6,7},{7,6},{8,9},{9,8},{10,11... | collective-permute-start | bytes 36872 | tf_op jit(solution)/shard_map/ppermute | solution.py:63
  432.8 8.8 %shard_map.184.refs_14_.refs_0_ = bf16[2,1536,768]{2,1,0:T(8,128)(2,1)} custom-call(bf16[2,4,384,192]{3,2,1,0:T(8,128)(2,1)S(1)} %copy-done.29, f32[2,4,384,192]{3,2,1,0:T(8,128)} %get-tuple-element.404.dv_ref, f32[2,4,2,192]{3,2,1,0:T(2,128)S(1)} %fusion.10.back_ref, f32[2,4,384,192]{3,2,1,0:T(8,128)} %get-tuple-element.415.b_ref, ...), custom_call_target="tpu_custom_call" | custom-call | bytes 1300 | tf_op jit(solution)/shard_map/pallas_call | solution.py:145
  441.7 17.2 %shard_map.185 = bf16[4,2,400,768]{3,2,1,0:T(8,128)(2,1)} custom-call(bf16[400,1536]{1,0:T(8,128)(2,1)} %pad_maximum_fusion.refs_0_, bf16[192,1536]{1,0:T(8,128)(2,1)S(1)} %copy-done.25, bf16[208,1536]{1,0:T(8,128)(2,1)} %copy-done.16, bf16[192,1536]{1,0:T(8,128)(2,1)S(1)} %copy-done.22, bf16[208,1536]{1,0:T(8,128)(2,1)} %copy-done.14, ...), custom_call_target="tpu_custom_call" | custom-call | flops 724775 | bytes 2064 | tf_op jit(solution)/shard_map/pallas_call | solution.py:145
  458.9 1.4 fusion.22
  465.6 1.9 collective-permute-start.58
  468.4 2.0 collective-permute-done.54.refs_2_
  471.3 11.8 %shard_map.186 = (bf16[192,1536]{1,0:T(8,128)(2,1)S(1)}, bf16[192,1536]{1,0:T(8,128)(2,1)S(1)}, bf16[192,1536]{1,0:T(8,128)(2,1)S(1)}, bf16[192,1536]{1,0:T(8,12...) custom-call(bf16[2,1536,768]{2,1,0:T(8,128)(2,1)} %shard_map.184.refs_14_.refs_, ...), custom_call_target="tpu_custom_call" | custom-call | flops 724775 | bytes 1435 | tf_op jit(solution)/shard_map/pallas_call | solution.py:145
  486.1 3.9 shard_map.187
  490.2 5.9 collective-permute-done.59
  496.1 1.5 collective-permute-done.60
  497.6 6.7 %collective-permute-done.61.refs_2_ = bf16[192,1536]{1,0:T(8,128)(2,1)S(1)} collective-permute-done((bf16[192,1536]{1,0:T(8,128)(2,1)S(1)}, bf16[192,1536]{1,0:T(8,128)(2,1)S(1)}, u32[]{:S(2)}, u32[]{:S(2)}) %collective-permute-start.61) | collective-permute-done | bytes 589856 | tf_op jit(solution)/shard_map/ppermute | solution.py:56
  504.3 2.0 collective-permute-done.62.refs_3_
  511.3 17.7 %collective-permute-start.71 = (bf16[384,1536]{1,0:T(8,128)(2,1)}, bf16[384,1536]{1,0:T(8,128)(2,1)S(1)}, u32[]{:S(2)}, u32[]{:S(2)}) collective-permute-start(bf16[384,1536]{1,0:T(8,128)(2,1)} %get-tuple-element.477), channel_id=1, source_target_pairs={{0,1},{1,0},{2,3},{3,2},{4,5},{5,4},{6,7},{7,6},{8,9},{9,8},{10,11... | collective-permute-start | bytes 3538952 | tf_op jit(solution)/shard_map/ppermute | solution.py:63
  534.6 4.9 collective-permute-done.70
  542.1 3.5 shard_map.188
  545.6 4.3 reshape.193
  551.8 5.8 shard_map.190
  557.6 10.5 %collective-permute-start.72 = (f32[384,1536]{1,0:T(8,128)}, f32[384,1536]{1,0:T(8,128)S(1)}, u32[]{:S(2)}, u32[]{:S(2)}) collective-permute-start(f32[384,1536]{1,0:T(8,128)} %get-tuple-element.486), channel_id=1, source_target_pairs={{0,1},{1,0},{2,3},{3,2},{4,5},{5,4},{6,7},{7,6},{8,9},{9,8},{10,11... | collective-permute-start | bytes 7077896 | tf_op jit(solution)/shard_map/ppermute | solution.py:63
  568.9 15.7 %collective-permute-start.74 = (f32[3,1,48]{2,1,0:T(1,128)S(1)}, f32[3,1,48]{2,1,0:T(1,128)S(1)}, u32[]{:S(2)}, u32[]{:S(2)}) collective-permute-start(f32[3,1,48]{2,1,0:T(1,128)S(1)} %reshape.195), channel_id=1, source_target_pairs={{0,0},{8,2},{16,4},{24,6},{2,8},{10,10},{18,12},{26,14},{4,16},{12... | collective-permute-start | bytes 1736 | tf_op jit(solution)/shard_map/ppermute | solution.py:948
  585.7 1.4 maximum_select_fusion.14
  587.1 1.5 fusion.7
  593.3 1.6 shard_map.191
  (403 shorter events, 107.2 us)
Async XLA Ops:
  7.2 91.0 %all-gather.9.cloned.1.call-start = ((), (), s32[]{:S(2)}) async-start(), calls=%async_computation.8 | async-start | bytes 5529600 | tf_op jit(solution)/shard_map/all_gather | solution.py:803
  8.0 17.1 %collective-permute-start.12 = (bf16[1,144]{1,0:T(2,128)(2,1)S(1)}, bf16[1,144]{1,0:T(2,128)(2,1)S(1)}, u32[]{:S(2)}, u32[]{:S(2)}) collective-permute-start(bf16[1,144]{1,0:T(2,128)(2,1)S(1)} %reshape.183), channel_id=1, source_target_pairs={{0,0},{2,8},{4,16},{6,24},{8,2},{10,10},{12,18},{14,26},{16,4},{18... | collective-permute-start | bytes 872 | tf_op jit(solution)/shard_map/ppermute | solution.py:798
  26.0 164.4 %all-gather.5.cloned.1.call-start = ((), (), s32[]{:S(2)}) async-start(), calls=%async_computation.3 | async-start | bytes 10616832 | tf_op jit(solution)/shard_map/all_gather | solution.py:803
  33.0 42.0 %collective-permute-start.3 = (bf16[208,1536]{1,0:T(8,128)(2,1)S(1)}, bf16[208,1536]{1,0:T(8,128)(2,1)S(1)}, u32[]{:S(2)}, u32[]{:S(2)}) collective-permute-start(bf16[208,1536]{1,0:T(8,128)(2,1)S(1)} %pad_maximum_fusion.4), channel_id=1, source_target_pairs={{0,4},{4,0},{1,5},{5,1},{2,6},{6,2},{3,7},{7,3},{8,12},{12,8},{9,1... | collective-permute-start | bytes 1916936 | tf_op jit(solution)/shard_map/ppermute | solution.py:58
  34.6 40.5 %collective-permute-start.1 = (bf16[208,1536]{1,0:T(8,128)(2,1)S(1)}, bf16[208,1536]{1,0:T(8,128)(2,1)S(1)}, u32[]{:S(2)}, u32[]{:S(2)}) collective-permute-start(bf16[208,1536]{1,0:T(8,128)(2,1)S(1)} %pad_maximum_fusion.4), channel_id=1, source_target_pairs={{0,2},{2,0},{1,3},{3,1},{4,6},{6,4},{5,7},{7,5},{8,10},{10,8},{9,1... | collective-permute-start | bytes 1916936 | tf_op jit(solution)/shard_map/ppermute | solution.py:56
  34.8 26.7 %collective-permute-start.5 = (bf16[96,1536]{1,0:T(8,128)(2,1)S(1)}, bf16[96,1536]{1,0:T(8,128)(2,1)S(1)}, u32[]{:S(2)}, u32[]{:S(2)}) collective-permute-start(bf16[96,1536]{1,0:T(8,128)(2,1)S(1)} %get-tuple-element.528), channel_id=1, source_target_pairs={{0,4},{4,0},{1,5},{5,1},{2,6},{6,2},{3,7},{7,3},{8,12},{12,8},{9,1... | collective-permute-start | bytes 884744 | tf_op jit(solution)/shard_map/ppermute | solution.py:58
  36.3 37.9 %collective-permute-start.2 = (bf16[192,1536]{1,0:T(8,128)(2,1)S(1)}, bf16[192,1536]{1,0:T(8,128)(2,1)S(1)}, u32[]{:S(2)}, u32[]{:S(2)}) collective-permute-start(bf16[192,1536]{1,0:T(8,128)(2,1)S(1)} %get-tuple-element.253), channel_id=1, source_target_pairs={{0,4},{4,0},{1,5},{5,1},{2,6},{6,2},{3,7},{7,3},{8,12},{12,8},{9,1... | collective-permute-start | bytes 1769480 | tf_op jit(solution)/shard_map/ppermute | solution.py:58
  39.7 35.4 %collective-permute-start = (bf16[192,1536]{1,0:T(8,128)(2,1)S(1)}, bf16[192,1536]{1,0:T(8,128)(2,1)S(1)}, u32[]{:S(2)}, u32[]{:S(2)}) collective-permute-start(bf16[192,1536]{1,0:T(8,128)(2,1)S(1)} %get-tuple-element.253), channel_id=1, source_target_pairs={{0,2},{2,0},{1,3},{3,1},{4,6},{6,4},{5,7},{7,5},{8,10},{10,8},{9,1... | collective-permute-start | bytes 1769480 | tf_op jit(solution)/shard_map/ppermute | solution.py:56
  61.5 12.7 %collective-permute-start.4 = (bf16[96,1536]{1,0:T(8,128)(2,1)S(1)}, bf16[96,1536]{1,0:T(8,128)(2,1)S(1)}, u32[]{:S(2)}, u32[]{:S(2)}) collective-permute-start(bf16[96,1536]{1,0:T(8,128)(2,1)S(1)} %get-tuple-element.529), channel_id=1, source_target_pairs={{0,2},{2,0},{1,3},{3,1},{4,6},{6,4},{5,7},{7,5},{8,10},{10,8},{9,1... | collective-permute-start | bytes 884744 | tf_op jit(solution)/shard_map/ppermute | solution.py:56
  77.6 191.5 %all-gather.7.cloned.1.call-start = ((), (), s32[]{:S(2)}) async-start(), calls=%async_computation.4 | async-start | bytes 7962624 | tf_op jit(solution)/shard_map/all_gather | solution.py:803
  78.2 16.2 %collective-permute-start.8 = (bf16[208,1536]{1,0:T(8,128)(2,1)S(1)}, bf16[208,1536]{1,0:T(8,128)(2,1)S(1)}, u32[]{:S(2)}, u32[]{:S(2)}) collective-permute-start(bf16[208,1536]{1,0:T(8,128)(2,1)S(1)} %collective-permute-done.3.refs_4_), channel_id=1, source_target_pairs={{0,2},{2,0},{1,3},{3,1},{4,6},{6,4},{5,7},{7,5},{8,10},{10,8},{9,1... | collective-permute-start | bytes 1916936 | tf_op jit(solution)/shard_map/ppermute | solution.py:56
  80.0 14.3 %collective-permute-start.7 = (bf16[192,1536]{1,0:T(8,128)(2,1)S(1)}, bf16[192,1536]{1,0:T(8,128)(2,1)}, u32[]{:S(2)}, u32[]{:S(2)}) collective-permute-start(bf16[192,1536]{1,0:T(8,128)(2,1)S(1)} %collective-permute-done.refs_1_), channel_id=1, source_target_pairs={{0,4},{4,0},{1,5},{5,1},{2,6},{6,2},{3,7},{7,3},{8,12},{12,8},{9,1... | collective-permute-start | bytes 1769480 | tf_op jit(solution)/shard_map/ppermute | solution.py:58
  95.1 23.9 %collective-permute-start.15 = (bf16[192,1536]{1,0:T(8,128)(2,1)}, bf16[192,1536]{1,0:T(8,128)(2,1)S(1)}, u32[]{:S(2)}, u32[]{:S(2)}) collective-permute-start(bf16[192,1536]{1,0:T(8,128)(2,1)} %get-tuple-element.272), channel_id=1, source_target_pairs={{0,4},{4,0},{1,5},{5,1},{2,6},{6,2},{3,7},{7,3},{8,12},{12,8},{9,1... | collective-permute-start | bytes 1769480 | tf_op jit(solution)/shard_map/ppermute | solution.py:58
  96.7 22.3 %collective-permute-start.13 = (bf16[192,1536]{1,0:T(8,128)(2,1)}, bf16[192,1536]{1,0:T(8,128)(2,1)S(1)}, u32[]{:S(2)}, u32[]{:S(2)}) collective-permute-start(bf16[192,1536]{1,0:T(8,128)(2,1)} %get-tuple-element.272), channel_id=1, source_target_pairs={{0,2},{2,0},{1,3},{3,1},{4,6},{6,4},{5,7},{7,5},{8,10},{10,8},{9,1... | collective-permute-start | bytes 1769480 | tf_op jit(solution)/shard_map/ppermute | solution.py:56
  96.8 24.8 %collective-permute-start.16 = (bf16[192,1536]{1,0:T(8,128)(2,1)}, bf16[192,1536]{1,0:T(8,128)(2,1)S(1)}, u32[]{:S(2)}, u32[]{:S(2)}) collective-permute-start(bf16[192,1536]{1,0:T(8,128)(2,1)} %get-tuple-element.273), channel_id=1, source_target_pairs={{0,4},{4,0},{1,5},{5,1},{2,6},{6,2},{3,7},{7,3},{8,12},{12,8},{9,1... | collective-permute-start | bytes 1769480 | tf_op jit(solution)/shard_map/ppermute | solution.py:58
  98.0 25.1 %collective-permute-start.14 = (bf16[192,1536]{1,0:T(8,128)(2,1)}, bf16[192,1536]{1,0:T(8,128)(2,1)S(1)}, u32[]{:S(2)}, u32[]{:S(2)}) collective-permute-start(bf16[192,1536]{1,0:T(8,128)(2,1)} %get-tuple-element.273), channel_id=1, source_target_pairs={{0,2},{2,0},{1,3},{3,1},{4,6},{6,4},{5,7},{7,5},{8,10},{10,8},{9,1... | collective-permute-start | bytes 1769480 | tf_op jit(solution)/shard_map/ppermute | solution.py:56
  126.2 12.6 %collective-permute-start.21 = (bf16[96,1152]{1,0:T(8,128)(2,1)S(1)}, bf16[96,1152]{1,0:T(8,128)(2,1)S(1)}, u32[]{:S(2)}, u32[]{:S(2)}) collective-permute-start(bf16[96,1152]{1,0:T(8,128)(2,1)S(1)} %get-tuple-element.547), channel_id=1, source_target_pairs={{0,6},{2,4},{4,2},{6,0},{1,7},{3,5},{5,3},{7,1},{8,14},{10,12},{12... | collective-permute-start | bytes 663560 | tf_op jit(solution)/shard_map/ppermute | solution.py:59
  127.3 12.1 %collective-permute-start.20 = (bf16[96,1152]{1,0:T(8,128)(2,1)S(1)}, bf16[96,1152]{1,0:T(8,128)(2,1)S(1)}, u32[]{:S(2)}, u32[]{:S(2)}) collective-permute-start(bf16[96,1152]{1,0:T(8,128)(2,1)S(1)} %get-tuple-element.548), channel_id=1, source_target_pairs={{0,4},{4,0},{1,5},{5,1},{2,6},{6,2},{3,7},{7,3},{8,12},{12,8},{9,1... | collective-permute-start | bytes 663560 | tf_op jit(solution)/shard_map/ppermute | solution.py:58
  127.6 11.8 %collective-permute-start.19 = (bf16[96,1152]{1,0:T(8,128)(2,1)S(1)}, bf16[96,1152]{1,0:T(8,128)(2,1)S(1)}, u32[]{:S(2)}, u32[]{:S(2)}) collective-permute-start(bf16[96,1152]{1,0:T(8,128)(2,1)S(1)} %get-tuple-element.549), channel_id=1, source_target_pairs={{0,2},{2,0},{1,3},{3,1},{4,6},{6,4},{5,7},{7,5},{8,10},{10,8},{9,1... | collective-permute-start | bytes 663560 | tf_op jit(solution)/shard_map/ppermute | solution.py:56
  141.8 242.6 %reduce-scatter.4.cloned.1.call-start = ((), (), s32[]{:S(2)}) async-start(), calls=%async_computation.5 | async-start | bytes 10616832 | tf_op jit(solution)/shard_map/reduce_scatter | solution.py:874
  142.0 13.6 %collective-permute-start.22 = (bf16[192,1536]{1,0:T(8,128)(2,1)}, bf16[192,1536]{1,0:T(8,128)(2,1)S(1)}, u32[]{:S(2)}, u32[]{:S(2)}) collective-permute-start(bf16[192,1536]{1,0:T(8,128)(2,1)} %copy-done.58), channel_id=1, source_target_pairs={{0,2},{2,0},{1,3},{3,1},{4,6},{6,4},{5,7},{7,5},{8,10},{10,8},{9,1... | collective-permute-start | bytes 1769480 | tf_op jit(solution)/shard_map/ppermute | solution.py:56
  142.2 13.5 %collective-permute-start.23 = (bf16[192,1536]{1,0:T(8,128)(2,1)}, bf16[192,1536]{1,0:T(8,128)(2,1)S(1)}, u32[]{:S(2)}, u32[]{:S(2)}) collective-permute-start(bf16[192,1536]{1,0:T(8,128)(2,1)} %copy-done.57), channel_id=1, source_target_pairs={{0,4},{4,0},{1,5},{5,1},{2,6},{6,2},{3,7},{7,3},{8,12},{12,8},{9,1... | collective-permute-start | bytes 1769480 | tf_op jit(solution)/shard_map/ppermute | solution.py:58
  143.3 24.9 %collective-permute-start.24 = (bf16[192,1536]{1,0:T(8,128)(2,1)}, bf16[192,1536]{1,0:T(8,128)(2,1)S(1)}, u32[]{:S(2)}, u32[]{:S(2)}) collective-permute-start(bf16[192,1536]{1,0:T(8,128)(2,1)} %copy-done.56), channel_id=1, source_target_pairs={{0,2},{2,0},{1,3},{3,1},{4,6},{6,4},{5,7},{7,5},{8,10},{10,8},{9,1... | collective-permute-start | bytes 1769480 | tf_op jit(solution)/shard_map/ppermute | solution.py:56
  143.6 24.6 %collective-permute-start.25 = (bf16[192,1536]{1,0:T(8,128)(2,1)}, bf16[192,1536]{1,0:T(8,128)(2,1)S(1)}, u32[]{:S(2)}, u32[]{:S(2)}) collective-permute-start(bf16[192,1536]{1,0:T(8,128)(2,1)} %copy-done.55), channel_id=1, source_target_pairs={{0,4},{4,0},{1,5},{5,1},{2,6},{6,2},{3,7},{7,3},{8,12},{12,8},{9,1... | collective-permute-start | bytes 1769480 | tf_op jit(solution)/shard_map/ppermute | solution.py:58
  169.5 12.4 %collective-permute-start.27 = (bf16[192,1536]{1,0:T(8,128)(2,1)S(1)}, bf16[192,1536]{1,0:T(8,128)(2,1)S(1)}, u32[]{:S(2)}, u32[]{:S(2)}) collective-permute-start(bf16[192,1536]{1,0:T(8,128)(2,1)S(1)} %add_convert_fusion.6), channel_id=1, source_target_pairs={{0,4},{4,0},{1,5},{5,1},{2,6},{6,2},{3,7},{7,3},{8,12},{12,8},{9,1... | collective-permute-start | bytes 1769480 | tf_op jit(solution)/shard_map/ppermute | solution.py:58
  170.0 11.9 %collective-permute-start.26 = (bf16[192,1536]{1,0:T(8,128)(2,1)S(1)}, bf16[192,1536]{1,0:T(8,128)(2,1)S(1)}, u32[]{:S(2)}, u32[]{:S(2)}) collective-permute-start(bf16[192,1536]{1,0:T(8,128)(2,1)S(1)} %add_convert_fusion.7), channel_id=1, source_target_pairs={{0,2},{2,0},{1,3},{3,1},{4,6},{6,4},{5,7},{7,5},{8,10},{10,8},{9,1... | collective-permute-start | bytes 1769480 | tf_op jit(solution)/shard_map/ppermute | solution.py:56
  187.5 12.4 %collective-permute-start.30 = (bf16[192,1536]{1,0:T(8,128)(2,1)}, bf16[192,1536]{1,0:T(8,128)(2,1)}, u32[]{:S(2)}, u32[]{:S(2)}) collective-permute-start(bf16[192,1536]{1,0:T(8,128)(2,1)} %get-tuple-element.315), channel_id=1, source_target_pairs={{0,4},{4,0},{1,5},{5,1},{2,6},{6,2},{3,7},{7,3},{8,12},{12,8},{9,1... | collective-permute-start | bytes 1769480 | tf_op jit(solution)/shard_map/ppermute | solution.py:58
  188.8 11.6 %collective-permute-start.28 = (bf16[192,1536]{1,0:T(8,128)(2,1)}, bf16[192,1536]{1,0:T(8,128)(2,1)}, u32[]{:S(2)}, u32[]{:S(2)}) collective-permute-start(bf16[192,1536]{1,0:T(8,128)(2,1)} %get-tuple-element.315), channel_id=1, source_target_pairs={{0,2},{2,0},{1,3},{3,1},{4,6},{6,4},{5,7},{7,5},{8,10},{10,8},{9,1... | collective-permute-start | bytes 1769480 | tf_op jit(solution)/shard_map/ppermute | solution.py:56
  189.9 22.0 %collective-permute-start.31 = (bf16[192,1536]{1,0:T(8,128)(2,1)}, bf16[192,1536]{1,0:T(8,128)(2,1)}, u32[]{:S(2)}, u32[]{:S(2)}) collective-permute-start(bf16[192,1536]{1,0:T(8,128)(2,1)} %get-tuple-element.316), channel_id=1, source_target_pairs={{0,4},{4,0},{1,5},{5,1},{2,6},{6,2},{3,7},{7,3},{8,12},{12,8},{9,1... | collective-permute-start | bytes 1769480 | tf_op jit(solution)/shard_map/ppermute | solution.py:58
  189.9 23.1 %collective-permute-start.29 = (bf16[192,1536]{1,0:T(8,128)(2,1)}, bf16[192,1536]{1,0:T(8,128)(2,1)}, u32[]{:S(2)}, u32[]{:S(2)}) collective-permute-start(bf16[192,1536]{1,0:T(8,128)(2,1)} %get-tuple-element.316), channel_id=1, source_target_pairs={{0,2},{2,0},{1,3},{3,1},{4,6},{6,4},{5,7},{7,5},{8,10},{10,8},{9,1... | collective-permute-start | bytes 1769480 | tf_op jit(solution)/shard_map/ppermute | solution.py:56
  213.0 19.9 %collective-permute-start.33 = (bf16[192,1536]{1,0:T(8,128)(2,1)}, bf16[192,1536]{1,0:T(8,128)(2,1)S(1)}, u32[]{:S(2)}, u32[]{:S(2)}) collective-permute-start(bf16[192,1536]{1,0:T(8,128)(2,1)} %collective-permute-done.31.refs_1_.refs_4_), channel_id=1, source_target_pairs={{0,2},{2,0},{1,3},{3,1},{4,6},{6,4},{5,7},{7,5},{8,10},{10,8},{9,1... | collective-permute-start | bytes 1769480 | tf_op jit(solution)/shard_map/ppermute | solution.py:56
  214.0 23.5 %collective-permute-start.35 = (bf16[192,1536]{1,0:T(8,128)(2,1)S(1)}, bf16[192,1536]{1,0:T(8,128)(2,1)S(1)}, u32[]{:S(2)}, u32[]{:S(2)}) collective-permute-start(bf16[192,1536]{1,0:T(8,128)(2,1)S(1)} %collective-permute-done.16.refs_3_.refs_11_), channel_id=1, source_target_pairs={{0,2},{2,0},{1,3},{3,1},{4,6},{6,4},{5,7},{7,5},{8,10},{10,8},{9,1... | collective-permute-start | bytes 1769480 | tf_op jit(solution)/shard_map/ppermute | solution.py:56
  214.5 23.0 %collective-permute-start.32 = (bf16[192,1536]{1,0:T(8,128)(2,1)}, bf16[192,1536]{1,0:T(8,128)(2,1)S(1)}, u32[]{:S(2)}, u32[]{:S(2)}) collective-permute-start(bf16[192,1536]{1,0:T(8,128)(2,1)} %collective-permute-done.28.refs_0_.refs_1_), channel_id=1, source_target_pairs={{0,4},{4,0},{1,5},{5,1},{2,6},{6,2},{3,7},{7,3},{8,12},{12,8},{9,1... | collective-permute-start | bytes 1769480 | tf_op jit(solution)/shard_map/ppermute | solution.py:58
  214.8 22.7 %collective-permute-start.34 = (bf16[192,1536]{1,0:T(8,128)(2,1)S(1)}, bf16[192,1536]{1,0:T(8,128)(2,1)S(1)}, u32[]{:S(2)}, u32[]{:S(2)}) collective-permute-start(bf16[192,1536]{1,0:T(8,128)(2,1)S(1)} %collective-permute-done.13.refs_2_.refs_8_), channel_id=1, source_target_pairs={{0,4},{4,0},{1,5},{5,1},{2,6},{6,2},{3,7},{7,3},{8,12},{12,8},{9,1... | collective-permute-start | bytes 1769480 | tf_op jit(solution)/shard_map/ppermute | solution.py:58
  268.9 190.0 %reduce-scatter.6.cloned.1.call-start = ((), (), s32[]{:S(2)}) async-start(), calls=%async_computation.6 | async-start | bytes 7962624 | tf_op jit(solution)/shard_map/reduce_scatter | solution.py:874
  313.2 22.7 %collective-permute-start.36 = (bf16[192,1536]{1,0:T(8,128)(2,1)S(1)}, bf16[192,1536]{1,0:T(8,128)(2,1)S(1)}, u32[]{:S(2)}, u32[]{:S(2)}) collective-permute-start(bf16[192,1536]{1,0:T(8,128)(2,1)S(1)} %get-tuple-element.349), channel_id=1, source_target_pairs={{0,2},{2,0},{1,3},{3,1},{4,6},{6,4},{5,7},{7,5},{8,10},{10,8},{9,1... | collective-permute-start | bytes 1769480 | tf_op jit(solution)/shard_map/ppermute | solution.py:56
  314.1 21.8 %collective-permute-start.37 = (bf16[192,1536]{1,0:T(8,128)(2,1)S(1)}, bf16[192,1536]{1,0:T(8,128)(2,1)S(1)}, u32[]{:S(2)}, u32[]{:S(2)}) collective-permute-start(bf16[192,1536]{1,0:T(8,128)(2,1)S(1)} %get-tuple-element.350), channel_id=1, source_target_pairs={{0,4},{4,0},{1,5},{5,1},{2,6},{6,2},{3,7},{7,3},{8,12},{12,8},{9,1... | collective-permute-start | bytes 1769480 | tf_op jit(solution)/shard_map/ppermute | solution.py:58
  314.4 21.9 %collective-permute-start.38 = (bf16[192,1536]{1,0:T(8,128)(2,1)S(1)}, bf16[192,1536]{1,0:T(8,128)(2,1)S(1)}, u32[]{:S(2)}, u32[]{:S(2)}) collective-permute-start(bf16[192,1536]{1,0:T(8,128)(2,1)S(1)} %get-tuple-element.351), channel_id=1, source_target_pairs={{0,2},{2,0},{1,3},{3,1},{4,6},{6,4},{5,7},{7,5},{8,10},{10,8},{9,1... | collective-permute-start | bytes 1769480 | tf_op jit(solution)/shard_map/ppermute | solution.py:56
  315.0 21.8 %collective-permute-start.39 = (bf16[192,1536]{1,0:T(8,128)(2,1)S(1)}, bf16[192,1536]{1,0:T(8,128)(2,1)S(1)}, u32[]{:S(2)}, u32[]{:S(2)}) collective-permute-start(bf16[192,1536]{1,0:T(8,128)(2,1)S(1)} %get-tuple-element.352), channel_id=1, source_target_pairs={{0,4},{4,0},{1,5},{5,1},{2,6},{6,2},{3,7},{7,3},{8,12},{12,8},{9,1... | collective-permute-start | bytes 1769480 | tf_op jit(solution)/shard_map/ppermute | solution.py:58
  337.0 192.0 %reduce-scatter.8.cloned.1.call-start = ((), (), s32[]{:S(2)}) async-start(), calls=%async_computation.7 | async-start | bytes 5529600 | tf_op jit(solution)/shard_map/reduce_scatter | solution.py:874
  338.3 17.8 %collective-permute-start.41 = (bf16[192,1536]{1,0:T(8,128)(2,1)S(1)}, bf16[192,1536]{1,0:T(8,128)(2,1)S(1)}, u32[]{:S(2)}, u32[]{:S(2)}) collective-permute-start(bf16[192,1536]{1,0:T(8,128)(2,1)S(1)} %add_convert_fusion.4), channel_id=1, source_target_pairs={{0,4},{4,0},{1,5},{5,1},{2,6},{6,2},{3,7},{7,3},{8,12},{12,8},{9,1... | collective-permute-start | bytes 1769480 | tf_op jit(solution)/shard_map/ppermute | solution.py:58
  338.9 17.3 %collective-permute-start.40 = (bf16[192,1536]{1,0:T(8,128)(2,1)S(1)}, bf16[192,1536]{1,0:T(8,128)(2,1)S(1)}, u32[]{:S(2)}, u32[]{:S(2)}) collective-permute-start(bf16[192,1536]{1,0:T(8,128)(2,1)S(1)} %add_convert_fusion.5), channel_id=1, source_target_pairs={{0,2},{2,0},{1,3},{3,1},{4,6},{6,4},{5,7},{7,5},{8,10},{10,8},{9,1... | collective-permute-start | bytes 1769480 | tf_op jit(solution)/shard_map/ppermute | solution.py:56
  363.8 19.5 %collective-permute-start.45 = (bf16[192,1536]{1,0:T(8,128)(2,1)}, bf16[192,1536]{1,0:T(8,128)(2,1)S(1)}, u32[]{:S(2)}, u32[]{:S(2)}) collective-permute-start(bf16[192,1536]{1,0:T(8,128)(2,1)} %get-tuple-element.390), channel_id=1, source_target_pairs={{0,4},{4,0},{1,5},{5,1},{2,6},{6,2},{3,7},{7,3},{8,12},{12,8},{9,1... | collective-permute-start | bytes 1769480 | tf_op jit(solution)/shard_map/ppermute | solution.py:58
  364.1 20.2 %collective-permute-start.43 = (bf16[192,1536]{1,0:T(8,128)(2,1)}, bf16[192,1536]{1,0:T(8,128)(2,1)S(1)}, u32[]{:S(2)}, u32[]{:S(2)}) collective-permute-start(bf16[192,1536]{1,0:T(8,128)(2,1)} %get-tuple-element.390), channel_id=1, source_target_pairs={{0,2},{2,0},{1,3},{3,1},{4,6},{6,4},{5,7},{7,5},{8,10},{10,8},{9,1... | collective-permute-start | bytes 1769480 | tf_op jit(solution)/shard_map/ppermute | solution.py:56
  384.4 12.4 %collective-permute-start.46 = (bf16[192,1536]{1,0:T(8,128)(2,1)S(1)}, bf16[192,1536]{1,0:T(8,128)(2,1)S(1)}, u32[]{:S(2)}, u32[]{:S(2)}) collective-permute-start(bf16[192,1536]{1,0:T(8,128)(2,1)S(1)} %collective-permute-done.42.refs_1_.refs_8_), channel_id=1, source_target_pairs={{0,4},{4,0},{1,5},{5,1},{2,6},{6,2},{3,7},{7,3},{8,12},{12,8},{9,1... | collective-permute-start | bytes 1769480 | tf_op jit(solution)/shard_map/ppermute | solution.py:58
  384.7 13.3 %collective-permute-start.47 = (bf16[192,1536]{1,0:T(8,128)(2,1)S(1)}, bf16[192,1536]{1,0:T(8,128)(2,1)S(1)}, u32[]{:S(2)}, u32[]{:S(2)}) collective-permute-start(bf16[192,1536]{1,0:T(8,128)(2,1)S(1)} %collective-permute-done.45.refs_4_.refs_11_), channel_id=1, source_target_pairs={{0,2},{2,0},{1,3},{3,1},{4,6},{6,4},{5,7},{7,5},{8,10},{10,8},{9,1... | collective-permute-start | bytes 1769480 | tf_op jit(solution)/shard_map/ppermute | solution.py:56
  398.0 14.3 %collective-permute-start.48 = (bf16[192,1536]{1,0:T(8,128)(2,1)}, bf16[192,1536]{1,0:T(8,128)(2,1)}, u32[]{:S(2)}, u32[]{:S(2)}) collective-permute-start(bf16[192,1536]{1,0:T(8,128)(2,1)} %get-tuple-element.406), channel_id=1, source_target_pairs={{0,2},{2,0},{1,3},{3,1},{4,6},{6,4},{5,7},{7,5},{8,10},{10,8},{9,1... | collective-permute-start | bytes 1769480 | tf_op jit(solution)/shard_map/ppermute | solution.py:56
  398.5 13.9 %collective-permute-start.49 = (bf16[192,1536]{1,0:T(8,128)(2,1)}, bf16[192,1536]{1,0:T(8,128)(2,1)}, u32[]{:S(2)}, u32[]{:S(2)}) collective-permute-start(bf16[192,1536]{1,0:T(8,128)(2,1)} %get-tuple-element.407), channel_id=1, source_target_pairs={{0,4},{4,0},{1,5},{5,1},{2,6},{6,2},{3,7},{7,3},{8,12},{12,8},{9,1... | collective-permute-start | bytes 1769480 | tf_op jit(solution)/shard_map/ppermute | solution.py:58
  412.3 20.3 %collective-permute-start.50 = (f32[2,4,2,192]{3,2,1,0:T(2,128)S(1)}, f32[2,4,2,192]{3,2,1,0:T(2,128)S(1)}, u32[]{:S(2)}, u32[]{:S(2)}) collective-permute-start(f32[2,4,2,192]{3,2,1,0:T(2,128)S(1)} %get-tuple-element.413), channel_id=1, source_target_pairs={{0,1},{1,0},{2,3},{3,2},{4,5},{5,4},{6,7},{7,6},{8,9},{9,8},{10,11... | collective-permute-start | bytes 36872 | tf_op jit(solution)/shard_map/ppermute | solution.py:63
  464.9 18.2 %collective-permute-start.56 = (bf16[96,1536]{1,0:T(8,128)(2,1)S(1)}, bf16[96,1536]{1,0:T(8,128)(2,1)S(1)}, u32[]{:S(2)}, u32[]{:S(2)}) collective-permute-start(bf16[96,1536]{1,0:T(8,128)(2,1)S(1)} %copy-done.72), channel_id=1, source_target_pairs={{0,2},{2,0},{1,3},{3,1},{4,6},{6,4},{5,7},{7,5},{8,10},{10,8},{9,1... | collective-permute-start | bytes 884744 | tf_op jit(solution)/shard_map/ppermute | solution.py:56
  465.5 17.6 %collective-permute-start.57 = (bf16[96,1536]{1,0:T(8,128)(2,1)S(1)}, bf16[96,1536]{1,0:T(8,128)(2,1)S(1)}, u32[]{:S(2)}, u32[]{:S(2)}) collective-permute-start(bf16[96,1536]{1,0:T(8,128)(2,1)S(1)} %copy-done.71), channel_id=1, source_target_pairs={{0,4},{4,0},{1,5},{5,1},{2,6},{6,2},{3,7},{7,3},{8,12},{12,8},{9,1... | collective-permute-start | bytes 884744 | tf_op jit(solution)/shard_map/ppermute | solution.py:58
  465.6 17.5 %collective-permute-start.58 = (bf16[96,1536]{1,0:T(8,128)(2,1)S(1)}, bf16[96,1536]{1,0:T(8,128)(2,1)S(1)}, u32[]{:S(2)}, u32[]{:S(2)}) collective-permute-start(bf16[96,1536]{1,0:T(8,128)(2,1)S(1)} %copy-done.70), channel_id=1, source_target_pairs={{0,6},{2,4},{4,2},{6,0},{1,7},{3,5},{5,3},{7,1},{8,14},{10,12},{12... | collective-permute-start | bytes 884744 | tf_op jit(solution)/shard_map/ppermute | solution.py:59
  483.1 13.0 %collective-permute-start.59 = (bf16[192,1536]{1,0:T(8,128)(2,1)S(1)}, bf16[192,1536]{1,0:T(8,128)(2,1)S(1)}, u32[]{:S(2)}, u32[]{:S(2)}) collective-permute-start(bf16[192,1536]{1,0:T(8,128)(2,1)S(1)} %get-tuple-element.440), channel_id=1, source_target_pairs={{0,2},{2,0},{1,3},{3,1},{4,6},{6,4},{5,7},{7,5},{8,10},{10,8},{9,1... | collective-permute-start | bytes 1769480 | tf_op jit(solution)/shard_map/ppermute | solution.py:56
  483.8 13.8 %collective-permute-start.60 = (bf16[192,1536]{1,0:T(8,128)(2,1)S(1)}, bf16[192,1536]{1,0:T(8,128)(2,1)S(1)}, u32[]{:S(2)}, u32[]{:S(2)}) collective-permute-start(bf16[192,1536]{1,0:T(8,128)(2,1)S(1)} %get-tuple-element.441), channel_id=1, source_target_pairs={{0,4},{4,0},{1,5},{5,1},{2,6},{6,2},{3,7},{7,3},{8,12},{12,8},{9,1... | collective-permute-start | bytes 1769480 | tf_op jit(solution)/shard_map/ppermute | solution.py:58
  485.2 19.2 %collective-permute-start.61 = (bf16[192,1536]{1,0:T(8,128)(2,1)S(1)}, bf16[192,1536]{1,0:T(8,128)(2,1)S(1)}, u32[]{:S(2)}, u32[]{:S(2)}) collective-permute-start(bf16[192,1536]{1,0:T(8,128)(2,1)S(1)} %get-tuple-element.442), channel_id=1, source_target_pairs={{0,2},{2,0},{1,3},{3,1},{4,6},{6,4},{5,7},{7,5},{8,10},{10,8},{9,1... | collective-permute-start | bytes 1769480 | tf_op jit(solution)/shard_map/ppermute | solution.py:56
  486.0 20.3 %collective-permute-start.62 = (bf16[192,1536]{1,0:T(8,128)(2,1)S(1)}, bf16[192,1536]{1,0:T(8,128)(2,1)S(1)}, u32[]{:S(2)}, u32[]{:S(2)}) collective-permute-start(bf16[192,1536]{1,0:T(8,128)(2,1)S(1)} %get-tuple-element.443), channel_id=1, source_target_pairs={{0,4},{4,0},{1,5},{5,1},{2,6},{6,2},{3,7},{7,3},{8,12},{12,8},{9,1... | collective-permute-start | bytes 1769480 | tf_op jit(solution)/shard_map/ppermute | solution.py:58
  507.4 43.6 %collective-permute-start.64 = (bf16[192,1536]{1,0:T(8,128)(2,1)}, bf16[192,1536]{1,0:T(8,128)(2,1)}, u32[]{:S(2)}, u32[]{:S(2)}) collective-permute-start(bf16[192,1536]{1,0:T(8,128)(2,1)} %add_convert_fusion), channel_id=1, source_target_pairs={{0,4},{4,0},{1,5},{5,1},{2,6},{6,2},{3,7},{7,3},{8,12},{12,8},{9,1... | collective-permute-start | bytes 1769480 | tf_op jit(solution)/shard_map/ppermute | solution.py:58
  509.2 41.8 %collective-permute-start.63 = (bf16[192,1536]{1,0:T(8,128)(2,1)}, bf16[192,1536]{1,0:T(8,128)(2,1)}, u32[]{:S(2)}, u32[]{:S(2)}) collective-permute-start(bf16[192,1536]{1,0:T(8,128)(2,1)} %add_convert_fusion.1), channel_id=1, source_target_pairs={{0,2},{2,0},{1,3},{3,1},{4,6},{6,4},{5,7},{7,5},{8,10},{10,8},{9,1... | collective-permute-start | bytes 1769480 | tf_op jit(solution)/shard_map/ppermute | solution.py:56
  509.5 21.1 %collective-permute-start.68 = (bf16[96,1152]{1,0:T(8,128)(2,1)}, bf16[96,1152]{1,0:T(8,128)(2,1)S(1)}, u32[]{:S(2)}, u32[]{:S(2)}) collective-permute-start(bf16[96,1152]{1,0:T(8,128)(2,1)} %get-tuple-element.470), channel_id=1, source_target_pairs={{0,2},{2,0},{1,3},{3,1},{4,6},{6,4},{5,7},{7,5},{8,10},{10,8},{9,1... | collective-permute-start | bytes 663560 | tf_op jit(solution)/shard_map/ppermute | solution.py:56
  510.6 22.7 %collective-permute-start.69 = (bf16[96,1152]{1,0:T(8,128)(2,1)}, bf16[96,1152]{1,0:T(8,128)(2,1)}, u32[]{:S(2)}, u32[]{:S(2)}) collective-permute-start(bf16[96,1152]{1,0:T(8,128)(2,1)} %get-tuple-element.471), channel_id=1, source_target_pairs={{0,4},{4,0},{1,5},{5,1},{2,6},{6,2},{3,7},{7,3},{8,12},{12,8},{9,1... | collective-permute-start | bytes 663560 | tf_op jit(solution)/shard_map/ppermute | solution.py:58
  511.3 28.9 %collective-permute-start.71 = (bf16[384,1536]{1,0:T(8,128)(2,1)}, bf16[384,1536]{1,0:T(8,128)(2,1)S(1)}, u32[]{:S(2)}, u32[]{:S(2)}) collective-permute-start(bf16[384,1536]{1,0:T(8,128)(2,1)} %get-tuple-element.477), channel_id=1, source_target_pairs={{0,1},{1,0},{2,3},{3,2},{4,5},{5,4},{6,7},{7,6},{8,9},{9,8},{10,11... | collective-permute-start | bytes 3538952 | tf_op jit(solution)/shard_map/ppermute | solution.py:63
  533.4 17.6 %collective-permute-start.67 = (bf16[96,768]{1,0:T(8,128)(2,1)}, bf16[96,768]{1,0:T(8,128)(2,1)}, u32[]{:S(2)}, u32[]{:S(2)}) collective-permute-start(bf16[96,768]{1,0:T(8,128)(2,1)} %get-tuple-element.557), channel_id=1, source_target_pairs={{0,6},{2,4},{4,2},{6,0},{1,7},{3,5},{5,3},{7,1},{8,14},{10,12},{12... | collective-permute-start | bytes 442376 | tf_op jit(solution)/shard_map/ppermute | solution.py:59
  557.6 35.8 %collective-permute-start.72 = (f32[384,1536]{1,0:T(8,128)}, f32[384,1536]{1,0:T(8,128)S(1)}, u32[]{:S(2)}, u32[]{:S(2)}) collective-permute-start(f32[384,1536]{1,0:T(8,128)} %get-tuple-element.486), channel_id=1, source_target_pairs={{0,1},{1,0},{2,3},{3,2},{4,5},{5,4},{6,7},{7,6},{8,9},{9,8},{10,11... | collective-permute-start | bytes 7077896 | tf_op jit(solution)/shard_map/ppermute | solution.py:63
  568.9 16.7 %collective-permute-start.74 = (f32[3,1,48]{2,1,0:T(1,128)S(1)}, f32[3,1,48]{2,1,0:T(1,128)S(1)}, u32[]{:S(2)}, u32[]{:S(2)}) collective-permute-start(f32[3,1,48]{2,1,0:T(1,128)S(1)} %reshape.195), channel_id=1, source_target_pairs={{0,0},{8,2},{16,4},{24,6},{2,8},{10,10},{18,12},{26,14},{4,16},{12... | collective-permute-start | bytes 1736 | tf_op jit(solution)/shard_map/ppermute | solution.py:948
  (97 other events, 861.5 us)
Sparse Core Ops, SparseCore 0:
  26.1 51.9 all-gather.8
  80.4 89.2 all-gather.4
  171.9 69.7 all-gather.6
  269.0 109.1 reduce-scatter.3
  380.4 75.5 reduce-scatter.5
  459.0 65.9 reduce-scatter.7

commit v4 on v3

--- a/solution.py
+++ b/solution.py
@@ -197,51 +197,89 @@
     def body(*refs):
         hat_refs, pack_ref = refs[:BLOCKS], refs[BLOCKS]
         b_ref, c_ref, x_ref, u_ref, keep_ref, taps_ref, tails_ref, gate_ref = refs[BLOCKS + 1 :]
-        for segment, place in enumerate((0, 2, 4, 6)):
-            below = hat_refs[place].shape[0] - 16
-            begins = hat_refs[place][below:, :seg].astype(f32)[0:1]
-            begins = jnp.transpose(jnp.broadcast_to(begins, (LANES, seg)))
-            before = jnp.where(rows_of((seg, LANES)) == 0, 0.0, pltpu.roll(begins, 1, 0))
-            keep_one = (1.0 - begins)[:, :1]
-            keep_ref[0, segment] = keep_one
-            keep_ref[1, segment] = ((1.0 - begins) * (1.0 - before))[:, :1]
-            gate_ref[segment, 0:1] = keep_one[seg - 1 :]
-            gate_ref[segment, 1:2] = jnp.ones((1, 1), f32)
-        for half in range(2):
-            weights = pack_ref[:, half, :rows, :].reshape(width, cols)
-            for plane in range(planes):
-                row = pack_ref[plane, half, rows:, :].astype(f32)[0:1]
-                for k in range(3):
-                    at = pl.ds(plane * tap_len, tap_len)
-                    taps_ref[half, k : k + 1, at] = row[:, k * tap_len : (k + 1) * tap_len]
-            for place, segment, low, count in spans(seg):
-                proj = nn(hat_refs[place][:count, :], weights)
-                b_val, c_val, x_val = (
-                    proj[:, :chan],
-                    proj[:, chan : 2 * chan],
-                    proj[:, 3 * chan :],
-                )
-                at = (half, segment, pl.ds(low, count))
-                b_ref[at] = b_val
-                c_ref[at] = c_val
-                x_ref[at] = x_val
-                u_val = b_val * x_val
-                u_ref[at] = u_val.astype(bf16)
-                if low + count == seg:
-                    last = u_val[count - 2 :].astype(bf16).astype(f32) * gate_ref[segment]
-                    tails_ref[half, segment] = last.astype(bf16)
+
+        @pl.when(pl.program_id(0) == 0)
+        def _():
+            for segment, place in enumerate((0, 2, 4, 6)):
+                below = hat_refs[place].shape[0] - 16
+                begins = hat_refs[place][below:, :seg].astype(f32)[0:1]
+                begins = jnp.transpose(jnp.broadcast_to(begins, (LANES, seg)))
+                before = jnp.where(rows_of((seg, LANES)) == 0, 0.0, pltpu.roll(begins, 1, 0))
+                keep_one = (1.0 - begins)[:, :1]
+                keep_ref[0, segment] = keep_one
+                keep_ref[1, segment] = ((1.0 - begins) * (1.0 - before))[:, :1]
+                gate_ref[segment, 0:1] = keep_one[seg - 1 :]
+                gate_ref[segment, 1:2] = jnp.ones((1, 1), f32)
+
+        weights = pack_ref[:, 0, :rows, :].reshape(width, cols)
+        for plane in range(planes):
+            row = pack_ref[plane, 0, rows:, :].astype(f32)[0:1]
+            for k in range(3):
+                at = pl.ds(plane * tap_len, tap_len)
+                taps_ref[0, k : k + 1, at] = row[:, k * tap_len : (k + 1) * tap_len]
+        for place, segment, low, count in spans(seg):
+            proj = nn(hat_refs[place][:count, :], weights)
+            b_val, c_val, x_val = proj[:, :chan], proj[:, chan : 2 * chan], proj[:, 3 * chan :]
+            at = (0, segment, pl.ds(low, count))
+            b_ref[at] = b_val
+            c_ref[at] = c_val
+            x_ref[at] = x_val
+            u_val = b_val * x_val
+            u_ref[at] = u_val.astype(bf16)
+            if low + count == seg:
+                last = u_val[count - 2 :].astype(bf16).astype(f32) * gate_ref[segment]
+                tails_ref[0, segment] = last.astype(bf16)
 
     shape = (2, 4, seg, chan)
+    shapes = [out(shape, f32)] * 3 + [out(shape, bf16), out((2, 4, seg, 1), f32)]
+    shapes += [out((2, 3, chan), f32), out((2, 4, 2, chan), bf16), out((4, 2, 1), f32)]
+
+    def of_half(value):
+        rest = value.shape[1:]
+        return pl.BlockSpec((1,) + rest, lambda h: (h,) + (0,) * len(rest))
+
+    def fixed(value):
+        zeros = (0,) * len(value.shape)
+        return pl.BlockSpec(value.shape, lambda h: zeros)
+
     results = call(
         body,
-        [out(shape, f32)] * 3
-        + [out(shape, bf16), out((2, 4, seg, 1), f32), out((2, 3, chan), f32)]
-        + [out((2, 4, 2, chan), bf16), out((4, 2, 1), f32)],
+        shapes,
         *hats,
         pack,
+        grid=(2,),
+        in_specs=[fixed(v) for v in hats]
+        + [pl.BlockSpec((planes, 1, rows_taps, cols), lambda h: (0, h, 0, 0))],
+        out_specs=[of_half(v) for v in shapes[:4]]
+        + [fixed(shapes[4]), of_half(shapes[5]), of_half(shapes[6]), fixed(shapes[7])],
         flops=2 * 4 * seg * width * cols * 2,
     )
     return results[:4], results[4:]
+
+
+def by_segment(value):
+    rest = value.shape[2:]
+    return pl.BlockSpec((value.shape[0], 1) + rest, lambda s: (0, s) + (0,) * len(rest))
+
+
+def every_step(value):
+    zeros = (0,) * len(value.shape)
+    return pl.BlockSpec(value.shape, lambda s: zeros)
+
+
+def out_columns(pack):
+    chan = pack.shape[3] // 4
+    first, count = 2 * chan // LANES, -(-chan // LANES)
+    block = pack.shape[:3] + (LANES,)
+    return [
+        pl.BlockSpec(block, functools.partial(lambda c, s: (0, 0, 0, c), first + k))
+        for k in range(count)
+    ]
+
+
+def out_matrix(refs, half, rows, chan):
+    parts = [ref[:, half, :rows, :].reshape(-1, LANES) for ref in refs]
+    return jnp.concatenate(parts, axis=1)[:, :chan]
 
 
 def rows_of(shape):
@@ -260,35 +298,44 @@
     rows, chan = rows_taps - 16, cols // 4
     width = planes * rows
 
-    def body(u_ref, halo_ref, c_ref, keep_ref, taps_ref, pack_ref, v_ref, y_ref, *split):
-        outs = [
-            pack_ref[:, half, :rows, 2 * chan : 3 * chan].reshape(width, chan) for half in range(2)
-        ]
+    columns = out_columns(pack)
+
+    def body(u_ref, halo_ref, c_ref, keep_ref, taps_ref, *refs):
+        pack_refs, (v_ref, y_ref, *split) = refs[: len(columns)], refs[len(columns) :]
+        keep_one, keep_two = keep_ref[0, 0], keep_ref[1, 0]
+        total = None
+        for half in range(2):
+            u_val = u_ref[half, 0].astype(f32)
+            one, two = earlier_rows(u_val, halo_ref[half, 0])
+            tap = taps_ref[half]
+            v_val = tap[0:1] * u_val + tap[1:2] * keep_one * one + tap[2:3] * keep_two * two
+            y_val = (c_ref[half, 0] * v_val).astype(bf16)
+            v_ref[half, 0] = v_val
+            y_ref[half, 0] = y_val
+            term = nt(y_val, out_matrix(pack_refs, half, rows, chan))
+            total = term if total is None else total + term
         for segment in range(4):
-            keep_one, keep_two = keep_ref[0, segment], keep_ref[1, segment]
-            total = None
-            for half in range(2):
-                u_val = u_ref[half, segment].astype(f32)
-                one, two = earlier_rows(u_val, halo_ref[half, segment])
-                tap = taps_ref[half]
-                v_val = tap[0:1] * u_val + tap[1:2] * keep_one * one + tap[2:3] * keep_two * two
-                y_val = (c_ref[half, segment] * v_val).astype(bf16)
-                v_ref[half, segment] = v_val
-                y_ref[half, segment] = y_val
-                term = nt(y_val, outs[half])
-                total = term if total is None else total + term
-            split_store(split, segment, total)
+
+            @pl.when(pl.program_id(0) == segment)
+            def _(segment=segment):
+                split_store(split, segment, total)
 
     shape = (2, 4, seg, chan)
+    shapes = [out(shape, f32), out(shape, bf16)] + split_shapes(seg, width)
     results = call(
         body,
-        [out(shape, f32), out(shape, bf16)] + split_shapes(seg, width),
+        shapes,
         u_vals,
         halo,
         c_part,
         keeps,
         taps,
-        pack,
+        *[pack] * len(columns),
+        grid=(4,),
+        in_specs=[by_segment(v) for v in (u_vals, halo, c_part, keeps)]
+        + [every_step(taps)]
+        + columns,
+        out_specs=[by_segment(v) for v in shapes[:2]] + [every_step(v) for v in shapes[2:]],
         flops=2 * 4 * seg * width * 2 * chan,
     )
     return results[0], results[1], results[2:]
@@ -299,36 +346,46 @@
     rows, chan = rows_taps - 16, cols // 4
     width = planes * rows
 
+    columns = out_columns(pack)
+
     def body(*refs):
         mix_refs, refs = refs[:BLOCKS], refs[BLOCKS:]
-        u_ref, halo_ref, c_ref, v_ref, keep_ref, taps_ref, pack_ref = refs[:7]
-        dc_ref, dv_ref, sums_ref, heads_ref = refs[7:]
+        u_ref, halo_ref, c_ref, v_ref, keep_ref, taps_ref, *refs = refs
+        pack_refs, refs = refs[: len(columns)], refs[len(columns) :]
+        dc_ref, dv_ref, sums_ref, heads_ref = refs
+        keep_one, keep_two = keep_ref[0, 0], keep_ref[1, 0]
+
+        @pl.when(pl.program_id(0) == 0)
+        def _():
+            sums_ref[...] = jnp.zeros_like(sums_ref)
+
         for half in range(2):
-            outs = pack_ref[:, half, :rows, 2 * chan : 3 * chan].reshape(width, chan)
+            outs = out_matrix(pack_refs, half, rows, chan)
             for place, segment, low, count in spans(seg):
-                at = (half, segment, pl.ds(low, count))
-                grad_y = nn(mix_refs[place][:count, :], outs)
-                dc_ref[at] = (grad_y * v_ref[at]).astype(bf16)
-                dv_ref[at] = grad_y * c_ref[at]
-            sums = [jnp.zeros((1, chan), f32)] * 3
+
+                @pl.when(pl.program_id(0) == segment)
+                def _(place=place, low=low, count=count):
+                    at = (half, 0, pl.ds(low, count))
+                    grad_y = nn(mix_refs[place][:count, :], outs)
+                    dc_ref[at] = (grad_y * v_ref[at]).astype(bf16)
+                    dv_ref[at] = grad_y * c_ref[at]
+
             tap = taps_ref[half]
-            for segment in range(4):
-                keep_one, keep_two = keep_ref[0, segment], keep_ref[1, segment]
-                u_val = u_ref[half, segment].astype(f32)
-                one, two = earlier_rows(u_val, halo_ref[half, segment])
-                grad_v = dv_ref[half, segment]
-                once, twice = keep_one * grad_v, keep_two * grad_v
-                for k, term in enumerate((grad_v * u_val, once * one, twice * two)):
-                    sums[k] = sums[k] + jnp.sum(term, axis=0, keepdims=True)
-                heads_ref[half, segment, 0:1] = tap[2:3] * twice[0:1]
-                heads_ref[half, segment, 1:2] = tap[1:2] * once[0:1] + tap[2:3] * twice[1:2]
-            for k in range(3):
-                sums_ref[half, k : k + 1] = sums[k]
+            u_val = u_ref[half, 0].astype(f32)
+            one, two = earlier_rows(u_val, halo_ref[half, 0])
+            grad_v = dv_ref[half, 0]
+            once, twice = keep_one * grad_v, keep_two * grad_v
+            for k, term in enumerate((grad_v * u_val, once * one, twice * two)):
+                sums_ref[half, k : k + 1] += jnp.sum(term, axis=0, keepdims=True)
+            heads_ref[half, 0, 0:1] = tap[2:3] * twice[0:1]
+            heads_ref[half, 0, 1:2] = tap[1:2] * once[0:1] + tap[2:3] * twice[1:2]
 
     shape = (2, 4, seg, chan)
+    shapes = [out(shape, bf16), out(shape, f32)]
+    shapes += [out((2, 3, chan), f32), out((2, 4, 2, chan), f32)]
     return call(
         body,
-        [out(shape, bf16), out(shape, f32), out((2, 3, chan), f32), out((2, 4, 2, chan), f32)],
+        shapes,
         *grad_mixer,
         u_vals,
         halo,
@@ -336,7 +393,14 @@
         v_vals,
         keeps,
         taps,
-        pack,
+        *[pack] * len(columns),
+        grid=(4,),
+        in_specs=[every_step(v) for v in grad_mixer]
+        + [by_segment(v) for v in (u_vals, halo, c_part, v_vals, keeps)]
+        + [every_step(taps)]
+        + columns,
+        out_specs=[by_segment(shapes[0]), by_segment(shapes[1])]
+        + [every_step(shapes[2]), by_segment(shapes[3])],
         flops=2 * 4 * seg * width * 2 * chan,
     )
 
@@ -346,28 +410,27 @@
 
     def body(dc_ref, dv_ref, back_ref, b_ref, x_ref, keep_ref, taps_ref, dp_ref):
         row = rows_of((seg, chan))
-        for segment in range(4):
-            keep_one, keep_two = keep_ref[0, segment], keep_ref[1, segment]
-            for half in range(2):
-                tap = taps_ref[half]
-                grad_val = dv_ref[half, segment]
-                once = jnp.where(row == seg - 1, 0.0, pltpu.roll(keep_one * grad_val, seg - 1, 0))
-                twice = jnp.where(row >= seg - 2, 0.0, pltpu.roll(keep_two * grad_val, seg - 2, 0))
-                grad_u = tap[0:1] * grad_val + tap[1:2] * once + tap[2:3] * twice
-                ends = back_ref[half, segment]
-                grad_u = grad_u + jnp.where(
-                    row == seg - 2, ends[0:1], jnp.where(row == seg - 1, ends[1:2], 0.0)
-                )
-                grad_u = grad_u.astype(bf16).astype(f32)
-                dp_ref[half, segment * seg : (segment + 1) * seg, :] = jnp.concatenate(
-                    [
-                        grad_u * x_ref[half, segment],
-                        dc_ref[half, segment].astype(f32),
-                        jnp.zeros((seg, chan), f32),
-                        grad_u * b_ref[half, segment],
-                    ],
-                    axis=1,
-                ).astype(bf16)
+        keep_one, keep_two = keep_ref[0, 0], keep_ref[1, 0]
+        for half in range(2):
+            tap = taps_ref[half]
+            grad_val = dv_ref[half, 0]
+            once = jnp.where(row == seg - 1, 0.0, pltpu.roll(keep_one * grad_val, seg - 1, 0))
+            twice = jnp.where(row >= seg - 2, 0.0, pltpu.roll(keep_two * grad_val, seg - 2, 0))
+            grad_u = tap[0:1] * grad_val + tap[1:2] * once + tap[2:3] * twice
+            ends = back_ref[half, 0]
+            grad_u = grad_u + jnp.where(
+                row == seg - 2, ends[0:1], jnp.where(row == seg - 1, ends[1:2], 0.0)
+            )
+            grad_u = grad_u.astype(bf16).astype(f32)
+            dp_ref[half] = jnp.concatenate(
+                [
+                    grad_u * x_ref[half, 0],
+                    dc_ref[half, 0].astype(f32),
+                    jnp.zeros((seg, chan), f32),
+                    grad_u * b_ref[half, 0],
+                ],
+                axis=1,
+            ).astype(bf16)
 
     return call(
         body,
@@ -379,6 +442,10 @@
         x_part,
         keeps,
         taps,
+        grid=(4,),
+        in_specs=[by_segment(v) for v in (grad_c, grad_v, back, b_part, x_part, keeps)]
+        + [every_step(taps)],
+        out_specs=[pl.BlockSpec((2, seg, 4 * chan), lambda s: (0, s, 0))],
     )[0]
 
 
@@ -442,14 +509,13 @@
                             fill = jnp.zeros((rows, LANES - count), f32)
                             weight = jnp.concatenate([weight, fill], axis=1)
                         total = total + values[side] * weight
-                        base = side * half_f + at
-                        gu_ref[:, base : base + count] = (values[side] * scale)[:, :count]
+                        gu_ref[:, side, at : at + count] = (values[side] * scale)[:, :count]
                     down_ref[:, at : at + count] = values[2][:, :count]
         sum_ref[...] = jnp.sum(total, axis=1, keepdims=True)
 
     return call(
         body,
-        [out((rows, 2 * half_f), f32), out((rows, half_f), f32), out((rows, 1), f32)],
+        [out((rows, 2, half_f), f32), out((rows, half_f), f32), out((rows, 1), f32)],
         place,
         first,
         second,
@@ -824,25 +890,25 @@
         gate_up[:, 0], gate_up[:, 1], w_down.T, gain_two[:, 0], place, cuts, hid
     )
     first_quart, second_quart = packs
-    first_got = exchange_first(first_quart)
-    hats_near, first_got = together(hats_near, first_got)
+    hats_near, (first_quart,) = together(hats_near, (first_quart,))
     hats = [hat_own] + hats_near + gather_second(hats_near)
-    first_pack = exchange_second(first_got).reshape(plane_rows, -1)
+    first_got = exchange_first(after(first_quart, *hats[5:]))
     cot, cot_top, cot_low = lax.optimization_barrier(
         (cot, cot[:half_seg], cot[half_seg:], *hats[5:])
     )[:3]
     cots_near = gather_first(cot_top, cot_low)
 
     projected, marks = conv_project(hats, conv_all, seg, tap_len)
-    projected, marks, cots_near, (second_quart,) = together(
-        projected, marks, cots_near, (second_quart,)
-    )
+    projected, marks, (second_quart,), first_got = together(
+        projected, marks, (second_quart,), first_got
+    )
+    first_pack = exchange_second(first_got).reshape(plane_rows, -1)
     b_part, c_part, x_part, mixed_in = projected
     keeps, taps, tails, tail_gate = marks
     second_got = exchange_first(second_quart)
     halo = halo_forward(tails).astype(f32)
     convolved, gated, mixer = conv_mix(mixed_in, halo, c_part, keeps, taps, conv_all, seg)
-    mixer, second_got = together(mixer, second_got)
+    mixer, second_got, cots_near = together(mixer, second_got, cots_near)
     far, near = reduce_far(mixer), reduce_near(mixer)
     second_pack = exchange_second(second_got).reshape(plane_rows, -1)
     ffn_all = [over_all(first_pack), over_all(second_pack)]
@@ -895,7 +961,7 @@
     near = gather_first(mix_top, mix_low)
     near, (back_one,) = together(near, (red_one,))
     grad_mixer = [mix_own] + near + gather_second(near)
-    ffn_out, grad_mixer = together(ffn_out, grad_mixer)
+    ffn_out, grad_mixer, back_one = together(ffn_out, grad_mixer, ordered(back_one))
     ffn_far = reduce_far(ffn_out)
     grad_c, grad_v, tap_sums, heads = conv_back(
         grad_mixer, mixed_in, halo, c_part, convolved, keeps, taps, conv_all, seg
@@ -904,9 +970,7 @@
     ffn_passed = reduce_passed(ffn_out, ffn_far)[1]
     back = halo_backward(heads) * tail_gate
     grad_proj = conv_grads(grad_c, grad_v, back, b_part, x_part, keeps, taps, seg)
-    (grad_proj,), ffn_passed, back_one = together((grad_proj,), ffn_passed, ordered(back_one))
-    first_got = exchange_first(back_one)
-    ffn_near = reduce_near(ffn_out)
+    (grad_proj,), ffn_passed, back_one = together((grad_proj,), ffn_passed, back_one)
     gated = gated.reshape(2, 4 * seg, chan)
     tap_rows = jnp.transpose(tap_sums.reshape(2, 3, planes, tap_len), (2, 0, 1, 3))
     tap_rows = tap_rows.reshape(planes, 2, 1, 3 * tap_len).astype(bf16)
@@ -914,18 +978,31 @@
     sum_conv = weight_grad(
         hats, grad_proj, grad_mixer, gated, 2 * chan, plane_rows, seg, tap_rows
     )
-    red_conv = over_owners(sum_conv)
-    (grad_proj,), ffn_near, _ = together((grad_proj,), ffn_near, (sum_conv,))
-    grad_hat1 = turned_back([grad_proj], [conv_all], 0, plane_rows, seg)
-    grad_hat1, first_got, back_two = together(grad_hat1, first_got, ordered(red_two))
+    first_got = exchange_first(back_one)
+    (sum_held,), first_got = together((sum_conv,), first_got)
+    red_conv = over_owners(sum_held)
+    ffn_near = reduce_near(ffn_out)
+    grad_hat1 = turned_back([after(grad_proj, sum_conv)], [conv_all], 0, plane_rows, seg)
+    grad_hat1, ffn_near, ffn_out, (middle, back_two) = together(
+        grad_hat1, ffn_near, ffn_out, (middle, red_two)
+    )
     far, near = reduce_far(grad_hat1), reduce_near(grad_hat1)
+    back_two = ordered(back_two)
+    far, near, grad_hat1, back_two, first_got, ffn_out, ffn_near, (middle,) = together(
+        far, near, grad_hat1, back_two, first_got, ffn_out, ffn_near, (middle,)
+    )
+    passed = reduce_passed(grad_hat1, far)[1]
+    second_got = exchange_first(back_two)
     out_own, out_both = block_out(ffn_out, ffn_passed + ffn_near, middle, own_half)
-    far, near, grad_hat1, (out_own, out_both) = together(far, near, grad_hat1, (out_own, out_both))
-    sent, passed = reduce_passed(grad_hat1, far)
-    back_two, _ = together(back_two, sent)
-    second_got = exchange_first(back_two)
-    output_vals = fill_other(out_both, core_swap(after(out_own, *sent)), own_half)
-
+
+    conv_got = exchange_first(ordered(red_conv[:plane_rows]))
+    passed, near, grad_hat1, second_got, conv_got, (out_own, out_both) = together(
+        passed, near, grad_hat1, second_got, conv_got, (out_own, out_both)
+    )
+    output_vals = fill_other(out_both, core_swap(out_own), own_half)
+    grad_own, grad_both = tokens_back(grad_hat1, passed + near, grad_middle, tokens, own_half)
+    second_got, _ = together(second_got, (grad_own,))
+    grad_inputs = fill_other(grad_both, core_swap(grad_own), own_half)
     out_gu, down_turned, gain_sum = ffn_unpack(
         jnp.stack(first_got),
         jnp.stack(second_got),
@@ -936,14 +1013,7 @@
         cuts,
         hid,
     )
-    out_gu = out_gu.reshape(rows, 2, half_f)
     out_down = down_turned.T
-    conv_got = exchange_first(ordered(red_conv[:plane_rows]))
-    last, grad_hat1, conv_got, (out_gu, out_down, gain_sum, output_vals) = together(
-        passed + near, grad_hat1, conv_got, (out_gu, out_down, gain_sum, output_vals)
-    )
-    grad_own, grad_both = tokens_back(grad_hat1, last, grad_middle, tokens, own_half)
-    grad_inputs = fill_other(grad_both, core_swap(grad_own), own_half)
     conv_grad = exchange_second(conv_got).astype(f32)
     tap_grad = lax.ppermute(
         red_conv[plane_rows, : 3 * tap_len].astype(f32).reshape(3, 1, tap_len),

time: 613 us -> 596 us (0.972)
  starting transfers between devices: 124 us -> 92.2 us
  waiting for transfers between devices: 161 us -> 173 us
  other arithmetic: 23.4 us -> 32.7 us
    ppermute x5, starting transfers between devices: 47.6 us -> 24.6 us  [core_swap(): return lax.ppermute(value, 'mp', SWAP)]
    reduce_scatter x3, waiting for transfers between devices: 0.02 us -> 14.9 us  [over_owners(): lax.psum_scatter(value, ('z', 'mp'), scatter_dimension=0, tiled=False)]
    ppermute x1, starting transfers between devices: 15.7 us -> 8.31 us  [per_device(): lax.ppermute(red_conv[plane_rows, :3 * tap_len].astype(f32).reshape(3, 1,...]
    ppermute x30, waiting for transfers between devices: 60.7 us -> 53.4 us  [plane_swap(): return lax.ppermute(value, 'x', SWAP)]
    unnamed x162 -> x178, local copies, waits for them, and re-layouts: 23.2 us -> 18 us
  transfers between devices with their start and end apart: 81 -> 81, of which waited for: 33 -> 39; matrix products, arithmetic and copies ran while one was open for 7% -> 8% of each run, Pallas kernels for 38% -> 39%
where the time goes in v4:
time: 596 us; the launch traced here: 586 us
  Pallas kernels  233 us (39%)
  waiting for transfers between devices  173 us (29%)
  starting transfers between devices  92.2 us (15%)
  local copies, waits for them, and re-layouts  39.1 us (7%)
  other arithmetic  32.7 us (5%)
  between operations  16 us (3%)
    pallas_call x23, Pallas kernels, call(): pl.pallas_call(body, out_shape=out_shapes, grid_spec=pltpu.PrefetchScalar...  233 us
    ppermute x30, waiting for transfers between devices, plane_swap(): return lax.ppermute(value, 'y', SWAP)  95.5 us
    ppermute x30, waiting for transfers between devices, plane_swap(): return lax.ppermute(value, 'x', SWAP)  53.4 us
    ppermute x30, starting transfers between devices, plane_swap(): return lax.ppermute(value, 'y', SWAP)  25.2 us
    ppermute x5, starting transfers between devices, core_swap(): return lax.ppermute(value, 'mp', SWAP)  24.6 us
    ppermute x30, starting transfers between devices, plane_swap(): return lax.ppermute(value, 'x', SWAP)  19.1 us
    unnamed x178, local copies, waits for them, and re-layouts  18 us
    reduce_scatter x3, waiting for transfers between devices, over_owners(): lax.psum_scatter(value, ('z', 'mp'), scatter_dimension=0, tiled=False)  14.9 us
  transfers between devices with their start and end apart: 81, of which 39 were waited for; matrix products, arithmetic and copies ran while one was open for 8% of the time, Pallas kernels for 39%

profile of v4, /device:TPU:25, one launch (start us, length us, event | category | flops | bytes accessed | tf_op | source)
XLA Modules:
  0.0 585.7 jit_solution(2878314685561394013)
XLA Ops:
  8.0 3.7 collective-permute-start.9
  16.2 1.6 collective-permute-start.7
  21.8 2.9 collective-permute-done.7
  28.1 2.1 collective-permute-start.2
  31.9 4.1 fusion.17
  39.1 4.0 collective-permute-done.2.refs_3_
  43.1 1.6 collective-permute-done.refs_1_
  44.6 12.1 %collective-permute-done.3.refs_4_ = bf16[208,1536]{1,0:T(8,128)(2,1)S(1)} collective-permute-done((bf16[208,1536]{1,0:T(8,128)(2,1)S(1)}, bf16[208,1536]{1,0:T(8,128)(2,1)S(1)}, u32[]{:S(2)}, u32[]{:S(2)}) %collective-permute-start.3) | collective-permute-done | bytes 639008 | tf_op jit(solution)/shard_map/ppermute | solution.py:58
  56.8 1.6 collective-permute-done.1.refs_2_
  59.4 12.0 %collective-permute-done.4.refs_5_ = bf16[192,1536]{1,0:T(8,128)(2,1)S(1)} collective-permute-done((bf16[192,1536]{1,0:T(8,128)(2,1)S(1)}, bf16[192,1536]{1,0:T(8,128)(2,1)S(1)}, u32[]{:S(2)}, u32[]{:S(2)}) %collective-permute-start.4) | collective-permute-done | bytes 589856 | tf_op jit(solution)/shard_map/ppermute | solution.py:58
  76.5 3.7 all-gather.9.cloned.1.call-done
  81.2 13.1 %shard_map.170 = (f32[2,4,384,192]{3,2,1,0:T(8,128)}, f32[2,4,384,192]{3,2,1,0:T(8,128)}, f32[2,4,384,192]{3,2,1,0:T(8,128)}, bf16[2,4,384,192]{3,2,1,0:T(8,128)...) custom-call(bf16[400,1536]{1,0:T(8,128)(2,1)} %pad_maximum_fusion.re, ...), custom_call_target="tpu_custom_call" | custom-call | flops 724775 | bytes 1811 | tf_op jit(solution)/shard_map/pallas_call | solution.py:145
  96.0 1.7 maximum_select_fusion
  97.8 2.7 maximum_select_fusion.1
  101.0 1.5 collective-permute-start.20
  104.1 1.4 collective-permute-start.13
  107.2 2.4 collective-permute-start.17
  109.6 6.3 %collective-permute-done.20.refs_2_.refs_10_ = bf16[192,1536]{1,0:T(8,128)(2,1)S(1)} collective-permute-done((bf16[192,1536]{1,0:T(8,128)(2,1)S(1)}, bf16[192,1536]{1,0:T(8,128)(2,1)S(1)}, u32[]{:S(2)}, u32[]{:S(2)}) %collective-permute-start.20) | collective-permute-done | bytes 589856 | tf_op jit(solution)/shard_map/ppermute | solution.py:58
  115.9 1.4 collective-permute-start.16
  118.6 9.0 %shard_map.171 = (f32[2,4,384,192]{3,2,1,0:T(8,128)}, bf16[2,4,384,192]{3,2,1,0:T(8,128)(2,1)}, bf16[192,1536]{1,0:T(8,128)(2,1)S(1)}, bf16[192,1536]{1,0:T(8,12...) custom-call(bf16[2,4,384,192]{3,2,1,0:T(8,128)(2,1)} %get-tuple-elem, ...), custom_call_target="tpu_custom_call" | custom-call | flops 181193 | bytes 2165 | tf_op jit(solution)/shard_map/pallas_call | solution.py:145
  129.6 4.6 collective-permute-done.17
  134.3 3.7 collective-permute-done.16
  143.9 10.9 %collective-permute-done.22 = bf16[192,1536]{1,0:T(8,128)(2,1)S(1)} collective-permute-done((bf16[192,1536]{1,0:T(8,128)(2,1)}, bf16[192,1536]{1,0:T(8,128)(2,1)S(1)}, u32[]{:S(2)}, u32[]{:S(2)}) %collective-permute-start.22) | collective-permute-done | bytes 589856 | tf_op jit(solution)/shard_map/ppermute | solution.py:56
  155.7 11.7 %collective-permute-done.24.refs_2_ = bf16[192,1536]{1,0:T(8,128)(2,1)S(1)} collective-permute-done((bf16[192,1536]{1,0:T(8,128)(2,1)}, bf16[192,1536]{1,0:T(8,128)(2,1)S(1)}, u32[]{:S(2)}, u32[]{:S(2)}) %collective-permute-start.24) | collective-permute-done | bytes 589856 | tf_op jit(solution)/shard_map/ppermute | solution.py:56
  170.5 11.6 %collective-permute-done.27.refs_1_ = bf16[192,1536]{1,0:T(8,128)(2,1)S(1)} collective-permute-done((bf16[192,1536]{1,0:T(8,128)(2,1)S(1)}, bf16[192,1536]{1,0:T(8,128)(2,1)S(1)}, u32[]{:S(2)}, u32[]{:S(2)}) %collective-permute-start.27) | collective-permute-done | bytes 589856 | tf_op jit(solution)/shard_map/ppermute | solution.py:58
  182.4 4.5 shard_map.172
  191.8 8.2 %shard_map.173 = (bf16[2,1536,512]{2,1,0:T(8,128)(2,1)}, bf16[2,1536,1024]{2,1,0:T(8,128)(2,1)}) custom-call(bf16[384,1536]{1,0:T(8,128)(2,1)S(1)} %copy-done.1, bf16[384,1536]{1,0:T(8,128)(2,1)S(1)} %constant_dynamic-slice_fusion.2.refs_1_.refs_7_.refs_6_, bf16[4,2,384,1536]{3,2,1,0:T(8,128)(2,1)} %bitcast.241, bf16[4,2,384,1536]{3,2,1,0:T(8,128)(2,1)} %bitcast.242), custom_call_target="tpu_custom_call" | custom-call | flops 362387 | bytes 3067 | tf_op jit(solution)/shard_map/pallas_call | solution.py:145
  200.2 11.7 %collective-permute-done.31.refs_1_.refs_4_ = bf16[192,1536]{1,0:T(8,128)(2,1)} collective-permute-done((bf16[192,1536]{1,0:T(8,128)(2,1)}, bf16[192,1536]{1,0:T(8,128)(2,1)}, u32[]{:S(2)}, u32[]{:S(2)}) %collective-permute-start.31) | collective-permute-done | bytes 589856 | tf_op jit(solution)/shard_map/ppermute | solution.py:58
  215.7 8.4 %shard_map.174 = (bf16[2,1536,512]{2,1,0:T(8,128)(2,1)}, bf16[2,1536,1024]{2,1,0:T(8,128)(2,1)}) custom-call(bf16[192,1536]{1,0:T(8,128)(2,1)} %collective-permute-done.28.refs_0_.refs_1_, bf16[192,1536]{1,0:T(8,128)(2,1)} %collective-permute-done.29.refs_1_.refs_2_, ...), custom_call_target="tpu_custom_call", output_to_operand_aliasing={{0}: (6, {}), {1}: (7, {})} | custom-call | flops 362387 | bytes 4010 | tf_op jit(solution)/shard_map/pallas_call | solution.py:145
  224.2 8.5 %shard_map.175 = (bf16[2,1536,512]{2,1,0:T(8,128)(2,1)}, bf16[2,1536,1024]{2,1,0:T(8,128)(2,1)}) custom-call(bf16[192,1536]{1,0:T(8,128)(2,1)} %collective-permute-done.30.refs_0_.refs_3_, bf16[192,1536]{1,0:T(8,128)(2,1)} %collective-permute-done.31.refs_1_.refs_4_, ...), custom_call_target="tpu_custom_call", output_to_operand_aliasing={{0}: (6, {}), {1}: (7, {})} | custom-call | flops 362387 | bytes 4010 | tf_op jit(solution)/shard_map/pallas_call | solution.py:145
  232.7 4.5 collective-permute-done.35.refs_3_.refs_13_
  237.2 8.7 %shard_map.176 = (bf16[2,1536,512]{2,1,0:T(8,128)(2,1)}, bf16[2,1536,1024]{2,1,0:T(8,128)(2,1)}) custom-call(bf16[192,1536]{1,0:T(8,128)(2,1)S(1)} %collective-permute-done.32.refs_0_.refs_5_, bf16[192,1536]{1,0:T(8,128)(2,1)S(1)} %collective-permute-done.33.refs_1_.refs_6_, ...), custom_call_target="tpu_custom_call", output_to_operand_aliasing={{0}: (6, {}), {1}: (7, {})} | custom-call | flops 362387 | bytes 4010 | tf_op jit(solution)/shard_map/pallas_call | solution.py:145
  246.0 22.8 %shard_map.177 = bf16[4,2,384,1536]{3,2,1,0:T(8,128)(2,1)} custom-call(bf16[384,1536]{1,0:T(8,128)(2,1)} %get-tuple-element.326.refs_0_, bf16[192,1536]{1,0:T(8,128)(2,1)} %collective-permute-done.28.refs_0_.refs_1_, bf16[192,1536]{1,0:T(8,128)(2,1)} %collective-permute-done.29.refs_1_.refs_2_, bf16[192,1536]{1,0:T(8,128)(2,1)} %collective-permute-done.30.refs_0_.refs_3_, ...), custom_call_target="tpu_custom_call" | custom-call | flops 1449551 | bytes 2831 | tf_op jit(solution)/shard_map/pallas_call | solution.py:145
  269.8 17.2 %shard_map.178 = (bf16[2,1536,384]{2,1,0:T(8,128)(2,1)}, bf16[2,1536,768]{2,1,0:T(8,128)(2,1)}) custom-call(bf16[384,1536]{1,0:T(8,128)(2,1)} %get-tuple-element.326.refs_0_, bf16[192,1536]{1,0:T(8,128)(2,1)} %collective-permute-done.28.refs_0_.refs_1_, bf16[192,1536]{1,0:T(8,128)(2,1)} %collective-permute-done.29.refs_1_.refs_2_, ...), custom_call_target="tpu_custom_call" | custom-call | flops 1087163 | bytes 3067 | tf_op jit(solution)/shard_map/pallas_call | solution.py:145
  287.1 24.5 %shard_map.179 = (bf16[192,1536]{1,0:T(8,128)(2,1)S(1)}, bf16[192,1536]{1,0:T(8,128)(2,1)S(1)}, bf16[192,1536]{1,0:T(8,128)(2,1)S(1)}, bf16[192,1536]{1,0:T(8,12...) custom-call(bf16[2,1536,1024]{2,1,0:T(8,128)(2,1)} %get-tuple-element.360.refs_, ...), custom_call_target="tpu_custom_call" | custom-call | flops 1691143 | bytes 3224 | tf_op jit(solution)/shard_map/pallas_call | solution.py:145
  315.3 19.7 %shard_map.180 = bf16[4,2,384,1152]{3,2,1,0:T(8,128)(2,1)} custom-call(bf16[384,1536]{1,0:T(8,128)(2,1)} %get-tuple-element.326.refs_0_, bf16[192,1536]{1,0:T(8,128)(2,1)} %collective-permute-done.28.refs_0_.refs_1_, bf16[192,1536]{1,0:T(8,128)(2,1)} %collective-permute-done.29.refs_1_.refs_2_, bf16[192,1536]{1,0:T(8,128)(2,1)} %collective-permute-done.30.refs_0_.refs_3_, ...), custom_call_target="tpu_custom_call" | custom-call | flops 1087163 | bytes 2359 | tf_op jit(solution)/shard_map/pallas_call | solution.py:145
  338.7 14.8 %shard_map.181 = (bf16[192,1536]{1,0:T(8,128)(2,1)}, bf16[192,1536]{1,0:T(8,128)(2,1)}, bf16[192,1536]{1,0:T(8,128)(2,1)}, bf16[192,1536]{1,0:T(8,128)(2,1)}, bf...) custom-call(bf16[2,1536,512]{2,1,0:T(8,128)(2,1)} %get-tuple-element.365.refs_15_.refs_0_, ...), custom_call_target="tpu_custom_call" | custom-call | flops 845571 | bytes 2673 | tf_op jit(solution)/shard_map/pallas_call | solution.py:145
  355.2 5.4 shard_map.182
  363.6 5.8 collective-permute-done.44.refs_3_.refs_10_
  370.3 10.8 %collective-permute-done.45.refs_4_.refs_11_ = bf16[192,1536]{1,0:T(8,128)(2,1)S(1)} collective-permute-done((bf16[192,1536]{1,0:T(8,128)(2,1)S(1)}, bf16[192,1536]{1,0:T(8,128)(2,1)S(1)}, u32[]{:S(2)}, u32[]{:S(2)}) %collective-permute-start.45) | collective-permute-done | bytes 589856 | tf_op jit(solution)/shard_map/ppermute | solution.py:58
  386.3 8.7 %collective-permute-done.46.refs_5_.refs_12_ = bf16[192,1536]{1,0:T(8,128)(2,1)S(1)} collective-permute-done((bf16[192,1536]{1,0:T(8,128)(2,1)S(1)}, bf16[192,1536]{1,0:T(8,128)(2,1)S(1)}, u32[]{:S(2)}, u32[]{:S(2)}) %collective-permute-start.46) | collective-permute-done | bytes 589856 | tf_op jit(solution)/shard_map/ppermute | solution.py:58
  400.8 10.4 %shard_map.183 = (bf16[2,4,384,192]{3,2,1,0:T(8,128)(2,1)}, f32[2,4,384,192]{3,2,1,0:T(8,128)}, f32[2,3,192]{2,1,0:T(4,128)S(1)}, f32[2,4,2,192]{3,2,1,0:T(2,128)S(1)}) custom-call(bf16[384,1536]{1,0:T(8,128)(2,1)} %get-tuple-element.415.refs_0_.refs_7_, bf16[192,1536]{1,0:T(8,128)(2,1)S(1)} %collective-permute-done.42.refs_1_.refs_8_, ...), custom_call_target="tpu_custom_call" | custom-call | flops 181193 | bytes 2403 | tf_op jit(solution)/shard_map/pallas_call | solution.py:145
  411.3 16.5 %collective-permute-start.50 = (f32[2,4,2,192]{3,2,1,0:T(2,128)S(1)}, f32[2,4,2,192]{3,2,1,0:T(2,128)S(1)}, u32[]{:S(2)}, u32[]{:S(2)}) collective-permute-start(f32[2,4,2,192]{3,2,1,0:T(2,128)S(1)} %get-tuple-element.433), channel_id=1, source_target_pairs={{0,1},{1,0},{2,3},{3,2},{4,5},{5,4},{6,7},{7,6},{8,9},{9,8},{10,11... | collective-permute-start | bytes 36872 | tf_op jit(solution)/shard_map/ppermute | solution.py:63
  428.7 1.4 add_convert_fusion.2
  432.4 7.6 %shard_map.184.refs_14_.refs_0_ = bf16[2,1536,768]{2,1,0:T(8,128)(2,1)} custom-call(bf16[2,4,384,192]{3,2,1,0:T(8,128)(2,1)S(1)} %copy-done.29, f32[2,4,384,192]{3,2,1,0:T(8,128)} %get-tuple-element.424.dv_ref, f32[2,4,2,192]{3,2,1,0:T(2,128)S(1)} %fusion.10.back_ref, f32[2,4,384,192]{3,2,1,0:T(8,128)} %get-tuple-element.435.b_ref, ...), custom_call_target="tpu_custom_call" | custom-call | bytes 1300 | tf_op jit(solution)/shard_map/pallas_call | solution.py:145
  440.0 2.4 collective-permute-done.53.refs_1_
  444.6 1.7 collective-permute-start.61
  447.3 16.8 %shard_map.185 = bf16[4,2,400,768]{3,2,1,0:T(8,128)(2,1)} custom-call(bf16[400,1536]{1,0:T(8,128)(2,1)} %pad_maximum_fusion.refs_0_, bf16[192,1536]{1,0:T(8,128)(2,1)S(1)} %copy-done.20, bf16[208,1536]{1,0:T(8,128)(2,1)} %copy-done.15, bf16[192,1536]{1,0:T(8,128)(2,1)S(1)} %copy-done.18, bf16[208,1536]{1,0:T(8,128)(2,1)} %copy-done.14, ...), custom_call_target="tpu_custom_call" | custom-call | flops 724775 | bytes 2064 | tf_op jit(solution)/shard_map/pallas_call | solution.py:145
  464.7 1.5 collective-permute-start.55
  466.2 11.8 %shard_map.186 = (bf16[192,1536]{1,0:T(8,128)(2,1)}, bf16[192,1536]{1,0:T(8,128)(2,1)}, bf16[192,1536]{1,0:T(8,128)(2,1)S(1)}, bf16[192,1536]{1,0:T(8,128)(2,1)S...) custom-call(bf16[2,1536,768]{2,1,0:T(8,128)(2,1)} %shard_map.184.refs_14_.refs_0_, ...), custom_call_target="tpu_custom_call" | custom-call | flops 724775 | bytes 1435 | tf_op jit(solution)/shard_map/pallas_call | solution.py:145
  481.2 1.5 collective-permute-start.59
  485.4 4.3 collective-permute-done.56
  490.2 12.2 %collective-permute-done.58.refs_2_ = bf16[192,1536]{1,0:T(8,128)(2,1)S(1)} collective-permute-done((bf16[192,1536]{1,0:T(8,128)(2,1)}, bf16[192,1536]{1,0:T(8,128)(2,1)S(1)}, u32[]{:S(2)}, u32[]{:S(2)}) %collective-permute-start.58) | collective-permute-done | bytes 589856 | tf_op jit(solution)/shard_map/ppermute | solution.py:56
  503.6 1.8 collective-permute-start.67
  508.3 14.9 %reduce-scatter.8.cloned.1.call-done = bf16[1,400,768]{2,1,0:T(8,128)(2,1)} async-done(((bf16[8,400,768]{2,1,0:T(8,128)(2,1)}), bf16[1,400,768]{2,1,0:T(8,128)(2,1)}) %reduce-scatter.8.cloned.1.call-update) | async-done | bytes 614416 | tf_op jit(solution)/shard_map/reduce_scatter | solution.py:940
  525.6 2.3 collective-permute-start.70
  528.3 4.0 shard_map.187
  532.5 8.3 %collective-permute-start.74 = (f32[3,1,48]{2,1,0:T(1,128)S(1)}, f32[3,1,48]{2,1,0:T(1,128)S(1)}, u32[]{:S(2)}, u32[]{:S(2)}) collective-permute-start(f32[3,1,48]{2,1,0:T(1,128)S(1)} %reshape.195), channel_id=1, source_target_pairs={{0,0},{8,2},{16,4},{24,6},{2,8},{10,10},{18,12},{26,14},{4,16},{12... | collective-permute-start | bytes 1736 | tf_op jit(solution)/shard_map/ppermute | solution.py:1018
  540.8 5.9 %shard_map.189 = (f32[384,1536]{1,0:T(8,128)}, f32[768,1536]{1,0:T(8,128)}) custom-call(s32[1]{0:T(128)} %bitcast.core_ref, bf16[384,1536]{1,0:T(8,128)(2,1)S(1)} %copy-done.30, bf16[192,1536]{1,0:T(8,128)(2,1)} %collective-permute-done.63.refs_0_, bf16[192,1536]{1,0:T(8,128)(2,1)} %collective-permute-done.64.refs_1_, ...), custom_call_target="tpu_custom_call" | custom-call | bytes 1533 | tf_op jit(solution)/shard_map/pallas_call | solution.py:145
  546.7 6.1 %collective-permute-start.72 = (f32[384,1536]{1,0:T(8,128)}, f32[384,1536]{1,0:T(8,128)S(1)}, u32[]{:S(2)}, u32[]{:S(2)}) collective-permute-start(f32[384,1536]{1,0:T(8,128)} %get-tuple-element.508), channel_id=1, source_target_pairs={{0,1},{1,0},{2,3},{3,2},{4,5},{5,4},{6,7},{7,6},{8,9},{9,8},{10,11... | collective-permute-start | bytes 7077896 | tf_op jit(solution)/shard_map/ppermute | solution.py:63
  554.2 1.4 maximum_select_fusion.14
  555.7 1.5 fusion.7
  560.5 7.5 %shard_map.191 = (f32[96,2,3456]{2,1,0:T(2,128)}, f32[96,3456]{1,0:T(8,128)}, f32[96,1]{1,0:T(8,128)S(1)}) custom-call(s32[1]{0:T(128)} %bitcast.18.place_ref, bf16[4,96,1536]{2,1,0:T(8,128)(2,1)S(1)} %pad_maximum_fusion.1.first_ref, bf16[4,96,1152]{2,1,0:T(8,128)(2,1)S(1)} %pad_maximum_fusion.3.second_ref, bf16[96,3456]{1,0:T(8,128)(2,1)S(1)} %copy-done.13, ...), custom_call_target="tpu_custom_call" | custom-call | bytes 737 | tf_op jit(solution)/shard_map/pallas_call | solution.py:145
  576.2 1.6 shard_map.190
  (418 shorter events, 110.7 us)
Async XLA Ops:
  7.2 73.0 %all-gather.9.cloned.1.call-start = ((), (), s32[]{:S(2)}) async-start(), calls=%async_computation.8 | async-start | bytes 5529600 | tf_op jit(solution)/shard_map/all_gather | solution.py:869
  8.0 19.1 %collective-permute-start.9 = (bf16[1,144]{1,0:T(2,128)(2,1)S(1)}, bf16[1,144]{1,0:T(2,128)(2,1)S(1)}, u32[]{:S(2)}, u32[]{:S(2)}) collective-permute-start(bf16[1,144]{1,0:T(2,128)(2,1)S(1)} %reshape.183), channel_id=1, source_target_pairs={{0,0},{2,8},{4,16},{6,24},{8,2},{10,10},{12,18},{14,26},{16,4},{18... | collective-permute-start | bytes 872 | tf_op jit(solution)/shard_map/ppermute | solution.py:864
  28.0 162.5 %all-gather.5.cloned.1.call-start = ((), (), s32[]{:S(2)}) async-start(), calls=%async_computation.3 | async-start | bytes 10616832 | tf_op jit(solution)/shard_map/all_gather | solution.py:869
  28.1 15.0 %collective-permute-start.2 = (bf16[192,1536]{1,0:T(8,128)(2,1)}, bf16[192,1536]{1,0:T(8,128)(2,1)S(1)}, u32[]{:S(2)}, u32[]{:S(2)}) collective-permute-start(bf16[192,1536]{1,0:T(8,128)(2,1)} %get-tuple-element.270), channel_id=1, source_target_pairs={{0,4},{4,0},{1,5},{5,1},{2,6},{6,2},{3,7},{7,3},{8,12},{12,8},{9,1... | collective-permute-start | bytes 1769480 | tf_op jit(solution)/shard_map/ppermute | solution.py:58
  30.2 14.4 %collective-permute-start = (bf16[192,1536]{1,0:T(8,128)(2,1)}, bf16[192,1536]{1,0:T(8,128)(2,1)S(1)}, u32[]{:S(2)}, u32[]{:S(2)}) collective-permute-start(bf16[192,1536]{1,0:T(8,128)(2,1)} %get-tuple-element.270), channel_id=1, source_target_pairs={{0,2},{2,0},{1,3},{3,1},{4,6},{6,4},{5,7},{7,5},{8,10},{10,8},{9,1... | collective-permute-start | bytes 1769480 | tf_op jit(solution)/shard_map/ppermute | solution.py:56
  30.2 26.5 %collective-permute-start.3 = (bf16[208,1536]{1,0:T(8,128)(2,1)S(1)}, bf16[208,1536]{1,0:T(8,128)(2,1)S(1)}, u32[]{:S(2)}, u32[]{:S(2)}) collective-permute-start(bf16[208,1536]{1,0:T(8,128)(2,1)S(1)} %pad_maximum_fusion.4), channel_id=1, source_target_pairs={{0,4},{4,0},{1,5},{5,1},{2,6},{6,2},{3,7},{7,3},{8,12},{12,8},{9,1... | collective-permute-start | bytes 1916936 | tf_op jit(solution)/shard_map/ppermute | solution.py:58
  31.5 26.9 %collective-permute-start.1 = (bf16[208,1536]{1,0:T(8,128)(2,1)S(1)}, bf16[208,1536]{1,0:T(8,128)(2,1)S(1)}, u32[]{:S(2)}, u32[]{:S(2)}) collective-permute-start(bf16[208,1536]{1,0:T(8,128)(2,1)S(1)} %pad_maximum_fusion.4), channel_id=1, source_target_pairs={{0,2},{2,0},{1,3},{3,1},{4,6},{6,4},{5,7},{7,5},{8,10},{10,8},{9,1... | collective-permute-start | bytes 1916936 | tf_op jit(solution)/shard_map/ppermute | solution.py:56
  58.3 14.4 %collective-permute-start.5 = (bf16[208,1536]{1,0:T(8,128)(2,1)S(1)}, bf16[208,1536]{1,0:T(8,128)(2,1)S(1)}, u32[]{:S(2)}, u32[]{:S(2)}) collective-permute-start(bf16[208,1536]{1,0:T(8,128)(2,1)S(1)} %collective-permute-done.3.refs_4_), channel_id=1, source_target_pairs={{0,2},{2,0},{1,3},{3,1},{4,6},{6,4},{5,7},{7,5},{8,10},{10,8},{9,1... | collective-permute-start | bytes 1916936 | tf_op jit(solution)/shard_map/ppermute | solution.py:56
  58.3 13.1 %collective-permute-start.4 = (bf16[192,1536]{1,0:T(8,128)(2,1)S(1)}, bf16[192,1536]{1,0:T(8,128)(2,1)S(1)}, u32[]{:S(2)}, u32[]{:S(2)}) collective-permute-start(bf16[192,1536]{1,0:T(8,128)(2,1)S(1)} %collective-permute-done.refs_1_), channel_id=1, source_target_pairs={{0,4},{4,0},{1,5},{5,1},{2,6},{6,2},{3,7},{7,3},{8,12},{12,8},{9,1... | collective-permute-start | bytes 1769480 | tf_op jit(solution)/shard_map/ppermute | solution.py:58
  73.8 22.2 %collective-permute-start.12 = (bf16[96,1536]{1,0:T(8,128)(2,1)}, bf16[96,1536]{1,0:T(8,128)(2,1)}, u32[]{:S(2)}, u32[]{:S(2)}) collective-permute-start(bf16[96,1536]{1,0:T(8,128)(2,1)} %get-tuple-element.561), channel_id=1, source_target_pairs={{0,6},{2,4},{4,2},{6,0},{1,7},{3,5},{5,3},{7,1},{8,14},{10,12},{12... | collective-permute-start | bytes 884744 | tf_op jit(solution)/shard_map/ppermute | solution.py:59
  75.2 20.8 %collective-permute-start.11 = (bf16[96,1536]{1,0:T(8,128)(2,1)}, bf16[96,1536]{1,0:T(8,128)(2,1)}, u32[]{:S(2)}, u32[]{:S(2)}) collective-permute-start(bf16[96,1536]{1,0:T(8,128)(2,1)} %get-tuple-element.562), channel_id=1, source_target_pairs={{0,4},{4,0},{1,5},{5,1},{2,6},{6,2},{3,7},{7,3},{8,12},{12,8},{9,1... | collective-permute-start | bytes 884744 | tf_op jit(solution)/shard_map/ppermute | solution.py:58
  76.0 20.1 %collective-permute-start.10 = (bf16[96,1536]{1,0:T(8,128)(2,1)}, bf16[96,1536]{1,0:T(8,128)(2,1)}, u32[]{:S(2)}, u32[]{:S(2)}) collective-permute-start(bf16[96,1536]{1,0:T(8,128)(2,1)} %get-tuple-element.563), channel_id=1, source_target_pairs={{0,2},{2,0},{1,3},{3,1},{4,6},{6,4},{5,7},{7,5},{8,10},{10,8},{9,1... | collective-permute-start | bytes 884744 | tf_op jit(solution)/shard_map/ppermute | solution.py:56
  100.5 168.7 %all-gather.7.cloned.1.call-start = ((), (), s32[]{:S(2)}) async-start(), calls=%async_computation.4 | async-start | bytes 7962624 | tf_op jit(solution)/shard_map/all_gather | solution.py:869
  101.0 14.8 %collective-permute-start.20 = (bf16[192,1536]{1,0:T(8,128)(2,1)S(1)}, bf16[192,1536]{1,0:T(8,128)(2,1)S(1)}, u32[]{:S(2)}, u32[]{:S(2)}) collective-permute-start(bf16[192,1536]{1,0:T(8,128)(2,1)S(1)} %get-tuple-element.305), channel_id=1, source_target_pairs={{0,4},{4,0},{1,5},{5,1},{2,6},{6,2},{3,7},{7,3},{8,12},{12,8},{9,1... | collective-permute-start | bytes 1769480 | tf_op jit(solution)/shard_map/ppermute | solution.py:58
  102.5 14.8 %collective-permute-start.18 = (bf16[192,1536]{1,0:T(8,128)(2,1)S(1)}, bf16[192,1536]{1,0:T(8,128)(2,1)S(1)}, u32[]{:S(2)}, u32[]{:S(2)}) collective-permute-start(bf16[192,1536]{1,0:T(8,128)(2,1)S(1)} %get-tuple-element.305), channel_id=1, source_target_pairs={{0,2},{2,0},{1,3},{3,1},{4,6},{6,4},{5,7},{7,5},{8,10},{10,8},{9,1... | collective-permute-start | bytes 1769480 | tf_op jit(solution)/shard_map/ppermute | solution.py:56
  103.7 24.8 %collective-permute-start.21 = (bf16[192,1536]{1,0:T(8,128)(2,1)S(1)}, bf16[192,1536]{1,0:T(8,128)(2,1)S(1)}, u32[]{:S(2)}, u32[]{:S(2)}) collective-permute-start(bf16[192,1536]{1,0:T(8,128)(2,1)S(1)} %get-tuple-element.306), channel_id=1, source_target_pairs={{0,4},{4,0},{1,5},{5,1},{2,6},{6,2},{3,7},{7,3},{8,12},{12,8},{9,1... | collective-permute-start | bytes 1769480 | tf_op jit(solution)/shard_map/ppermute | solution.py:58
  104.0 25.6 %collective-permute-start.19 = (bf16[192,1536]{1,0:T(8,128)(2,1)S(1)}, bf16[192,1536]{1,0:T(8,128)(2,1)S(1)}, u32[]{:S(2)}, u32[]{:S(2)}) collective-permute-start(bf16[192,1536]{1,0:T(8,128)(2,1)S(1)} %get-tuple-element.306), channel_id=1, source_target_pairs={{0,2},{2,0},{1,3},{3,1},{4,6},{6,4},{5,7},{7,5},{8,10},{10,8},{9,1... | collective-permute-start | bytes 1769480 | tf_op jit(solution)/shard_map/ppermute | solution.py:56
  107.2 27.1 %collective-permute-start.17 = (bf16[96,1152]{1,0:T(8,128)(2,1)S(1)}, bf16[96,1152]{1,0:T(8,128)(2,1)S(1)}, u32[]{:S(2)}, u32[]{:S(2)}) collective-permute-start(bf16[96,1152]{1,0:T(8,128)(2,1)S(1)} %get-tuple-element.581), channel_id=1, source_target_pairs={{0,6},{2,4},{4,2},{6,0},{1,7},{3,5},{5,3},{7,1},{8,14},{10,12},{12... | collective-permute-start | bytes 663560 | tf_op jit(solution)/shard_map/ppermute | solution.py:59
  115.9 22.1 %collective-permute-start.16 = (bf16[96,1152]{1,0:T(8,128)(2,1)S(1)}, bf16[96,1152]{1,0:T(8,128)(2,1)S(1)}, u32[]{:S(2)}, u32[]{:S(2)}) collective-permute-start(bf16[96,1152]{1,0:T(8,128)(2,1)S(1)} %get-tuple-element.582), channel_id=1, source_target_pairs={{0,4},{4,0},{1,5},{5,1},{2,6},{6,2},{3,7},{7,3},{8,12},{12,8},{9,1... | collective-permute-start | bytes 663560 | tf_op jit(solution)/shard_map/ppermute | solution.py:58
  117.3 21.8 %collective-permute-start.15 = (bf16[96,1152]{1,0:T(8,128)(2,1)S(1)}, bf16[96,1152]{1,0:T(8,128)(2,1)S(1)}, u32[]{:S(2)}, u32[]{:S(2)}) collective-permute-start(bf16[96,1152]{1,0:T(8,128)(2,1)S(1)} %get-tuple-element.583), channel_id=1, source_target_pairs={{0,2},{2,0},{1,3},{3,1},{4,6},{6,4},{5,7},{7,5},{8,10},{10,8},{9,1... | collective-permute-start | bytes 663560 | tf_op jit(solution)/shard_map/ppermute | solution.py:56
  140.8 240.5 %reduce-scatter.4.cloned.1.call-start = ((), (), s32[]{:S(2)}) async-start(), calls=%async_computation.5 | async-start | bytes 10616832 | tf_op jit(solution)/shard_map/reduce_scatter | solution.py:940
  140.8 13.9 %collective-permute-start.22 = (bf16[192,1536]{1,0:T(8,128)(2,1)}, bf16[192,1536]{1,0:T(8,128)(2,1)S(1)}, u32[]{:S(2)}, u32[]{:S(2)}) collective-permute-start(bf16[192,1536]{1,0:T(8,128)(2,1)} %copy-done.64), channel_id=1, source_target_pairs={{0,2},{2,0},{1,3},{3,1},{4,6},{6,4},{5,7},{7,5},{8,10},{10,8},{9,1... | collective-permute-start | bytes 1769480 | tf_op jit(solution)/shard_map/ppermute | solution.py:56
  142.1 13.6 %collective-permute-start.23 = (bf16[192,1536]{1,0:T(8,128)(2,1)}, bf16[192,1536]{1,0:T(8,128)(2,1)S(1)}, u32[]{:S(2)}, u32[]{:S(2)}) collective-permute-start(bf16[192,1536]{1,0:T(8,128)(2,1)} %copy-done.62), channel_id=1, source_target_pairs={{0,4},{4,0},{1,5},{5,1},{2,6},{6,2},{3,7},{7,3},{8,12},{12,8},{9,1... | collective-permute-start | bytes 1769480 | tf_op jit(solution)/shard_map/ppermute | solution.py:58
  142.4 25.0 %collective-permute-start.24 = (bf16[192,1536]{1,0:T(8,128)(2,1)}, bf16[192,1536]{1,0:T(8,128)(2,1)S(1)}, u32[]{:S(2)}, u32[]{:S(2)}) collective-permute-start(bf16[192,1536]{1,0:T(8,128)(2,1)} %copy-done.60), channel_id=1, source_target_pairs={{0,2},{2,0},{1,3},{3,1},{4,6},{6,4},{5,7},{7,5},{8,10},{10,8},{9,1... | collective-permute-start | bytes 1769480 | tf_op jit(solution)/shard_map/ppermute | solution.py:56
  142.7 25.7 %collective-permute-start.25 = (bf16[192,1536]{1,0:T(8,128)(2,1)}, bf16[192,1536]{1,0:T(8,128)(2,1)S(1)}, u32[]{:S(2)}, u32[]{:S(2)}) collective-permute-start(bf16[192,1536]{1,0:T(8,128)(2,1)} %copy-done.59), channel_id=1, source_target_pairs={{0,4},{4,0},{1,5},{5,1},{2,6},{6,2},{3,7},{7,3},{8,12},{12,8},{9,1... | collective-permute-start | bytes 1769480 | tf_op jit(solution)/shard_map/ppermute | solution.py:58
  169.5 12.6 %collective-permute-start.27 = (bf16[192,1536]{1,0:T(8,128)(2,1)S(1)}, bf16[192,1536]{1,0:T(8,128)(2,1)S(1)}, u32[]{:S(2)}, u32[]{:S(2)}) collective-permute-start(bf16[192,1536]{1,0:T(8,128)(2,1)S(1)} %add_convert_fusion.6), channel_id=1, source_target_pairs={{0,4},{4,0},{1,5},{5,1},{2,6},{6,2},{3,7},{7,3},{8,12},{12,8},{9,1... | collective-permute-start | bytes 1769480 | tf_op jit(solution)/shard_map/ppermute | solution.py:58
  189.0 22.9 %collective-permute-start.31 = (bf16[192,1536]{1,0:T(8,128)(2,1)}, bf16[192,1536]{1,0:T(8,128)(2,1)}, u32[]{:S(2)}, u32[]{:S(2)}) collective-permute-start(bf16[192,1536]{1,0:T(8,128)(2,1)} %get-tuple-element.335), channel_id=1, source_target_pairs={{0,4},{4,0},{1,5},{5,1},{2,6},{6,2},{3,7},{7,3},{8,12},{12,8},{9,1... | collective-permute-start | bytes 1769480 | tf_op jit(solution)/shard_map/ppermute | solution.py:58
  189.6 23.2 %collective-permute-start.29 = (bf16[192,1536]{1,0:T(8,128)(2,1)}, bf16[192,1536]{1,0:T(8,128)(2,1)}, u32[]{:S(2)}, u32[]{:S(2)}) collective-permute-start(bf16[192,1536]{1,0:T(8,128)(2,1)} %get-tuple-element.335), channel_id=1, source_target_pairs={{0,2},{2,0},{1,3},{3,1},{4,6},{6,4},{5,7},{7,5},{8,10},{10,8},{9,1... | collective-permute-start | bytes 1769480 | tf_op jit(solution)/shard_map/ppermute | solution.py:56
  212.8 19.9 %collective-permute-start.33 = (bf16[192,1536]{1,0:T(8,128)(2,1)}, bf16[192,1536]{1,0:T(8,128)(2,1)S(1)}, u32[]{:S(2)}, u32[]{:S(2)}) collective-permute-start(bf16[192,1536]{1,0:T(8,128)(2,1)} %collective-permute-done.31.refs_1_.refs_4_), channel_id=1, source_target_pairs={{0,2},{2,0},{1,3},{3,1},{4,6},{6,4},{5,7},{7,5},{8,10},{10,8},{9,1... | collective-permute-start | bytes 1769480 | tf_op jit(solution)/shard_map/ppermute | solution.py:56
  213.0 24.2 %collective-permute-start.35 = (bf16[192,1536]{1,0:T(8,128)(2,1)S(1)}, bf16[192,1536]{1,0:T(8,128)(2,1)S(1)}, u32[]{:S(2)}, u32[]{:S(2)}) collective-permute-start(bf16[192,1536]{1,0:T(8,128)(2,1)S(1)} %collective-permute-done.21.refs_3_.refs_11_), channel_id=1, source_target_pairs={{0,2},{2,0},{1,3},{3,1},{4,6},{6,4},{5,7},{7,5},{8,10},{10,8},{9,1... | collective-permute-start | bytes 1769480 | tf_op jit(solution)/shard_map/ppermute | solution.py:56
  214.3 23.0 %collective-permute-start.32 = (bf16[192,1536]{1,0:T(8,128)(2,1)}, bf16[192,1536]{1,0:T(8,128)(2,1)S(1)}, u32[]{:S(2)}, u32[]{:S(2)}) collective-permute-start(bf16[192,1536]{1,0:T(8,128)(2,1)} %collective-permute-done.28.refs_0_.refs_1_), channel_id=1, source_target_pairs={{0,4},{4,0},{1,5},{5,1},{2,6},{6,2},{3,7},{7,3},{8,12},{12,8},{9,1... | collective-permute-start | bytes 1769480 | tf_op jit(solution)/shard_map/ppermute | solution.py:58
  214.6 22.7 %collective-permute-start.34 = (bf16[192,1536]{1,0:T(8,128)(2,1)S(1)}, bf16[192,1536]{1,0:T(8,128)(2,1)S(1)}, u32[]{:S(2)}, u32[]{:S(2)}) collective-permute-start(bf16[192,1536]{1,0:T(8,128)(2,1)S(1)} %collective-permute-done.18.refs_2_.refs_8_), channel_id=1, source_target_pairs={{0,4},{4,0},{1,5},{5,1},{2,6},{6,2},{3,7},{7,3},{8,12},{12,8},{9,1... | collective-permute-start | bytes 1769480 | tf_op jit(solution)/shard_map/ppermute | solution.py:58
  268.8 210.9 %reduce-scatter.6.cloned.1.call-start = ((), (), s32[]{:S(2)}) async-start(), calls=%async_computation.6 | async-start | bytes 7962624 | tf_op jit(solution)/shard_map/reduce_scatter | solution.py:940
  312.4 22.6 %collective-permute-start.36 = (bf16[192,1536]{1,0:T(8,128)(2,1)S(1)}, bf16[192,1536]{1,0:T(8,128)(2,1)S(1)}, u32[]{:S(2)}, u32[]{:S(2)}) collective-permute-start(bf16[192,1536]{1,0:T(8,128)(2,1)S(1)} %get-tuple-element.368), channel_id=1, source_target_pairs={{0,2},{2,0},{1,3},{3,1},{4,6},{6,4},{5,7},{7,5},{8,10},{10,8},{9,1... | collective-permute-start | bytes 1769480 | tf_op jit(solution)/shard_map/ppermute | solution.py:56
  312.7 22.3 %collective-permute-start.37 = (bf16[192,1536]{1,0:T(8,128)(2,1)S(1)}, bf16[192,1536]{1,0:T(8,128)(2,1)S(1)}, u32[]{:S(2)}, u32[]{:S(2)}) collective-permute-start(bf16[192,1536]{1,0:T(8,128)(2,1)S(1)} %get-tuple-element.369), channel_id=1, source_target_pairs={{0,4},{4,0},{1,5},{5,1},{2,6},{6,2},{3,7},{7,3},{8,12},{12,8},{9,1... | collective-permute-start | bytes 1769480 | tf_op jit(solution)/shard_map/ppermute | solution.py:58
  313.3 21.8 %collective-permute-start.38 = (bf16[192,1536]{1,0:T(8,128)(2,1)S(1)}, bf16[192,1536]{1,0:T(8,128)(2,1)S(1)}, u32[]{:S(2)}, u32[]{:S(2)}) collective-permute-start(bf16[192,1536]{1,0:T(8,128)(2,1)S(1)} %get-tuple-element.370), channel_id=1, source_target_pairs={{0,2},{2,0},{1,3},{3,1},{4,6},{6,4},{5,7},{7,5},{8,10},{10,8},{9,1... | collective-permute-start | bytes 1769480 | tf_op jit(solution)/shard_map/ppermute | solution.py:56
  314.2 20.8 %collective-permute-start.39 = (bf16[192,1536]{1,0:T(8,128)(2,1)S(1)}, bf16[192,1536]{1,0:T(8,128)(2,1)S(1)}, u32[]{:S(2)}, u32[]{:S(2)}) collective-permute-start(bf16[192,1536]{1,0:T(8,128)(2,1)S(1)} %get-tuple-element.371), channel_id=1, source_target_pairs={{0,4},{4,0},{1,5},{5,1},{2,6},{6,2},{3,7},{7,3},{8,12},{12,8},{9,1... | collective-permute-start | bytes 1769480 | tf_op jit(solution)/shard_map/ppermute | solution.py:58
  336.0 187.1 %reduce-scatter.8.cloned.1.call-start = ((), (), s32[]{:S(2)}) async-start(), calls=%async_computation.7 | async-start | bytes 5529600 | tf_op jit(solution)/shard_map/reduce_scatter | solution.py:940
  337.4 17.8 %collective-permute-start.41 = (bf16[192,1536]{1,0:T(8,128)(2,1)S(1)}, bf16[192,1536]{1,0:T(8,128)(2,1)S(1)}, u32[]{:S(2)}, u32[]{:S(2)}) collective-permute-start(bf16[192,1536]{1,0:T(8,128)(2,1)S(1)} %add_convert_fusion.4), channel_id=1, source_target_pairs={{0,4},{4,0},{1,5},{5,1},{2,6},{6,2},{3,7},{7,3},{8,12},{12,8},{9,1... | collective-permute-start | bytes 1769480 | tf_op jit(solution)/shard_map/ppermute | solution.py:58
  338.1 17.1 %collective-permute-start.40 = (bf16[192,1536]{1,0:T(8,128)(2,1)S(1)}, bf16[192,1536]{1,0:T(8,128)(2,1)S(1)}, u32[]{:S(2)}, u32[]{:S(2)}) collective-permute-start(bf16[192,1536]{1,0:T(8,128)(2,1)S(1)} %add_convert_fusion.5), channel_id=1, source_target_pairs={{0,2},{2,0},{1,3},{3,1},{4,6},{6,4},{5,7},{7,5},{8,10},{10,8},{9,1... | collective-permute-start | bytes 1769480 | tf_op jit(solution)/shard_map/ppermute | solution.py:56
  362.6 18.4 %collective-permute-start.45 = (bf16[192,1536]{1,0:T(8,128)(2,1)S(1)}, bf16[192,1536]{1,0:T(8,128)(2,1)S(1)}, u32[]{:S(2)}, u32[]{:S(2)}) collective-permute-start(bf16[192,1536]{1,0:T(8,128)(2,1)S(1)} %get-tuple-element.409), channel_id=1, source_target_pairs={{0,4},{4,0},{1,5},{5,1},{2,6},{6,2},{3,7},{7,3},{8,12},{12,8},{9,1... | collective-permute-start | bytes 1769480 | tf_op jit(solution)/shard_map/ppermute | solution.py:58
  363.1 18.2 %collective-permute-start.43 = (bf16[192,1536]{1,0:T(8,128)(2,1)S(1)}, bf16[192,1536]{1,0:T(8,128)(2,1)S(1)}, u32[]{:S(2)}, u32[]{:S(2)}) collective-permute-start(bf16[192,1536]{1,0:T(8,128)(2,1)S(1)} %get-tuple-element.409), channel_id=1, source_target_pairs={{0,2},{2,0},{1,3},{3,1},{4,6},{6,4},{5,7},{7,5},{8,10},{10,8},{9,1... | collective-permute-start | bytes 1769480 | tf_op jit(solution)/shard_map/ppermute | solution.py:56
  381.3 13.8 %collective-permute-start.46 = (bf16[192,1536]{1,0:T(8,128)(2,1)S(1)}, bf16[192,1536]{1,0:T(8,128)(2,1)S(1)}, u32[]{:S(2)}, u32[]{:S(2)}) collective-permute-start(bf16[192,1536]{1,0:T(8,128)(2,1)S(1)} %collective-permute-done.42.refs_1_.refs_8_), channel_id=1, source_target_pairs={{0,4},{4,0},{1,5},{5,1},{2,6},{6,2},{3,7},{7,3},{8,12},{12,8},{9,1... | collective-permute-start | bytes 1769480 | tf_op jit(solution)/shard_map/ppermute | solution.py:58
  382.3 13.7 %collective-permute-start.47 = (bf16[192,1536]{1,0:T(8,128)(2,1)S(1)}, bf16[192,1536]{1,0:T(8,128)(2,1)S(1)}, u32[]{:S(2)}, u32[]{:S(2)}) collective-permute-start(bf16[192,1536]{1,0:T(8,128)(2,1)S(1)} %collective-permute-done.45.refs_4_.refs_11_), channel_id=1, source_target_pairs={{0,2},{2,0},{1,3},{3,1},{4,6},{6,4},{5,7},{7,5},{8,10},{10,8},{9,1... | collective-permute-start | bytes 1769480 | tf_op jit(solution)/shard_map/ppermute | solution.py:56
  396.0 15.4 %collective-permute-start.48 = (bf16[192,1536]{1,0:T(8,128)(2,1)}, bf16[192,1536]{1,0:T(8,128)(2,1)}, u32[]{:S(2)}, u32[]{:S(2)}) collective-permute-start(bf16[192,1536]{1,0:T(8,128)(2,1)} %get-tuple-element.426), channel_id=1, source_target_pairs={{0,2},{2,0},{1,3},{3,1},{4,6},{6,4},{5,7},{7,5},{8,10},{10,8},{9,1... | collective-permute-start | bytes 1769480 | tf_op jit(solution)/shard_map/ppermute | solution.py:56
  397.0 14.3 %collective-permute-start.49 = (bf16[192,1536]{1,0:T(8,128)(2,1)}, bf16[192,1536]{1,0:T(8,128)(2,1)}, u32[]{:S(2)}, u32[]{:S(2)}) collective-permute-start(bf16[192,1536]{1,0:T(8,128)(2,1)} %get-tuple-element.427), channel_id=1, source_target_pairs={{0,4},{4,0},{1,5},{5,1},{2,6},{6,2},{3,7},{7,3},{8,12},{12,8},{9,1... | collective-permute-start | bytes 1769480 | tf_op jit(solution)/shard_map/ppermute | solution.py:58
  411.3 20.8 %collective-permute-start.50 = (f32[2,4,2,192]{3,2,1,0:T(2,128)S(1)}, f32[2,4,2,192]{3,2,1,0:T(2,128)S(1)}, u32[]{:S(2)}, u32[]{:S(2)}) collective-permute-start(f32[2,4,2,192]{3,2,1,0:T(2,128)S(1)} %get-tuple-element.433), channel_id=1, source_target_pairs={{0,1},{1,0},{2,3},{3,2},{4,5},{5,4},{6,7},{7,6},{8,9},{9,8},{10,11... | collective-permute-start | bytes 36872 | tf_op jit(solution)/shard_map/ppermute | solution.py:63
  444.4 19.7 %collective-permute-start.60 = (bf16[96,1536]{1,0:T(8,128)(2,1)}, bf16[96,1536]{1,0:T(8,128)(2,1)}, u32[]{:S(2)}, u32[]{:S(2)}) collective-permute-start(bf16[96,1536]{1,0:T(8,128)(2,1)} %get-tuple-element.469), channel_id=1, source_target_pairs={{0,2},{2,0},{1,3},{3,1},{4,6},{6,4},{5,7},{7,5},{8,10},{10,8},{9,1... | collective-permute-start | bytes 884744 | tf_op jit(solution)/shard_map/ppermute | solution.py:56
  444.6 19.5 %collective-permute-start.61 = (bf16[96,1536]{1,0:T(8,128)(2,1)}, bf16[96,1536]{1,0:T(8,128)(2,1)}, u32[]{:S(2)}, u32[]{:S(2)}) collective-permute-start(bf16[96,1536]{1,0:T(8,128)(2,1)} %get-tuple-element.470), channel_id=1, source_target_pairs={{0,4},{4,0},{1,5},{5,1},{2,6},{6,2},{3,7},{7,3},{8,12},{12,8},{9,1... | collective-permute-start | bytes 884744 | tf_op jit(solution)/shard_map/ppermute | solution.py:58
  446.3 17.8 %collective-permute-start.62 = (bf16[96,1536]{1,0:T(8,128)(2,1)}, bf16[96,1536]{1,0:T(8,128)(2,1)}, u32[]{:S(2)}, u32[]{:S(2)}) collective-permute-start(bf16[96,1536]{1,0:T(8,128)(2,1)} %get-tuple-element.471), channel_id=1, source_target_pairs={{0,6},{2,4},{4,2},{6,0},{1,7},{3,5},{5,3},{7,1},{8,14},{10,12},{12... | collective-permute-start | bytes 884744 | tf_op jit(solution)/shard_map/ppermute | solution.py:59
  464.1 15.5 %collective-permute-start.54 = (bf16[192,1536]{1,0:T(8,128)(2,1)}, bf16[192,1536]{1,0:T(8,128)(2,1)S(1)}, u32[]{:S(2)}, u32[]{:S(2)}) collective-permute-start(bf16[192,1536]{1,0:T(8,128)(2,1)} %get-tuple-element.456), channel_id=1, source_target_pairs={{0,2},{2,0},{1,3},{3,1},{4,6},{6,4},{5,7},{7,5},{8,10},{10,8},{9,1... | collective-permute-start | bytes 1769480 | tf_op jit(solution)/shard_map/ppermute | solution.py:56
  464.7 14.9 %collective-permute-start.55 = (bf16[192,1536]{1,0:T(8,128)(2,1)}, bf16[192,1536]{1,0:T(8,128)(2,1)S(1)}, u32[]{:S(2)}, u32[]{:S(2)}) collective-permute-start(bf16[192,1536]{1,0:T(8,128)(2,1)} %get-tuple-element.457), channel_id=1, source_target_pairs={{0,4},{4,0},{1,5},{5,1},{2,6},{6,2},{3,7},{7,3},{8,12},{12,8},{9,1... | collective-permute-start | bytes 1769480 | tf_op jit(solution)/shard_map/ppermute | solution.py:58
  480.7 21.8 %collective-permute-start.58 = (bf16[192,1536]{1,0:T(8,128)(2,1)}, bf16[192,1536]{1,0:T(8,128)(2,1)S(1)}, u32[]{:S(2)}, u32[]{:S(2)}) collective-permute-start(bf16[192,1536]{1,0:T(8,128)(2,1)} %copy-done.63), channel_id=1, source_target_pairs={{0,2},{2,0},{1,3},{3,1},{4,6},{6,4},{5,7},{7,5},{8,10},{10,8},{9,1... | collective-permute-start | bytes 1769480 | tf_op jit(solution)/shard_map/ppermute | solution.py:56
  481.2 21.6 %collective-permute-start.59 = (bf16[192,1536]{1,0:T(8,128)(2,1)}, bf16[192,1536]{1,0:T(8,128)(2,1)S(1)}, u32[]{:S(2)}, u32[]{:S(2)}) collective-permute-start(bf16[192,1536]{1,0:T(8,128)(2,1)} %copy-done.61), channel_id=1, source_target_pairs={{0,4},{4,0},{1,5},{5,1},{2,6},{6,2},{3,7},{7,3},{8,12},{12,8},{9,1... | collective-permute-start | bytes 1769480 | tf_op jit(solution)/shard_map/ppermute | solution.py:58
  502.8 22.8 %collective-permute-start.65 = (bf16[96,1152]{1,0:T(8,128)(2,1)}, bf16[96,1152]{1,0:T(8,128)(2,1)}, u32[]{:S(2)}, u32[]{:S(2)}) collective-permute-start(bf16[96,1152]{1,0:T(8,128)(2,1)} %get-tuple-element.488), channel_id=1, source_target_pairs={{0,2},{2,0},{1,3},{3,1},{4,6},{6,4},{5,7},{7,5},{8,10},{10,8},{9,1... | collective-permute-start | bytes 663560 | tf_op jit(solution)/shard_map/ppermute | solution.py:56
  503.6 24.4 %collective-permute-start.66 = (bf16[96,1152]{1,0:T(8,128)(2,1)}, bf16[96,1152]{1,0:T(8,128)(2,1)}, u32[]{:S(2)}, u32[]{:S(2)}) collective-permute-start(bf16[96,1152]{1,0:T(8,128)(2,1)} %get-tuple-element.489), channel_id=1, source_target_pairs={{0,4},{4,0},{1,5},{5,1},{2,6},{6,2},{3,7},{7,3},{8,12},{12,8},{9,1... | collective-permute-start | bytes 663560 | tf_op jit(solution)/shard_map/ppermute | solution.py:58
  503.6 24.6 %collective-permute-start.67 = (bf16[96,1152]{1,0:T(8,128)(2,1)}, bf16[96,1152]{1,0:T(8,128)(2,1)}, u32[]{:S(2)}, u32[]{:S(2)}) collective-permute-start(bf16[96,1152]{1,0:T(8,128)(2,1)} %get-tuple-element.490), channel_id=1, source_target_pairs={{0,6},{2,4},{4,2},{6,0},{1,7},{3,5},{5,3},{7,1},{8,14},{10,12},{12... | collective-permute-start | bytes 663560 | tf_op jit(solution)/shard_map/ppermute | solution.py:59
  506.5 26.0 %collective-permute-start.64 = (bf16[192,1536]{1,0:T(8,128)(2,1)}, bf16[192,1536]{1,0:T(8,128)(2,1)}, u32[]{:S(2)}, u32[]{:S(2)}) collective-permute-start(bf16[192,1536]{1,0:T(8,128)(2,1)} %add_convert_fusion), channel_id=1, source_target_pairs={{0,4},{4,0},{1,5},{5,1},{2,6},{6,2},{3,7},{7,3},{8,12},{12,8},{9,1... | collective-permute-start | bytes 1769480 | tf_op jit(solution)/shard_map/ppermute | solution.py:58
  507.6 33.2 %collective-permute-start.63 = (bf16[192,1536]{1,0:T(8,128)(2,1)}, bf16[192,1536]{1,0:T(8,128)(2,1)}, u32[]{:S(2)}, u32[]{:S(2)}) collective-permute-start(bf16[192,1536]{1,0:T(8,128)(2,1)} %add_convert_fusion.1), channel_id=1, source_target_pairs={{0,2},{2,0},{1,3},{3,1},{4,6},{6,4},{5,7},{7,5},{8,10},{10,8},{9,1... | collective-permute-start | bytes 1769480 | tf_op jit(solution)/shard_map/ppermute | solution.py:56
  525.6 15.1 %collective-permute-start.70 = (bf16[96,768]{1,0:T(8,128)(2,1)}, bf16[96,768]{1,0:T(8,128)(2,1)}, u32[]{:S(2)}, u32[]{:S(2)}) collective-permute-start(bf16[96,768]{1,0:T(8,128)(2,1)} %get-tuple-element.591), channel_id=1, source_target_pairs={{0,6},{2,4},{4,2},{6,0},{1,7},{3,5},{5,3},{7,1},{8,14},{10,12},{12... | collective-permute-start | bytes 442376 | tf_op jit(solution)/shard_map/ppermute | solution.py:59
  528.0 12.8 %collective-permute-start.69 = (bf16[96,768]{1,0:T(8,128)(2,1)}, bf16[96,768]{1,0:T(8,128)(2,1)}, u32[]{:S(2)}, u32[]{:S(2)}) collective-permute-start(bf16[96,768]{1,0:T(8,128)(2,1)} %get-tuple-element.592), channel_id=1, source_target_pairs={{0,4},{4,0},{1,5},{5,1},{2,6},{6,2},{3,7},{7,3},{8,12},{12,8},{9,1... | collective-permute-start | bytes 442376 | tf_op jit(solution)/shard_map/ppermute | solution.py:58
  532.5 21.7 %collective-permute-start.74 = (f32[3,1,48]{2,1,0:T(1,128)S(1)}, f32[3,1,48]{2,1,0:T(1,128)S(1)}, u32[]{:S(2)}, u32[]{:S(2)}) collective-permute-start(f32[3,1,48]{2,1,0:T(1,128)S(1)} %reshape.195), channel_id=1, source_target_pairs={{0,0},{8,2},{16,4},{24,6},{2,8},{10,10},{18,12},{26,14},{4,16},{12... | collective-permute-start | bytes 1736 | tf_op jit(solution)/shard_map/ppermute | solution.py:1018
  546.7 29.5 %collective-permute-start.72 = (f32[384,1536]{1,0:T(8,128)}, f32[384,1536]{1,0:T(8,128)S(1)}, u32[]{:S(2)}, u32[]{:S(2)}) collective-permute-start(f32[384,1536]{1,0:T(8,128)} %get-tuple-element.508), channel_id=1, source_target_pairs={{0,1},{1,0},{2,3},{3,2},{4,5},{5,4},{6,7},{7,6},{8,9},{9,8},{10,11... | collective-permute-start | bytes 7077896 | tf_op jit(solution)/shard_map/ppermute | solution.py:63
  554.1 21.0 %collective-permute-start.71 = (bf16[384,1536]{1,0:T(8,128)(2,1)}, bf16[384,1536]{1,0:T(8,128)(2,1)S(1)}, u32[]{:S(2)}, u32[]{:S(2)}) collective-permute-start(bf16[384,1536]{1,0:T(8,128)(2,1)} %get-tuple-element.500), channel_id=1, source_target_pairs={{0,1},{1,0},{2,3},{3,2},{4,5},{5,4},{6,7},{7,6},{8,9},{9,8},{10,11... | collective-permute-start | bytes 3538952 | tf_op jit(solution)/shard_map/ppermute | solution.py:63
  (105 other events, 1115.5 us)
Sparse Core Ops, SparseCore 0:
  28.1 51.9 all-gather.8
  100.7 89.2 all-gather.4
  192.2 69.7 all-gather.6
  268.9 100.7 reduce-scatter.3
  371.9 75.5 reduce-scatter.5
  464.2 58.8 reduce-scatter.7
